TPU v7x, 32 devices: a whole 2x2x4 slice. The times are simulated.
32 devices in a mesh: dp: 8 (over z, y), row: 2 (over x), col: 2 (over core).
Axes of the slice: x: 2, y: 2, z: 4, core: 2. Of those that a mesh axis runs over, the one named last changes fastest.
Arguments:
- latents: bfloat16 [8192, 1152], P('dp', ('row', 'col')), may hold values from -6 to 6
- text: bfloat16 [8, 120, 4096], P('dp', None, ('row', 'col')), may hold values from -6 to 6
- text_len: int32 [8], replicated, may hold values from 1 to 120
- time_ids: int32 [8], replicated, may hold values from 0 to 15
- time_table: float32 [16, 6, 1152], P(None, None, ('row', 'col')), may hold values from -4 to 4
- shift_table: float32 [6, 1152], P(None, ('row', 'col')), may hold values from -4 to 4
- w_qkv: bfloat16 [1152, 3, 1152], P('row', None, 'col'), may hold values from -0.1875 to 0.1875
- b_qv: float32 [2, 1152], P(None, ('col', 'row')), may hold values from -3 to 3
- w_out: bfloat16 [1152, 1152], P('col', 'row'), may hold values from -0.75 to 0.75
- b_out: float32 [1152], P(('row', 'col')), may hold values from -3 to 3
- w_cross_q: bfloat16 [1152, 1152], P('row', 'col'), may hold values from -0.1875 to 0.1875
- b_cross_q: float32 [1152], P(('col', 'row')), may hold values from -3 to 3
- w_cross_kv: bfloat16 [4096, 2, 1152], P('row', None, 'col'), may hold values from -0.09375 to 0.09375
- b_cross_v: float32 [1152], P(('col', 'row')), may hold values from -3 to 3
- w_cross_out: bfloat16 [1152, 1152], P('col', 'row'), may hold values from -0.375 to 0.375
- b_cross_out: float32 [1152], P(('row', 'col')), may hold values from -3 to 3
- w_fc1: bfloat16 [1152, 4608], P('row', 'col'), may hold values from -0.1875 to 0.1875
- b_fc1: float32 [4608], P(('col', 'row')), may hold values from -3 to 3
- w_fc2: bfloat16 [4608, 1152], P('col', 'row'), may hold values from -0.09375 to 0.09375
- b_fc2: float32 [1152], P(('row', 'col')), may hold values from -3 to 3
- grad_out: bfloat16 [8192, 1152], P('dp', ('row', 'col')), may hold values from -6 to 6
Outputs:
- out: bfloat16 [8192, 1152], P('dp', ('row', 'col'))
- grad_latents: float32 [8192, 1152], P('dp', ('row', 'col'))
- grad_text: float32 [8, 120, 4096], P('dp', None, ('row', 'col'))
- grad_time_table: float32 [16, 6, 1152], P(None, None, ('row', 'col'))
- grad_shift_table: float32 [6, 1152], P(None, ('row', 'col'))
- grad_w_qkv: float32 [1152, 3, 1152], P(('row', 'dp'), None, 'col')
- grad_b_qv: float32 [2, 1152], P(None, ('col', 'row'))
- grad_w_out: float32 [1152, 1152], P(('col', 'dp'), 'row')
- grad_b_out: float32 [1152], P(('row', 'col'))
- grad_w_cross_q: float32 [1152, 1152], P(('row', 'dp'), 'col')
- grad_b_cross_q: float32 [1152], P(('col', 'row'))
- grad_w_cross_kv: float32 [4096, 2, 1152], P(('row', 'dp'), None, 'col')
- grad_b_cross_v: float32 [1152], P(('col', 'row'))
- grad_w_cross_out: float32 [1152, 1152], P(('col', 'dp'), 'row')
- grad_b_cross_out: float32 [1152], P(('row', 'col'))
- grad_w_fc1: float32 [1152, 4608], P(('row', 'dp'), 'col')
- grad_b_fc1: float32 [4608], P(('col', 'row'))
- grad_w_fc2: float32 [4608, 1152], P(('col', 'dp'), 'row')
- grad_b_fc2: float32 [1152], P(('row', 'col'))
All inputs are finite; a program needn't handle non-finite values.
Results may differ from a plain program's by a relative error of at most 0.018.
Values may be sent and summed in bfloat16 or wider, within the bound.
No kernel may reach another device: no remote copies, remote signals or barrier semaphores. Data moves between devices by JAX's collectives and lax.ppermute only.
A program may use at most 256 MiB of HBM per device.

v0:
```python
from functools import partial

import jax
import jax.numpy as jnp
from jax import lax
from jax.sharding import PartitionSpec as P

MODEL_WIDTH = 1152
HD = 72
TXT = 120
SEQ_DEV = 512
LPP = 2


norm_eps = 1e-06
masked_score = -1000000000.0


def partner(value, axis, distance):
    return lax.ppermute(value, axis, [(i, i ^ 1 << distance) for i in range(lax.axis_size(axis))])


def gather_cols(activations):
    return lax.all_gather(activations, "col", axis=2, tiled=True)


def gather_rows(activations):
    return lax.all_gather(activations, "row", axis=2, tiled=True)


def through_cols(activations, multiply):
    gathered = gather_cols(activations)
    return (gathered, lax.psum_scatter(multiply(gathered), "row", scatter_dimension=2, tiled=True))


def through_rows(activations, multiply):
    gathered = gather_rows(activations)
    return (gathered, lax.psum_scatter(multiply(gathered), "col", scatter_dimension=2, tiled=True))


def forward_by(weight):

    def multiply(gathered):
        return jnp.einsum("rai,iko->rko", gathered, weight, preferred_element_type=jnp.float32)

    return multiply


def backward_by(weight):

    def multiply(gathered):
        return jnp.einsum("rko,iko->ri", gathered, weight, preferred_element_type=jnp.float32)[
            :, None, :
        ]

    return multiply


def weight_grad(inputs, grad_rows):
    return jnp.einsum("rai,rko->iko", inputs, grad_rows, preferred_element_type=jnp.float32)


def stacked_block(matrix):
    return matrix.reshape(matrix.shape[0], 1, matrix.shape[1])


def swap_pair(pieces):
    return partner(pieces, "dp", 0)


def swap_grads(pieces):
    return partner(pieces.astype(jnp.bfloat16), "dp", 0).astype(pieces.dtype)


def feature_totals(first_terms, second_terms):
    return lax.psum(
        (
            jnp.sum(first_terms, axis=-1, keepdims=True),
            jnp.sum(second_terms, axis=-1, keepdims=True),
        ),
        ("row", "col"),
    )


def norm_forward(residual_state, feature_width):
    totals, squares = feature_totals(residual_state, residual_state * residual_state)
    mean_value = totals / feature_width
    variance = squares / feature_width - mean_value * mean_value
    inverse = lax.rsqrt(variance + norm_eps)
    return ((residual_state - mean_value) * inverse, inverse)


def norm_backward(grad_normed, normalized_rows, inverse, feature_width):
    totals, crossed = feature_totals(grad_normed, grad_normed * normalized_rows)
    return inverse * (
        grad_normed - totals / feature_width - normalized_rows * crossed / feature_width
    )


def masked_scores(queries, key_rows, key_valid):
    score_scale = queries.shape[-1] ** (-0.5)
    scores = (
        jnp.einsum("lqhe,lkhe->lhqk", queries, key_rows, preferred_element_type=jnp.float32)
        * score_scale
    )
    return jnp.where(key_valid[:, None, None, :], scores, masked_score)


def attention_forward(queries, key_rows, value_rows, key_valid):
    scores = masked_scores(queries, key_rows, key_valid)
    largest = jnp.max(scores, axis=-1, keepdims=True)
    raised = jnp.exp(scores - largest)
    row_total = jnp.sum(raised, axis=-1, keepdims=True)
    weights = (raised / row_total).astype(jnp.bfloat16)
    mixture = jnp.einsum("lhqk,lkhe->lqhe", weights, value_rows, preferred_element_type=jnp.float32)
    return (mixture.astype(jnp.bfloat16), largest + jnp.log(row_total))


def attention_backward(queries, key_rows, value_rows, key_valid, grad_mixture, log_total):
    score_scale = queries.shape[-1] ** (-0.5)
    scores = masked_scores(queries, key_rows, key_valid)
    weights = jnp.exp(scores - log_total)
    grad_weights = jnp.einsum(
        "lqhe,lkhe->lhqk", grad_mixture, value_rows, preferred_element_type=jnp.float32
    )
    grad_scores = weights * (grad_weights - jnp.sum(grad_weights * weights, axis=-1, keepdims=True))
    rounded = grad_scores.astype(jnp.bfloat16)
    grad_queries = (
        jnp.einsum("lhqk,lkhe->lqhe", rounded, key_rows, preferred_element_type=jnp.float32)
        * score_scale
    )
    grad_keys = (
        jnp.einsum("lhqk,lqhe->lkhe", rounded, queries, preferred_element_type=jnp.float32)
        * score_scale
    )
    grad_values = jnp.einsum(
        "lhqk,lqhe->lkhe",
        weights.astype(jnp.bfloat16),
        grad_mixture,
        preferred_element_type=jnp.float32,
    )
    return (grad_queries, grad_keys, grad_values)


def local(
    latents,
    text,
    text_len,
    time_ids,
    time_table,
    shift_table,
    w_qkv,
    b_qv,
    w_out,
    b_out,
    w_cross_q,
    b_cross_q,
    w_cross_kv,
    b_cross_v,
    w_cross_out,
    b_cross_out,
    w_fc1,
    b_fc1,
    w_fc2,
    b_fc2,
    grad_out,
):
    rows_here, quarter = latents.shape
    heads_here = quarter // HD
    half_count = text.shape[0]
    text_quarter = text.shape[2]
    pair_index = lax.axis_index("dp") // 2
    upper_half = lax.axis_index("dp") % 2
    pair_lengths = lax.dynamic_slice_in_dim(text_len, pair_index * LPP, LPP)
    pair_times = lax.dynamic_slice_in_dim(time_ids, pair_index * LPP, LPP)
    one_hot = (
        pair_times[:, None] == jnp.arange(time_table.shape[0], dtype=jnp.int32)[None, :]
    ).astype(jnp.float32)
    modulation_vectors = shift_table[None] + jnp.einsum(
        "ln,nkf->lkf", one_hot, time_table, precision=lax.Precision.HIGHEST
    )
    self_attention_offset = modulation_vectors[:, 0][:, None, :]
    self_attention_scale = modulation_vectors[:, 1][:, None, :]
    self_attention_gate = modulation_vectors[:, 2][:, None, :]
    feedforward_offset = modulation_vectors[:, 3][:, None, :]
    feedforward_scale = modulation_vectors[:, 4][:, None, :]
    feedforward_gate = modulation_vectors[:, 5][:, None, :]
    block_shape = (LPP, SEQ_DEV, quarter)
    head_shape = (LPP, SEQ_DEV, heads_here, HD)
    residual_state = latents.astype(jnp.float32).reshape(block_shape)
    first_normalized, first_inverse_deviation = norm_forward(residual_state, MODEL_WIDTH)
    modulated_one = (
        (first_normalized * (1.0 + self_attention_scale) + self_attention_offset)
        .astype(jnp.bfloat16)
        .reshape(rows_here, 1, quarter)
    )
    gathered_one, joined_qkv = through_cols(modulated_one, forward_by(w_qkv))
    queries = (joined_qkv[:, 0] + b_qv[0]).astype(jnp.bfloat16).reshape(head_shape)
    key_rows = joined_qkv[:, 1].astype(jnp.bfloat16).reshape(head_shape)
    value_rows = (joined_qkv[:, 2] + b_qv[1]).astype(jnp.bfloat16).reshape(head_shape)
    partner_pair = swap_pair(jnp.stack([key_rows, value_rows]))
    all_keys = jnp.concatenate([key_rows, partner_pair[0]], axis=1)
    all_values = jnp.concatenate([value_rows, partner_pair[1]], axis=1)
    every_key = jnp.ones((LPP, 2 * SEQ_DEV), jnp.bool_)
    attended, log_self = attention_forward(queries, all_keys, all_values, every_key)
    attended_flat = attended.reshape(rows_here, 1, quarter)
    gathered_attended, residual_branch = through_rows(
        attended_flat, forward_by(stacked_block(w_out))
    )
    residual_branch = residual_branch.reshape(block_shape) + b_out
    post_self_attention = residual_state + self_attention_gate * residual_branch
    cross_in = post_self_attention.astype(jnp.bfloat16).reshape(rows_here, 1, quarter)
    gathered_cross, cross_joined = through_cols(cross_in, forward_by(stacked_block(w_cross_q)))
    cross_queries = (cross_joined[:, 0] + b_cross_q).astype(jnp.bfloat16).reshape(head_shape)
    text_rows = text.reshape(half_count * TXT, 1, text_quarter)
    gathered_text, text_joined = through_cols(text_rows, forward_by(w_cross_kv))
    value_bias = jnp.stack([jnp.zeros_like(b_cross_v), b_cross_v])
    own_text = (
        (text_joined + value_bias).astype(jnp.bfloat16).reshape(half_count, TXT, 2, heads_here, HD)
    )
    partner_text = swap_pair(own_text)
    pair_text = jnp.where(
        upper_half == 0,
        jnp.concatenate([own_text, partner_text], axis=0),
        jnp.concatenate([partner_text, own_text], axis=0),
    )
    text_valid = jnp.arange(TXT, dtype=jnp.int32)[None, :] < pair_lengths[:, None]
    crossed, log_cross = attention_forward(
        cross_queries, pair_text[:, :, 0], pair_text[:, :, 1], text_valid
    )
    crossed_flat = crossed.reshape(rows_here, 1, quarter)
    gathered_crossed, cross_branch = through_rows(
        crossed_flat, forward_by(stacked_block(w_cross_out))
    )
    after_cross = post_self_attention + cross_branch.reshape(block_shape) + b_cross_out
    normed_two, inverse_two = norm_forward(after_cross, MODEL_WIDTH)
    modulated_two = (
        (normed_two * (1.0 + feedforward_scale) + feedforward_offset)
        .astype(jnp.bfloat16)
        .reshape(rows_here, 1, quarter)
    )
    gathered_two, hidden = through_cols(modulated_two, forward_by(stacked_block(w_fc1)))
    hidden = hidden[:, 0] + b_fc1
    activated = jax.nn.gelu(hidden, approximate=True).astype(jnp.bfloat16)[:, None, :]
    gathered_act, mlp_branch = through_rows(activated, forward_by(stacked_block(w_fc2)))
    mlp_out = mlp_branch.reshape(block_shape) + b_fc2
    result = after_cross + feedforward_gate * mlp_out
    output = result.astype(jnp.bfloat16).reshape(rows_here, quarter)
    grad_result = grad_out.astype(jnp.float32).reshape(block_shape)
    grad_mlp = feedforward_gate * grad_result
    grad_gate_mlp = jnp.sum(grad_result * mlp_out, axis=1)
    grad_b_fc2 = jnp.sum(grad_mlp, axis=(0, 1))
    gathered_grad_mlp, grad_activated = through_cols(
        grad_mlp.astype(jnp.bfloat16).reshape(rows_here, 1, quarter),
        backward_by(stacked_block(w_fc2)),
    )
    grad_w_fc2 = weight_grad(gathered_act, gathered_grad_mlp)[:, 0]
    grad_hidden = jax.vjp(partial(jax.nn.gelu, approximate=True), hidden)[1](grad_activated[:, 0])[
        0
    ]
    grad_b_fc1 = jnp.sum(grad_hidden, axis=0)
    gathered_grad_hidden, grad_modulated_two = through_rows(
        grad_hidden.astype(jnp.bfloat16)[:, None, :], backward_by(stacked_block(w_fc1))
    )
    grad_w_fc1 = weight_grad(gathered_two, gathered_grad_hidden)[:, 0]
    grad_modulated_two = grad_modulated_two.reshape(block_shape)
    grad_shift_mlp = jnp.sum(grad_modulated_two, axis=1)
    grad_scale_mlp = jnp.sum(grad_modulated_two * normed_two, axis=1)
    grad_after_cross = grad_result + norm_backward(
        grad_modulated_two * (1.0 + feedforward_scale), normed_two, inverse_two, MODEL_WIDTH
    )
    grad_b_cross_out = jnp.sum(grad_after_cross, axis=(0, 1))
    gathered_grad_cross, grad_crossed = through_cols(
        grad_after_cross.astype(jnp.bfloat16).reshape(rows_here, 1, quarter),
        backward_by(stacked_block(w_cross_out)),
    )
    grad_w_cross_out = weight_grad(gathered_crossed, gathered_grad_cross)[:, 0]
    grad_crossed = grad_crossed.astype(jnp.bfloat16).reshape(head_shape)
    grad_cross_queries, grad_pair_keys, grad_pair_values = attention_backward(
        cross_queries, pair_text[:, :, 0], pair_text[:, :, 1], text_valid, grad_crossed, log_cross
    )
    grad_pair_text = jnp.stack([grad_pair_keys, grad_pair_values], axis=2)
    own_part = jnp.where(upper_half == 0, grad_pair_text[:half_count], grad_pair_text[half_count:])
    partner_part = jnp.where(
        upper_half == 0, grad_pair_text[half_count:], grad_pair_text[:half_count]
    )
    grad_text_kv = (own_part + swap_grads(partner_part)).reshape(half_count * TXT, 2, quarter)
    grad_b_cross_v = jnp.sum(grad_text_kv[:, 1], axis=0)
    gathered_grad_text, grad_text_rows = through_rows(
        grad_text_kv.astype(jnp.bfloat16), backward_by(w_cross_kv)
    )
    grad_w_cross_kv = weight_grad(gathered_text, gathered_grad_text)
    grad_text = grad_text_rows.reshape(half_count, TXT, text_quarter)
    grad_cross_flat = grad_cross_queries.reshape(rows_here, quarter)
    grad_b_cross_q = jnp.sum(grad_cross_flat, axis=0)
    gathered_grad_cq, grad_cross_in = through_rows(
        grad_cross_flat.astype(jnp.bfloat16)[:, None, :], backward_by(stacked_block(w_cross_q))
    )
    grad_w_cross_q = weight_grad(gathered_cross, gathered_grad_cq)[:, 0]
    post_self_attention_gradient = grad_after_cross + grad_cross_in.reshape(block_shape)
    residual_branch_gradient = self_attention_gate * post_self_attention_gradient
    self_attention_gate_gradient = jnp.sum(post_self_attention_gradient * residual_branch, axis=1)
    grad_b_out = jnp.sum(residual_branch_gradient, axis=(0, 1))
    gathered_grad_branch, grad_attended = through_cols(
        residual_branch_gradient.astype(jnp.bfloat16).reshape(rows_here, 1, quarter),
        backward_by(stacked_block(w_out)),
    )
    grad_w_out = weight_grad(gathered_attended, gathered_grad_branch)[:, 0]
    grad_queries, grad_all_keys, grad_all_values = attention_backward(
        queries,
        all_keys,
        all_values,
        every_key,
        grad_attended.astype(jnp.bfloat16).reshape(head_shape),
        log_self,
    )
    grad_partner = swap_grads(jnp.stack([grad_all_keys[:, SEQ_DEV:], grad_all_values[:, SEQ_DEV:]]))
    grad_keys_own = grad_all_keys[:, :SEQ_DEV] + grad_partner[0]
    grad_values_own = grad_all_values[:, :SEQ_DEV] + grad_partner[1]
    grad_joined = jnp.stack(
        [
            grad_queries.reshape(rows_here, quarter),
            grad_keys_own.reshape(rows_here, quarter),
            grad_values_own.reshape(rows_here, quarter),
        ],
        axis=1,
    )
    grad_b_qv = jnp.stack([jnp.sum(grad_joined[:, 0], axis=0), jnp.sum(grad_joined[:, 2], axis=0)])
    gathered_grad_joined, first_modulated_gradient = through_rows(
        grad_joined.astype(jnp.bfloat16), backward_by(w_qkv)
    )
    grad_w_qkv = weight_grad(gathered_one, gathered_grad_joined)
    first_modulated_gradient = first_modulated_gradient.reshape(block_shape)
    self_attention_offset_gradient = jnp.sum(first_modulated_gradient, axis=1)
    self_attention_scale_gradient = jnp.sum(first_modulated_gradient * first_normalized, axis=1)
    grad_latents = post_self_attention_gradient + norm_backward(
        first_modulated_gradient * (1.0 + self_attention_scale),
        first_normalized,
        first_inverse_deviation,
        MODEL_WIDTH,
    )
    grad_modulation = jnp.stack(
        [
            self_attention_offset_gradient,
            self_attention_scale_gradient,
            self_attention_gate_gradient,
            grad_shift_mlp,
            grad_scale_mlp,
            grad_gate_mlp,
        ],
        axis=1,
    )
    table_part = jnp.einsum(
        "ln,lkf->nkf", one_hot, grad_modulation, precision=lax.Precision.HIGHEST
    )
    shift_part = jnp.sum(grad_modulation, axis=0)
    (
        grad_time_table,
        grad_shift_table,
        grad_b_qv,
        grad_b_out,
        grad_b_cross_q,
        grad_b_cross_v,
        grad_b_cross_out,
        grad_b_fc1,
        grad_b_fc2,
    ) = lax.psum(
        (
            table_part,
            shift_part,
            grad_b_qv,
            grad_b_out,
            grad_b_cross_q,
            grad_b_cross_v,
            grad_b_cross_out,
            grad_b_fc1,
            grad_b_fc2,
        ),
        "dp",
    )
    (
        summed_qkv,
        summed_out,
        summed_cross_q,
        summed_cross_kv,
        summed_cross_out,
        summed_fc1,
        summed_fc2,
    ) = (
        lax.psum_scatter(grad_w_qkv, "dp", scatter_dimension=0, tiled=True),
        lax.psum_scatter(grad_w_out, "dp", scatter_dimension=0, tiled=True),
        lax.psum_scatter(grad_w_cross_q, "dp", scatter_dimension=0, tiled=True),
        lax.psum_scatter(grad_w_cross_kv, "dp", scatter_dimension=0, tiled=True),
        lax.psum_scatter(grad_w_cross_out, "dp", scatter_dimension=0, tiled=True),
        lax.psum_scatter(grad_w_fc1, "dp", scatter_dimension=0, tiled=True),
        lax.psum_scatter(grad_w_fc2, "dp", scatter_dimension=0, tiled=True),
    )
    return (
        output,
        grad_latents.reshape(rows_here, quarter),
        grad_text,
        grad_time_table,
        grad_shift_table,
        summed_qkv,
        grad_b_qv,
        summed_out,
        grad_b_out,
        summed_cross_q,
        grad_b_cross_q,
        summed_cross_kv,
        grad_b_cross_v,
        summed_cross_out,
        grad_b_cross_out,
        summed_fc1,
        grad_b_fc1,
        summed_fc2,
        grad_b_fc2,
    )


def solution(mesh):
    return jax.shard_map(
        local,
        mesh=mesh,
        in_specs=(
            P("dp", ("row", "col")),
            P("dp", None, ("row", "col")),
            P(),
            P(),
            P(None, None, ("row", "col")),
            P(None, ("row", "col")),
            P("row", None, "col"),
            P(None, ("col", "row")),
            P("col", "row"),
            P(("row", "col")),
            P("row", "col"),
            P(("col", "row")),
            P("row", None, "col"),
            P(("col", "row")),
            P("col", "row"),
            P(("row", "col")),
            P("row", "col"),
            P(("col", "row")),
            P("col", "row"),
            P(("row", "col")),
            P("dp", ("row", "col")),
        ),
        out_specs=(
            P("dp", ("row", "col")),
            P("dp", ("row", "col")),
            P("dp", None, ("row", "col")),
            P(None, None, ("row", "col")),
            P(None, ("row", "col")),
            P(("row", "dp"), None, "col"),
            P(None, ("col", "row")),
            P(("col", "dp"), "row"),
            P(("row", "col")),
            P(("row", "dp"), "col"),
            P(("col", "row")),
            P(("row", "dp"), None, "col"),
            P(("col", "row")),
            P(("col", "dp"), "row"),
            P(("row", "col")),
            P(("row", "dp"), "col"),
            P(("col", "row")),
            P(("col", "dp"), "row"),
            P(("row", "col")),
        ),
        check_vma=False,
    )
```

profile of v0, /device:TPU:0, one launch (start us, length us, event | category | flops | bytes accessed | tf_op | source)
XLA Modules:
  0.0 1811.5 jit_solution(13498809196255560392)
XLA Ops:
  25.9 9.7 all-gather.36.cloned.1.call-done
  44.2 86.1 %reduce-scatter.28.cloned.1.call-done = f32[1024,3,288]{0,2,1:T(8,128)} async-done(((f32[1024,3,576]{0,2,1:T(8,128)}), f32[1024,3,288]{0,2,1:T(8,128)}) %reduce-scatter.28.cloned.1.call-update) | async-done | bytes 3538960 | tf_op jit(solution)/shard_map/reduce_scatter | solution.py:33
  159.3 15.6 collective-permute-done
  194.5 22.9 %all-gather.16.cloned.1.call-done = bf16[1024,1,576]{0,2,1:T(8,128)(2,1)} async-done(((bf16[1024,1,288]{0,2,1:T(8,128)(2,1)}), bf16[1024,1,576]{0,2,1:T(8,128)(2,1)}) %all-gather.16.cloned.1.call-update) | async-done | bytes 1179664 | tf_op jit(solution)/shard_map/all_gather | solution.py:28
  249.7 14.3 reduce-scatter.32.cloned.1.call-done
  270.8 30.2 %reduce-scatter.34.cloned.1.call-done = f32[1024,1,288]{0,2,1:T(8,128)} async-done(((f32[1024,1,576]{0,2,1:T(8,128)}), f32[1024,1,288]{0,2,1:T(8,128)}) %reduce-scatter.34.cloned.1.call-update) | async-done | bytes 1179664 | tf_op jit(solution)/shard_map/reduce_scatter | solution.py:33
  312.4 22.7 %all-gather.20.cloned.1.call-done = bf16[1024,1,576]{0,2,1:T(8,128)(2,1)} async-done(((bf16[1024,1,288]{0,2,1:T(8,128)(2,1)}), bf16[1024,1,576]{0,2,1:T(8,128)(2,1)}) %all-gather.20.cloned.1.call-update) | async-done | bytes 1179664 | tf_op jit(solution)/shard_map/all_gather | solution.py:28
  373.3 9.7 convolution_bitcast_fusion
  391.5 106.1 %reduce-scatter.42.cloned.1.call-done = f32[1024,1,1152]{2,0,1:T(8,128)} async-done(((f32[1024,1,2304]{2,0,1:T(8,128)}), f32[1024,1,1152]{2,0,1:T(8,128)}) %reduce-scatter.42.cloned.1.call-update) | async-done | bytes 4718608 | tf_op jit(solution)/shard_map/reduce_scatter | solution.py:33
  497.6 113.0 %reduce-scatter.38.cloned.1.call-done = f32[1024,1,1152]{2,0,1:T(8,128)} async-done(((f32[1024,1,2304]{2,0,1:T(8,128)}), f32[1024,1,1152]{2,0,1:T(8,128)}) %reduce-scatter.38.cloned.1.call-update) | async-done | bytes 4718608 | tf_op jit(solution)/shard_map/reduce_scatter | solution.py:33
  618.1 62.8 %all-gather.26.cloned.1.call-done = bf16[1024,1,2304]{2,0,1:T(8,128)(2,1)} async-done(((bf16[1024,1,1152]{2,0,1:T(8,128)(2,1)}), bf16[1024,1,2304]{2,0,1:T(8,128)(2,1)}) %all-gather.26.cloned.1.call-update) | async-done | bytes 4718608 | tf_op jit(solution)/shard_map/all_gather | solution.py:28
  687.6 10.0 reduce-scatter.44.cloned.1.call-done
  711.7 9.3 all-gather.28.cloned.1.call-done
  725.6 35.3 %reduce-scatter.46.cloned.1.call-done = f32[1024,1,288]{0,2,1:T(8,128)} async-done(((f32[1024,1,576]{0,2,1:T(8,128)}), f32[1024,1,288]{0,2,1:T(8,128)}) %reduce-scatter.46.cloned.1.call-update) | async-done | bytes 1179664 | tf_op jit(solution)/shard_map/reduce_scatter | solution.py:33
  770.5 22.9 %all-gather.30.cloned.1.call-done = bf16[1024,1,576]{0,2,1:T(8,128)(2,1)} async-done(((bf16[1024,1,288]{0,2,1:T(8,128)(2,1)}), bf16[1024,1,576]{0,2,1:T(8,128)(2,1)}) %all-gather.30.cloned.1.call-update) | async-done | bytes 1179664 | tf_op jit(solution)/shard_map/all_gather | solution.py:28
  797.5 10.0 reduce-scatter.48.cloned.1.call-done
  811.1 10.5 all-gather.32.cloned.1.call-done
  826.8 34.8 %reduce-scatter.50.cloned.1.call-done = f32[1024,1,288]{0,2,1:T(8,128)} async-done(((f32[1024,1,576]{0,2,1:T(8,128)}), f32[1024,1,288]{0,2,1:T(8,128)}) %reduce-scatter.50.cloned.1.call-update) | async-done | bytes 1179664 | tf_op jit(solution)/shard_map/reduce_scatter | solution.py:33
  866.0 13.7 multiply_reduce_fusion
  879.7 15.9 multiply_convert_fusion
  919.5 16.0 collective-permute-done.2
  960.3 41.7 %all-gather.34.cloned.1.call-done = bf16[1024,3,576]{0,2,1:T(8,128)(2,1)} async-done(((bf16[1024,3,288]{0,2,1:T(8,128)(2,1)}), bf16[1024,3,576]{0,2,1:T(8,128)(2,1)}) %all-gather.34.cloned.1.call-update) | async-done | bytes 3538960 | tf_op jit(solution)/shard_map/all_gather | solution.py:28
  1020.8 9.2 fusion.28
  1137.8 39.2 %all-reduce.4 = (f32[6,288]{1,0:T(8,128)}, f32[2,288]{1,0:T(2,128)}, f32[288]{0:T(512)}, f32[288]{0:T(512)}, f32[288]{0:T(512)}, /*index=5*/f32[288]{0:T(512)}, f32[1152]{0:T(1024)}, f32[288]{0:T(512)}) all-reduce(f32[6,288]{1,0:T(8,128)S(1)} %reduce_sum.340, ...), channel_id=1, replica_groups=mesh['dp'=8,'row'=2,'col'=2] {'dp'}, use_global_device_ids=true, to_apply=%region_44.45 | all-reduce | flops 4896 | bytes 39168 | tf_op jit(solution)/shard_map/psum | solution.py:367
  1181.2 24.5 %reduce-scatter.60.cloned.1.call-done = f32[72,2304]{1,0:T(8,128)} async-done(((f32[576,2304]{1,0:T(8,128)}), f32[72,2304]{1,0:T(8,128)}) %reduce-scatter.60.cloned.1.call-update) | async-done | bytes 663568 | tf_op jit(solution)/shard_map/reduce_scatter | solution.py:395
  1205.7 115.8 %reduce-scatter.62.cloned.1.call-done = f32[288,576]{1,0:T(8,128)} async-done(((f32[2304,576]{1,0:T(8,128)}), f32[288,576]{1,0:T(8,128)}) %reduce-scatter.62.cloned.1.call-update) | async-done | bytes 663568 | tf_op jit(solution)/shard_map/reduce_scatter | solution.py:396
  1321.6 11.2 reduce-scatter.54.cloned.1.call-done
  1332.7 68.9 %reduce-scatter.66.cloned.1.call-done = f32[72,576]{1,0:T(8,128)} async-done(((f32[576,576]{1,0:T(8,128)}), f32[72,576]{1,0:T(8,128)}) %reduce-scatter.66.cloned.1.call-update) | async-done | bytes 165904
  1401.6 66.8 %reduce-scatter.64.cloned.1.call-done = f32[72,576]{1,0:T(8,128)} async-done(((f32[576,576]{1,0:T(8,128)}), f32[72,576]{1,0:T(8,128)}) %reduce-scatter.64.cloned.1.call-update) | async-done | bytes 165904
  1468.5 167.3 %reduce-scatter.58.cloned.1.call-done = f32[256,2,576]{0,2,1:T(8,128)} async-done(((f32[2048,2,576]{0,2,1:T(8,128)}), f32[256,2,576]{0,2,1:T(8,128)}) %reduce-scatter.58.cloned.1.call-update) | async-done | bytes 1179664 | tf_op jit(solution)/shard_map/reduce_scatter | solution.py:393
  1635.8 73.1 %all-reduce.11.cloned.1.call-done = f32[16,6,288]{2,0,1:T(8,128)} async-done(((f32[16,6,288]{2,0,1:T(8,128)}), f32[16,6,288]{2,0,1:T(8,128)}) %all-reduce.11.cloned.1.call-update) | async-done | bytes 110608 | tf_op jit(solution)/shard_map/psum | solution.py:367
  1708.9 93.9 %reduce-scatter.56.cloned.1.call-done = f32[72,3,576]{2,0,1:T(8,128)} async-done(((f32[576,3,576]{2,0,1:T(8,128)}), f32[72,3,576]{2,0,1:T(8,128)}) %reduce-scatter.56.cloned.1.call-update) | async-done | bytes 497680 | tf_op jit(solution)/shard_map/reduce_scatter | solution.py:390
  (456 shorter events, 412.3 us)
Async XLA Ops:
  7.2 28.4 %all-gather.36.cloned.1.call-start = ((), (), s32[]{:S(2)}) async-start(), calls=%async_computation.50 | async-start | bytes 1769472 | tf_op jit(solution)/shard_map/all_gather | solution.py:24
  25.9 104.4 %reduce-scatter.28.cloned.1.call-start = ((), (), s32[]{:S(2)}) async-start(), calls=%async_computation.21 | async-start | bytes 10616832 | tf_op jit(solution)/shard_map/reduce_scatter | solution.py:33
  43.4 174.0 %all-gather.16.cloned.1.call-start = ((), (), s32[]{:S(2)}) async-start(), calls=%async_computation.22 | async-start | bytes 1769472 | tf_op jit(solution)/shard_map/all_gather | solution.py:28
  194.5 37.0 %reduce-scatter.30.cloned.1.call-start = ((), (), s32[]{:S(2)}) async-start(), calls=%async_computation.23 | async-start | bytes 3538944 | tf_op jit(solution)/shard_map/reduce_scatter | solution.py:38
  234.3 29.7 %reduce-scatter.32.cloned.1.call-start = ((), (), s32[]{:S(2)}) async-start(), calls=%async_computation.24 | async-start | bytes 884736 | tf_op jit(solution)/shard_map/reduce_scatter | solution.py:33
  241.9 59.2 %reduce-scatter.34.cloned.1.call-start = ((), (), s32[]{:S(2)}) async-start(), calls=%async_computation.26 | async-start | bytes 3538944 | tf_op jit(solution)/shard_map/reduce_scatter | solution.py:33
  248.9 86.3 %all-gather.20.cloned.1.call-start = ((), (), s32[]{:S(2)}) async-start(), calls=%async_computation.27 | async-start | bytes 1769472 | tf_op jit(solution)/shard_map/all_gather | solution.py:28
  312.2 45.0 %reduce-scatter.36.cloned.1.call-start = ((), (), s32[]{:S(2)}) async-start(), calls=%async_computation.28 | async-start | bytes 3538944 | tf_op jit(solution)/shard_map/reduce_scatter | solution.py:38
  339.2 34.1 %all-gather.38.cloned.1.call-start = ((), (), s32[]{:S(2)}) async-start(), calls=%async_computation.51 | async-start | bytes 1769472 | tf_op jit(solution)/shard_map/all_gather | solution.py:24
  344.6 39.0 %all-gather.22.cloned.1.call-start = ((), (), s32[]{:S(2)}) async-start(), calls=%async_computation.29 | async-start | bytes 1769472 | tf_op jit(solution)/shard_map/all_gather | solution.py:24
  373.2 124.4 %reduce-scatter.42.cloned.1.call-start = ((), (), s32[]{:S(2)}) async-start(), calls=%async_computation.33 | async-start | bytes 14155776 | tf_op jit(solution)/shard_map/reduce_scatter | solution.py:33
  383.0 227.6 %reduce-scatter.38.cloned.1.call-start = ((), (), s32[]{:S(2)}) async-start(), calls=%async_computation.30 | async-start | bytes 14155776 | tf_op jit(solution)/shard_map/reduce_scatter | solution.py:33
  391.5 289.3 %all-gather.26.cloned.1.call-start = ((), (), s32[]{:S(2)}) async-start(), calls=%async_computation.34 | async-start | bytes 7077888 | tf_op jit(solution)/shard_map/all_gather | solution.py:28
  618.0 79.6 %reduce-scatter.44.cloned.1.call-start = ((), (), s32[]{:S(2)}) async-start(), calls=%async_computation.35 | async-start | bytes 3538944 | tf_op jit(solution)/shard_map/reduce_scatter | solution.py:38
  687.6 33.4 %all-gather.28.cloned.1.call-start = ((), (), s32[]{:S(2)}) async-start(), calls=%async_computation.36 | async-start | bytes 1769472 | tf_op jit(solution)/shard_map/all_gather | solution.py:24
  711.6 49.3 %reduce-scatter.46.cloned.1.call-start = ((), (), s32[]{:S(2)}) async-start(), calls=%async_computation.37 | async-start | bytes 3538944 | tf_op jit(solution)/shard_map/reduce_scatter | solution.py:33
  724.9 68.5 %all-gather.30.cloned.1.call-start = ((), (), s32[]{:S(2)}) async-start(), calls=%async_computation.38 | async-start | bytes 1769472 | tf_op jit(solution)/shard_map/all_gather | solution.py:28
  770.4 37.1 %reduce-scatter.48.cloned.1.call-start = ((), (), s32[]{:S(2)}) async-start(), calls=%async_computation.39 | async-start | bytes 3538944 | tf_op jit(solution)/shard_map/reduce_scatter | solution.py:38
  811.1 50.6 %reduce-scatter.50.cloned.1.call-start = ((), (), s32[]{:S(2)}) async-start(), calls=%async_computation.41 | async-start | bytes 3538944 | tf_op jit(solution)/shard_map/reduce_scatter | solution.py:33
  825.6 127.0 %all-gather.24.cloned.1.call-start = ((), (), s32[]{:S(2)}) async-start(), calls=%async_computation.31 | async-start | bytes 7077888 | tf_op jit(solution)/shard_map/all_gather | solution.py:28
  826.4 175.6 %all-gather.34.cloned.1.call-start = ((), (), s32[]{:S(2)}) async-start(), calls=%async_computation.42 | async-start | bytes 5308416 | tf_op jit(solution)/shard_map/all_gather | solution.py:28
  952.6 124.0 %reduce-scatter.40.cloned.1.call-start = ((), (), s32[]{:S(2)}) async-start(), calls=%async_computation.32 | async-start | bytes 3538944 | tf_op jit(solution)/shard_map/reduce_scatter | solution.py:38
  960.2 122.8 %reduce-scatter.52.cloned.1.call-start = ((), (), s32[]{:S(2)}) async-start(), calls=%async_computation.43 | async-start | bytes 3538944 | tf_op jit(solution)/shard_map/reduce_scatter | solution.py:38
  1008.3 172.9 %reduce-scatter.68.cloned.1.call-start = ((), (), s32[]{:S(2)}) async-start(), calls=%async_computation.54 | async-start | bytes 1658880
  1012.3 193.4 %reduce-scatter.60.cloned.1.call-start = ((), (), s32[]{:S(2)}) async-start(), calls=%async_computation.48 | async-start | bytes 5971968 | tf_op jit(solution)/shard_map/reduce_scatter | solution.py:395
  1020.6 301.0 %reduce-scatter.62.cloned.1.call-start = ((), (), s32[]{:S(2)}) async-start(), calls=%async_computation.49 | async-start | bytes 6635520 | tf_op jit(solution)/shard_map/reduce_scatter | solution.py:396
  1030.1 302.7 %reduce-scatter.54.cloned.1.call-start = ((), (), s32[]{:S(2)}) async-start(), calls=%async_computation.44 | async-start | bytes 1474560 | tf_op jit(solution)/shard_map/reduce_scatter | solution.py:38
  1049.3 352.4 %reduce-scatter.66.cloned.1.call-start = ((), (), s32[]{:S(2)}) async-start(), calls=%async_computation.53 | async-start | bytes 1658880
  1052.9 415.5 %reduce-scatter.64.cloned.1.call-start = ((), (), s32[]{:S(2)}) async-start(), calls=%async_computation.52 | async-start | bytes 1658880
  1057.7 578.1 %reduce-scatter.58.cloned.1.call-start = ((), (), s32[]{:S(2)}) async-start(), calls=%async_computation.47 | async-start | bytes 10616832 | tf_op jit(solution)/shard_map/reduce_scatter | solution.py:393
  1063.8 645.2 %all-reduce.11.cloned.1.call-start = ((), (), s32[]{:S(2)}) async-start(), calls=%async_computation.45 | async-start | bytes 294912 | tf_op jit(solution)/shard_map/psum | solution.py:367
  1108.4 694.4 %reduce-scatter.56.cloned.1.call-start = ((), (), s32[]{:S(2)}) async-start(), calls=%async_computation.46 | async-start | bytes 4976640 | tf_op jit(solution)/shard_map/reduce_scatter | solution.py:390
  (104 other events, 1661.8 us)
Sparse Core Ops, SparseCore 0:
  26.0 9.5 all-gather.35
  43.5 86.7 reduce-scatter.27
  194.6 22.7 all-gather.15
  221.6 9.8 reduce-scatter.29
  234.4 10.3 all-gather.17
  247.5 16.4 reduce-scatter.31
  266.3 34.6 reduce-scatter.33
  312.3 22.7 all-gather.19
  339.3 9.8 reduce-scatter.35
  351.3 10.3 all-gather.37
  373.3 10.2 all-gather.21
  385.9 111.7 reduce-scatter.41
  500.0 110.5 reduce-scatter.37
  618.1 62.6 all-gather.25
  687.7 9.8 reduce-scatter.43
  725.0 35.8 reduce-scatter.45
  770.6 22.7 all-gather.29
  797.6 9.8 reduce-scatter.47
  811.2 10.3 all-gather.31
  825.8 35.8 reduce-scatter.49
  863.3 62.6 all-gather.23
  952.7 49.1 all-gather.33
  1004.1 9.9 reduce-scatter.39
  1016.3 11.0 reduce-scatter.51
  1031.8 64.5 reduce-scatter.67
  1100.8 104.9 reduce-scatter.59
  1210.0 111.5 reduce-scatter.61
  1337.1 64.5 reduce-scatter.65
  1406.1 62.2 reduce-scatter.63
  1473.1 162.6 reduce-scatter.57
  1639.9 68.9 all-reduce.10
  1713.2 89.6 reduce-scatter.55
  (2 shorter events, 17.4 us)
where the time goes:
time: 1820 us; the launch traced here: 1810 us
  waiting for transfers between devices  1310 us (72%)
  matrix products  166 us (9%)
  local copies, waits for them, and re-layouts  133 us (7%)
  other arithmetic  101 us (6%)
  blocking collectives  75.7 us (4%)
    reduce_scatter x7, waiting for transfers between devices, through_cols(): lax.psum_scatter(multiply(gathered), 'row', scatter_dimension=2, tiled=True)  420 us
    all_gather x6, waiting for transfers between devices, gather_rows(): return lax.all_gather(activations, 'row', axis=2, tiled=True)  173 us
    reduce_scatter x1, waiting for transfers between devices, local(): lax.psum_scatter(grad_w_cross_kv, 'dp', scatter_dimension=0, tiled=True)  167 us
    unnamed x37, waiting for transfers between devices  136 us
    reduce_scatter x1, waiting for transfers between devices, local(): lax.psum_scatter(grad_w_fc2, 'dp', scatter_dimension=0, tiled=True)  116 us
    reduce_scatter x1, waiting for transfers between devices, local(): lax.psum_scatter(grad_w_qkv, 'dp', scatter_dimension=0, tiled=True)  93.9 us
    psum x1, waiting for transfers between devices, local(): lax.psum((table_part, shift_part, grad_b_qv, grad_b_out, grad_b_cross_q,...  73.1 us
    dot_general x7, matrix products, weight_grad(): jnp.einsum('rai,rko->iko', inputs, grad_rows, preferred_element_type=jnp....  40.5 us
  transfers between devices with their start and end apart: 38, of which 32 were waited for; matrix products, arithmetic and copies ran while one was open for 15% of the time, Pallas kernels for 0%

commit v1 on v0

v1 whole, which is shorter than its diff:
```python
from functools import partial

import jax
import jax.numpy as jnp
from jax import lax
from jax.experimental import pallas as pl
from jax.experimental.pallas import tpu as pltpu
from jax.sharding import PartitionSpec as P

HD = 72
TXT = 120
TXT_PAD = 128
SEQ_DEV = 512
LPP = 2
HALF = 256

norm_eps = 1e-06
masked_score = -1000000000.0
f32 = jnp.float32
bf16 = jnp.bfloat16


def swap(value, axis):
    return lax.ppermute(value, axis, [(0, 1), (1, 0)])


def swap_dp(value, bit):
    return lax.ppermute(value, "dp", [(i, i ^ (1 << bit)) for i in range(lax.axis_size("dp"))])


def pick(pair_first, pair_second, index):
    return jnp.where(index == 0, pair_first, pair_second)


def in_order(mine, other, index, axis):
    return jnp.concatenate([pick(mine, other, index), pick(other, mine, index)], axis=axis)


def after(value, *earlier):
    return lax.optimization_barrier((value, *earlier))[0]


def dot(left, right, left_dim, right_dim):
    return lax.dot_general(
        left, right, (((left_dim,), (right_dim,)), ((), ())), preferred_element_type=f32
    )


def attend_kernel(masked, length_ref, q_ref, k_ref, v_ref, o_ref, log_ref):
    q, k, v = q_ref[0], k_ref[0], v_ref[0]
    scores = dot(k, q, 0, 0) * (HD ** (-0.5))
    if masked:
        place = lax.broadcasted_iota(jnp.int32, scores.shape, 0)
        scores = jnp.where(place < length_ref[0], scores, masked_score)
    largest = jnp.max(scores, axis=0, keepdims=True)
    raised = jnp.exp(scores - largest)
    total = jnp.sum(raised, axis=0, keepdims=True)
    mixture = dot(v, raised.astype(bf16), 1, 0)
    o_ref[0] = (mixture / total).astype(bf16)
    log_ref[0] = largest + jnp.log(total)


def attend(q, k, v, length, masked):
    heads, hd, nq = q.shape
    nk = k.shape[2]
    head = lambda h: (h, 0, 0)
    return pl.pallas_call(
        partial(attend_kernel, masked),
        grid=(heads,),
        in_specs=[
            pl.BlockSpec(memory_space=pltpu.SMEM),
            pl.BlockSpec((1, hd, nq), head),
            pl.BlockSpec((1, hd, nk), head),
            pl.BlockSpec((1, hd, nk), head),
        ],
        out_specs=[pl.BlockSpec((1, hd, nq), head), pl.BlockSpec((1, 1, nq), head)],
        out_shape=[
            jax.ShapeDtypeStruct((heads, hd, nq), bf16),
            jax.ShapeDtypeStruct((heads, 1, nq), f32),
        ],
        compiler_params=pltpu.CompilerParams(vmem_limit_bytes=32 * 2**20),
        cost_estimate=pl.CostEstimate(
            flops=4 * heads * nq * nk * 128,
            bytes_accessed=4 * heads * hd * (nq + nk),
            transcendentals=heads * nq * nk,
        ),
        name="attend_fwd",
    )(length, q, k, v)


def attend_grad_kernel(
    masked, length_ref, q_ref, k_ref, v_ref, g_ref, log_ref, dq_ref, dk_ref, dv_ref
):
    q, k, v, g = q_ref[0], k_ref[0], v_ref[0], g_ref[0]
    scores = dot(k, q, 0, 0) * (HD ** (-0.5))
    if masked:
        place = lax.broadcasted_iota(jnp.int32, scores.shape, 0)
        scores = jnp.where(place < length_ref[0], scores, masked_score)
    weights = jnp.exp(scores - log_ref[0])
    grad_weights = dot(v, g, 0, 0)
    crossed = jnp.sum(grad_weights * weights, axis=0, keepdims=True)
    grad_scores = (weights * (grad_weights - crossed)).astype(bf16)
    dq_ref[0] = (dot(k, grad_scores, 1, 0) * (HD ** (-0.5))).astype(bf16)
    dk_ref[0] = (dot(q, grad_scores, 1, 1) * (HD ** (-0.5))).astype(bf16)
    dv_ref[0] = dot(g, weights.astype(bf16), 1, 1).astype(bf16)


def attend_grad(q, k, v, g, log_total, length, masked):
    heads, hd, nq = q.shape
    nk = k.shape[2]
    head = lambda h: (h, 0, 0)
    return pl.pallas_call(
        partial(attend_grad_kernel, masked),
        grid=(heads,),
        in_specs=[
            pl.BlockSpec(memory_space=pltpu.SMEM),
            pl.BlockSpec((1, hd, nq), head),
            pl.BlockSpec((1, hd, nk), head),
            pl.BlockSpec((1, hd, nk), head),
            pl.BlockSpec((1, hd, nq), head),
            pl.BlockSpec((1, 1, nq), head),
        ],
        out_specs=[
            pl.BlockSpec((1, hd, nq), head),
            pl.BlockSpec((1, hd, nk), head),
            pl.BlockSpec((1, hd, nk), head),
        ],
        out_shape=[
            jax.ShapeDtypeStruct((heads, hd, nq), bf16),
            jax.ShapeDtypeStruct((heads, hd, nk), bf16),
            jax.ShapeDtypeStruct((heads, hd, nk), bf16),
        ],
        compiler_params=pltpu.CompilerParams(vmem_limit_bytes=40 * 2**20),
        cost_estimate=pl.CostEstimate(
            flops=10 * heads * nq * nk * 128,
            bytes_accessed=8 * heads * hd * (nq + nk),
            transcendentals=heads * nq * nk,
        ),
        name="attend_bwd",
    )(length, q, k, v, g, log_total)


def norm_forward(state):
    center = state - jnp.mean(state, axis=0, keepdims=True)
    inverse = lax.rsqrt(jnp.mean(center * center, axis=0, keepdims=True) + norm_eps)
    return (center * inverse, inverse)


def norm_backward(grad_normed, normed, inverse):
    return inverse * (
        grad_normed
        - jnp.mean(grad_normed, axis=0, keepdims=True)
        - normed * jnp.mean(grad_normed * normed, axis=0, keepdims=True)
    )


def split_sum(partial_rows):
    other = swap(partial_rows[:, HALF:].astype(bf16), "col")
    return partial_rows[:, :HALF] + other.astype(f32)


def join_cols(own):
    return jnp.concatenate([own, swap(own, "col")], axis=1)


def through_in(own_w, other_w, rows):
    k = own_w.shape[0]
    return dot(own_w, rows[:k], 0, 0) + dot(other_w, rows[k:], 0, 0)


def reduce_weight(grads, order, row_index, dp_index):
    bits = lax.axis_size("dp").bit_length() - 1
    rows, n = grads.shape[1:]
    block = rows >> bits
    held = grads.reshape((2,) + (2,) * bits + (block, n))
    left = ["row"] + list(range(bits - 1, -1, -1))
    for step, name in enumerate(order):
        axis = left.index(name)
        if name == "row":
            keep = lax.index_in_dim(held, 0, axis, keepdims=False)
            send = lax.index_in_dim(held, 1, axis, keepdims=False)
            got = swap(send, "row")
        else:
            bit = (dp_index >> name) & 1
            first = lax.index_in_dim(held, 0, axis, keepdims=False)
            second = lax.index_in_dim(held, 1, axis, keepdims=False)
            keep = pick(first, second, bit)
            got = swap_dp(pick(second, first, bit), name)
        left.pop(axis)
        held = keep.astype(f32) + got.astype(f32)
        if step < len(order) - 1:
            held = held.astype(bf16)
    return held.reshape(block, n)


def local(
    latents,
    text,
    text_len,
    time_ids,
    time_table,
    shift_table,
    w_qkv,
    b_qv,
    w_out,
    b_out,
    w_cross_q,
    b_cross_q,
    w_cross_kv,
    b_cross_v,
    w_cross_out,
    b_cross_out,
    w_fc1,
    b_fc1,
    w_fc2,
    b_fc2,
    grad_out,
):
    quarter = latents.shape[1]
    half = 2 * quarter
    heads = half // HD
    n_dp = lax.axis_size("dp")
    bits = n_dp.bit_length() - 1
    d = lax.axis_index("dp")
    r = lax.axis_index("row")
    c = lax.axis_index("col")
    upper = d % 2
    pair = d // 2
    my_latent = pair * LPP + r

    def to_latent(values):
        turned = values.reshape(LPP, SEQ_DEV, quarter).transpose(0, 2, 1)
        mine, others = pick(turned[0], turned[1], r), pick(turned[1], turned[0], r)
        return jnp.stack([mine, swap(others, "row")])

    def all_features(halves):
        other = swap(halves, "col")
        both = jnp.stack([pick(halves, other, c), pick(other, halves, c)], axis=1)
        both = both.reshape(2 * half, SEQ_DEV)
        first, second = both[:, :HALF], both[:, HALF:]
        return jnp.concatenate([pick(first, second, c), pick(second, first, c)], axis=1)

    lat_half = to_latent(latents)
    lat_far = swap_dp(lat_half, 0)
    grad_half = to_latent(grad_out)
    w_qkv_o = swap(after(w_qkv, lat_far), "row")

    pair_times = lax.dynamic_slice_in_dim(time_ids, pair * LPP, LPP)
    one_hot = (
        pair_times[:, None] == jnp.arange(time_table.shape[0], dtype=jnp.int32)[None, :]
    ).astype(f32)
    modulation = shift_table[None] + jnp.einsum(
        "ln,nkf->lkf", one_hot, time_table, precision=lax.Precision.HIGHEST
    )
    feature_biases = jnp.stack([b_out, b_cross_out, b_fc2])
    wide = jnp.concatenate(
        [modulation, jnp.broadcast_to(feature_biases, (LPP, 3, quarter))], axis=1
    )
    col_biases = jnp.concatenate([b_qv.reshape(-1), b_cross_q, b_cross_v, b_fc1])
    sent = jnp.concatenate([pick(wide[1], wide[0], r).reshape(-1), col_biases])
    got = swap(sent, "row")
    wide_rows = jnp.stack([pick(wide[0], wide[1], r), got[: 9 * quarter].reshape(9, quarter)])
    wide_other = swap(wide_rows, "col")
    wide_all = jnp.stack(
        [pick(wide_rows, wide_other, c), pick(wide_other, wide_rows, c)], axis=1
    )
    vectors = wide_all.transpose(2, 0, 1, 3).reshape(9, 2 * half)
    shift_one, scale_one, gate_one, shift_two, scale_two, gate_two, bias_out, bias_co, bias_fc2 = (
        vectors[i][:, None] for i in range(9)
    )
    got_cols = got[9 * quarter :]

    def col_bias(start, width):
        return in_order(col_biases[start : start + width], got_cols[start : start + width], r, 0)

    bias_q = col_bias(0, quarter)[:, None]
    bias_v = col_bias(quarter, quarter)[:, None]
    bias_cq = col_bias(2 * quarter, quarter)[:, None]
    bias_cv = col_bias(3 * quarter, quarter)[:, None]
    bias_fc1 = col_bias(4 * quarter, b_fc1.shape[0])[:, None]

    text_own = text[0]
    text_row = in_order(text_own, swap(text_own, "col"), c, 1)
    kv_part = jnp.einsum("ti,iko->kot", text_row, w_cross_kv, preferred_element_type=f32)
    kv_total = kv_part + swap(kv_part.astype(bf16), "row").astype(f32)
    kv_total = jnp.concatenate(
        [kv_total[0].astype(bf16), (kv_total[1] + bias_cv).astype(bf16)]
    )
    kv_far = swap_dp(kv_total, 0)
    kv_mine = pick(kv_total, kv_far, r ^ upper).reshape(2, heads, HD, TXT)
    kv_mine = jnp.pad(kv_mine, ((0, 0), (0, 0), (0, 0), (0, TXT_PAD - TXT)))
    text_k, text_v = kv_mine[0], kv_mine[1]
    length = lax.dynamic_slice_in_dim(text_len, my_latent, 1)

    lat_all = jnp.concatenate([all_features(lat_half), all_features(lat_far)], axis=1).astype(f32)
    normed_all, inverse_all = norm_forward(lat_all)
    mod_all = (normed_all * (1.0 + scale_one) + shift_one).astype(bf16)
    normed_one, inverse_one = normed_all[:, :HALF], inverse_all[:, :HALF]
    mod_own = mod_all[:, :SEQ_DEV]
    w_q, w_k, w_v = (
        jnp.concatenate([w_qkv[:, i], w_qkv_o[:, i]], axis=0) for i in range(3)
    )
    keys = dot(w_k, mod_all, 0, 0).astype(bf16).reshape(heads, HD, -1)
    values = (dot(w_v, mod_all, 0, 0) + bias_v).astype(bf16).reshape(heads, HD, -1)
    queries = (dot(w_q, mod_own, 0, 0) + bias_q).astype(bf16).reshape(heads, HD, -1)
    w_out_o = swap(after(w_out, w_qkv_o), "row")
    w_cq_o = swap(after(w_cross_q, w_out_o), "row")
    w_co_o = swap(after(w_cross_out, w_cq_o), "row")
    w_fc1_o = swap(after(w_fc1, w_co_o), "row")
    w_fc2_o = swap(after(w_fc2, w_fc1_o), "row")
    attended, log_self = attend(queries, keys, values, length, False)
    attended = attended.reshape(half, -1)

    w_out_all = jnp.concatenate([w_out, w_out_o], axis=1)
    branch = split_sum(dot(w_out_all, attended, 0, 0)) + bias_out
    residual = lat_all[:, :HALF]
    after_self = residual + gate_one * branch
    cross_in = join_cols(after_self.astype(bf16))

    w_cq_all = jnp.concatenate([w_cross_q, w_cq_o], axis=0)
    cross_q = (dot(w_cq_all, cross_in, 0, 0) + bias_cq).astype(bf16).reshape(heads, HD, -1)
    crossed, log_cross = attend(cross_q, text_k, text_v, length, True)
    crossed = crossed.reshape(half, -1)
    w_co_all = jnp.concatenate([w_cross_out, w_co_o], axis=1)
    after_cross = after_self + split_sum(dot(w_co_all, crossed, 0, 0)) + bias_co

    normed_two, inverse_two = norm_forward(after_cross)
    mod_two = join_cols((normed_two * (1.0 + scale_two) + shift_two).astype(bf16))
    w_fc1_all = jnp.concatenate([w_fc1, w_fc1_o], axis=0)
    hidden = dot(w_fc1_all, mod_two, 0, 0) + bias_fc1
    activated = jax.nn.gelu(hidden, approximate=True).astype(bf16)

    grad_all = all_features(grad_half).astype(f32)
    grad_mlp = (gate_two * grad_all).astype(bf16)
    w_fc2_all = jnp.concatenate([w_fc2, w_fc2_o], axis=1)
    grad_activated = dot(w_fc2_all, grad_mlp, 1, 0)
    grad_hidden = jax.vjp(partial(jax.nn.gelu, approximate=True), hidden)[1](grad_activated)[0]
    grad_b_fc1 = jnp.sum(grad_hidden, axis=1)
    grad_hidden = grad_hidden.astype(bf16)

    def weight_grad_in(inputs, grads):
        return dot(inputs, grads, 1, 1).astype(bf16).reshape(2, -1, grads.shape[0])

    def weight_grad_out(inputs, grads):
        n = grads.shape[0] // 2
        return jnp.stack([dot(inputs, g, 1, 1).astype(bf16) for g in (grads[:n], grads[n:])])

    dp_bits = list(range(bits))
    order_x = ["row"] + dp_bits
    order_y = [0, "row"] + dp_bits[1:]
    order_z = [1, "row", 0] + dp_bits[2:]
    summed_fc2 = reduce_weight(weight_grad_out(activated, grad_mlp), order_x, r, d)
    summed_fc1 = reduce_weight(weight_grad_in(mod_two, grad_hidden), order_y, r, d)

    grad_mod_two = split_sum(dot(w_fc1_all, grad_hidden, 1, 0))
    grad_own = grad_all[:, :HALF]
    grad_after_cross = grad_own + norm_backward(
        grad_mod_two * (1.0 + scale_two), normed_two, inverse_two
    )
    grad_cross = join_cols(grad_after_cross.astype(bf16))

    mlp_out = split_sum(dot(w_fc2_all, activated, 0, 0)) + bias_fc2
    result = (after_cross + gate_two * mlp_out).astype(bf16)

    grad_crossed = dot(w_co_all, grad_cross, 1, 0).astype(bf16).reshape(heads, HD, -1)
    summed_co = reduce_weight(weight_grad_out(crossed, grad_cross), order_z, r, d)
    grad_cq, grad_tk, grad_tv = attend_grad(
        cross_q, text_k, text_v, grad_crossed, log_cross, length, True
    )
    grad_cq = grad_cq.reshape(half, -1)
    summed_cq = reduce_weight(weight_grad_in(cross_in, grad_cq), order_z, r, d)
    grad_b_cq = jnp.sum(grad_cq.astype(f32), axis=1)
    grad_after_self = grad_after_cross + split_sum(dot(w_cq_all, grad_cq, 1, 0))
    grad_branch = join_cols((gate_one * grad_after_self).astype(bf16))

    grad_kv = jnp.stack([grad_tk, grad_tv])[..., :TXT].reshape(2, half, TXT)
    grad_kv = grad_kv.astype(f32) + swap_dp(grad_kv, 0).astype(f32)
    grad_b_cv = jnp.sum(grad_kv[1], axis=1)
    grad_kv_latent = grad_kv.astype(bf16)
    grad_kv_other = swap(grad_kv_latent, "row")
    grad_kv_own = pick(grad_kv_latent, grad_kv_other, r ^ upper)
    grad_text_part = jnp.einsum(
        "kot,iko->ti", grad_kv_own, w_cross_kv, preferred_element_type=f32
    )
    text_quarter = text.shape[2]
    keep_text = pick(grad_text_part[:, :text_quarter], grad_text_part[:, text_quarter:], c)
    send_text = pick(grad_text_part[:, text_quarter:], grad_text_part[:, :text_quarter], c)
    grad_text = (keep_text + swap(send_text.astype(bf16), "col").astype(f32))[None]
    blocks = text_row.reshape((TXT,) + (2,) * bits + (-1,))
    held = blocks[None]
    kv_held = grad_kv_own[None]
    for bit in range(bits):
        axis = held.ndim - 2
        first = lax.index_in_dim(held, 0, axis, keepdims=False)
        second = lax.index_in_dim(held, 1, axis, keepdims=False)
        mine = (d >> bit) & 1
        got_text = swap_dp(pick(second, first, mine), bit)
        held = jnp.concatenate([pick(first, second, mine), got_text], axis=0)
        kv_held = jnp.concatenate([kv_held, swap_dp(kv_held, bit)], axis=0)
    summed_ckv = jnp.einsum("lti,lkot->iko", held, kv_held, preferred_element_type=f32)

    grad_attended = dot(w_out_all, grad_branch, 1, 0).astype(bf16).reshape(heads, HD, -1)
    summed_out = reduce_weight(weight_grad_out(attended, grad_branch), order_z, r, d)
    grad_q, grad_k, grad_v = attend_grad(
        queries, keys, values, grad_attended, log_self, length, False
    )
    grad_q, grad_k, grad_v = (g.reshape(half, -1) for g in (grad_q, grad_k, grad_v))
    summed_k = reduce_weight(weight_grad_in(mod_all, grad_k), order_x, r, d)
    summed_v = reduce_weight(weight_grad_in(mod_all, grad_v), order_y, r, d)
    summed_q = reduce_weight(weight_grad_in(mod_own, grad_q), order_z, r, d)
    summed_qkv = jnp.stack([summed_q, summed_k, summed_v], axis=1)
    grad_b_q = jnp.sum(grad_q.astype(f32), axis=1)
    grad_b_v = jnp.sum(grad_v.astype(f32), axis=1)
    grad_mod_kv = dot(w_k, grad_k, 1, 0) + dot(w_v, grad_v, 1, 0)
    far_part = swap_dp(split_sum(grad_mod_kv[:, SEQ_DEV:]).astype(bf16), 0)
    near_part = split_sum(grad_mod_kv[:, :SEQ_DEV] + dot(w_q, grad_q, 1, 0))
    grad_mod_one = near_part + far_part.astype(f32)
    grad_latents = grad_after_self + norm_backward(
        grad_mod_one * (1.0 + scale_one), normed_one, inverse_one
    )

    def to_features(own):
        blocks = own.reshape(2, 2, quarter, HALF)
        keep = pick(blocks[:, 0], blocks[:, 1], c)
        got = swap(pick(blocks[:, 1], blocks[:, 0], c), "col")
        tokens = in_order(keep, got, c, 2)
        other = swap(tokens[1], "row")
        return in_order(tokens[0].T, other.T, r, 0)

    output = to_features(result)
    grad_latents = to_features(grad_latents.astype(bf16)).astype(f32)

    grad_vectors = jnp.stack(
        [
            jnp.sum(grad_mod_one, axis=1),
            jnp.sum(grad_mod_one * normed_one, axis=1),
            jnp.sum(grad_after_self * branch, axis=1),
            jnp.sum(grad_mod_two, axis=1),
            jnp.sum(grad_mod_two * normed_two, axis=1),
            jnp.sum(grad_own * mlp_out, axis=1),
            gate_one[:, 0] * jnp.sum(grad_after_self, axis=1),
            jnp.sum(grad_after_cross, axis=1),
            gate_two[:, 0] * jnp.sum(grad_own, axis=1),
        ]
    ).reshape(9, 2, 2, quarter)
    keep = pick(grad_vectors[:, :, 0], grad_vectors[:, :, 1], c)
    keep = keep + swap(pick(grad_vectors[:, :, 1], grad_vectors[:, :, 0], c), "col")
    col_grads = jnp.concatenate(
        [
            g.reshape(2, -1)
            for g in (grad_b_q, grad_b_v, grad_b_cq, grad_b_cv, grad_b_fc1)
        ],
        axis=1,
    )
    pair_once = jnp.concatenate(
        [
            jnp.ones((3 * quarter,), f32),
            jnp.full((quarter,), 0.5, f32),
            jnp.ones((col_grads.shape[1] - 4 * quarter,), f32),
        ]
    )
    col_grads = col_grads * pair_once
    mine_cols = pick(col_grads[0], col_grads[1], r)
    sent = jnp.concatenate([keep[:, 1].reshape(-1), pick(col_grads[1], col_grads[0], r)])
    got = swap(sent, "row")
    got_wide = got[: 9 * quarter].reshape(9, quarter)
    own_wide = keep[:, 0]
    latent_wide = jnp.stack([pick(own_wide, got_wide, r), pick(got_wide, own_wide, r)])
    mine_cols = mine_cols + got[9 * quarter :]
    table_part = jnp.einsum(
        "ln,lkf->nkf", one_hot, latent_wide[:, :6], precision=lax.Precision.HIGHEST
    )
    ntab = time_table.shape[0]
    flat = jnp.concatenate(
        [table_part.reshape(-1), (own_wide + got_wide).reshape(-1), mine_cols]
    )
    for bit in range(bits):
        flat = flat + swap_dp(flat, bit)
    n_table = ntab * 6 * quarter
    grad_time_table = flat[:n_table].reshape(ntab, 6, quarter)
    rest = flat[n_table:]
    wide_sums = rest[: 9 * quarter].reshape(9, quarter)
    grad_shift_table = wide_sums[:6]
    cols = rest[9 * quarter :]
    grad_b_qv = cols[: 2 * quarter].reshape(2, quarter)
    return (
        output,
        grad_latents,
        grad_text,
        grad_time_table,
        grad_shift_table,
        summed_qkv,
        grad_b_qv,
        summed_out,
        wide_sums[6],
        summed_cq,
        cols[2 * quarter : 3 * quarter],
        summed_ckv,
        cols[3 * quarter : 4 * quarter],
        summed_co,
        wide_sums[7],
        summed_fc1,
        cols[4 * quarter :],
        summed_fc2,
        wide_sums[8],
    )


def solution(mesh):
    return jax.shard_map(
        local,
        mesh=mesh,
        in_specs=(
            P("dp", ("row", "col")),
            P("dp", None, ("row", "col")),
            P(),
            P(),
            P(None, None, ("row", "col")),
            P(None, ("row", "col")),
            P("row", None, "col"),
            P(None, ("col", "row")),
            P("col", "row"),
            P(("row", "col")),
            P("row", "col"),
            P(("col", "row")),
            P("row", None, "col"),
            P(("col", "row")),
            P("col", "row"),
            P(("row", "col")),
            P("row", "col"),
            P(("col", "row")),
            P("col", "row"),
            P(("row", "col")),
            P("dp", ("row", "col")),
        ),
        out_specs=(
            P("dp", ("row", "col")),
            P("dp", ("row", "col")),
            P("dp", None, ("row", "col")),
            P(None, None, ("row", "col")),
            P(None, ("row", "col")),
            P(("row", "dp"), None, "col"),
            P(None, ("col", "row")),
            P(("col", "dp"), "row"),
            P(("row", "col")),
            P(("row", "dp"), "col"),
            P(("col", "row")),
            P(("row", "dp"), None, "col"),
            P(("col", "row")),
            P(("col", "dp"), "row"),
            P(("row", "col")),
            P(("row", "dp"), "col"),
            P(("col", "row")),
            P(("col", "dp"), "row"),
            P(("row", "col")),
        ),
        check_vma=False,
    )
```

time: 1820 us -> 740 us (0.41)
  waiting for transfers between devices: 1310 us -> 397 us
  matrix products: 166 us -> 77.5 us
  blocking collectives: 75.7 us -> 0 us
  local copies, waits for them, and re-layouts: 133 us -> 66.7 us
  starting transfers between devices: 8.22 us -> 67.3 us
  Pallas kernels: 0 us -> 35.5 us
    reduce_scatter x18 -> x0, waiting for transfers between devices: 858 us -> none  [the longest x7 420 us: through_cols(): lax.psum_scatter(multiply(gathered), 'row', scatter_dimension=2, tiled=True)]
    ppermute x4 -> x79, waiting for transfers between devices: 39.2 us -> 397 us  [the longest x42 231 us: swap(): return lax.ppermute(value, axis, [(0, 1), (1, 0)])]
    all_gather x12 -> x0, waiting for transfers between devices: 206 us -> none  [the longest x6 173 us: gather_rows(): return lax.all_gather(activations, 'row', axis=2, tiled=True)]
    unnamed x37 -> x0, waiting for transfers between devices: 136 us -> none
    dot_general x34 -> x31, matrix products: 165 us -> 77.3 us  [the longest x27 65.5 us: dot(): lax.dot_general(left, right, (((left_dim,), (right_dim,)), ((), ())), pre...]
    psum x1 -> x0, waiting for transfers between devices: 73.1 us -> none  [local(): lax.psum((table_part, shift_part, grad_b_qv, grad_b_out, grad_b_cross_q,...]
    psum x5 -> x0, blocking collectives: 67.7 us -> none  [the longest x1 39.2 us: local(): lax.psum((table_part, shift_part, grad_b_qv, grad_b_out, grad_b_cross_q,...]
    ppermute x4 -> x79, starting transfers between devices: 5.8 us -> 67.3 us  [the longest x37 39.6 us: swap_dp(): lax.ppermute(value, 'dp', [(i, i ^ 1 << bit) for i in range(lax.axis_size...]
  transfers between devices with their start and end apart: 38 -> 79, of which waited for: 32 -> 39; matrix products, arithmetic and copies ran while one was open for 15% -> 29% of each run, Pallas kernels for 0% -> 5%
where the time goes in v1:
time: 740 us; the launch traced here: 734 us
  waiting for transfers between devices  397 us (54%)
  other arithmetic  85.4 us (12%)
  matrix products  77.5 us (10%)
  starting transfers between devices  67.3 us (9%)
  local copies, waits for them, and re-layouts  66.7 us (9%)
  Pallas kernels  35.5 us (5%)
    ppermute x42, waiting for transfers between devices, swap(): return lax.ppermute(value, axis, [(0, 1), (1, 0)])  231 us
    ppermute x37, waiting for transfers between devices, swap_dp(): lax.ppermute(value, 'dp', [(i, i ^ 1 << bit) for i in range(lax.axis_size...  166 us
    dot_general x27, matrix products, dot(): lax.dot_general(left, right, (((left_dim,), (right_dim,)), ((), ())), pre...  65.5 us
    ppermute x37, starting transfers between devices, swap_dp(): lax.ppermute(value, 'dp', [(i, i ^ 1 << bit) for i in range(lax.axis_size...  39.6 us
    ppermute x42, starting transfers between devices, swap(): return lax.ppermute(value, axis, [(0, 1), (1, 0)])  27.7 us
    pallas_call x2, Pallas kernels, attend_grad(): pl.pallas_call(partial(attend_grad_kernel, masked), grid=(heads,), in_spe...  21.6 us
    select_n x45, other arithmetic, pick(): return jnp.where(index == 0, pair_first, pair_second)  20 us
    unnamed x323, local copies, waits for them, and re-layouts  18.9 us
  transfers between devices with their start and end apart: 79, of which 39 were waited for; matrix products, arithmetic and copies ran while one was open for 29% of the time, Pallas kernels for 5%

profile of v1, /device:TPU:0, one launch (start us, length us, event | category | flops | bytes accessed | tf_op | source)
XLA Modules:
  0.0 733.5 jit_solution(13469649368492567363)
XLA Ops:
  30.1 5.0 collective-permute-done.61
  38.5 8.6 %collective-permute-done.2 = bf16[2,288,512]{2,1,0:T(8,128)(2,1)S(1)} collective-permute-done((bf16[2,288,512]{2,1,0:T(8,128)(2,1)S(1)}, bf16[2,288,512]{2,1,0:T(8,128)(2,1)S(1)}, u32[]{:S(2)}, u32[]{:S(2)}) %collective-permute-start.2) | collective-permute-done | bytes 589856 | tf_op jit(solution)/shard_map/ppermute | solution.py:28
  59.8 42.5 %collective-permute-done.6 = bf16[576,3,576]{2,0,1:T(8,128)(2,1)S(1)} collective-permute-done((bf16[576,3,576]{2,0,1:T(8,128)(2,1)S(1)}, bf16[576,3,576]{2,0,1:T(8,128)(2,1)S(1)}, u32[]{:S(2)}, u32[]{:S(2)}) %collective-permute-start.6) | collective-permute-done | bytes 1990688 | tf_op jit(solution)/shard_map/ppermute | solution.py:24
  108.7 9.5 %attend_fwd.2 = (bf16[8,72,512]{2,1,0:T(8,128)(2,1)S(1)}, f32[8,1,512]{2,1,0:T(1,128)S(1)}) custom-call(s32[1]{0:T(128)} %dynamic_slice.7.length_ref, bf16[8,72,512]{2,1,0:T(8,128)(2,1)S(1)} %bitcast.489, bf16[8,72,1024]{2,1,0:T(8,128)(2,1)S(1)} %bitcast.480, bf16[8,72,1024]{2,1,0:T(8,128)(2,1)S(1)} %bitcast.482), custom_call_target="tpu_custom_call" | custom-call | flops 2147483648 | bytes 3538944 | tf_op jit(solution)/shard_map/attend_fwd/pallas_call | solution.py:67
  125.2 16.3 %collective-permute-done.9 = bf16[576,576]{1,0:T(8,128)(2,1)S(1)} collective-permute-done((bf16[576,576]{1,0:T(8,128)(2,1)S(1)}, bf16[576,576]{1,0:T(8,128)(2,1)S(1)}, u32[]{:S(2)}, u32[]{:S(2)}) %collective-permute-start.9) | collective-permute-done | bytes 663584 | tf_op jit(solution)/shard_map/ppermute | solution.py:24
  149.1 9.9 %collective-permute-done.10 = bf16[576,576]{1,0:T(8,128)(2,1)S(1)} collective-permute-done((bf16[576,576]{1,0:T(8,128)(2,1)S(1)}, bf16[576,576]{1,0:T(8,128)(2,1)S(1)}, u32[]{:S(2)}, u32[]{:S(2)}) %collective-permute-start.10) | collective-permute-done | bytes 663584 | tf_op jit(solution)/shard_map/ppermute | solution.py:24
  166.6 50.0 %collective-permute-done.16 = bf16[576,2304]{1,0:T(8,128)(2,1)S(1)} collective-permute-done((bf16[576,2304]{1,0:T(8,128)(2,1)S(1)}, bf16[576,2304]{1,0:T(8,128)(2,1)S(1)}, u32[]{:S(2)}, u32[]{:S(2)}) %collective-permute-start.16) | collective-permute-done | bytes 2654240 | tf_op jit(solution)/shard_map/ppermute | solution.py:24
  229.4 6.4 copy.125
  235.8 6.1 convolution_convert_fusion.1
  246.9 30.5 %collective-permute-done.17 = bf16[2304,576]{0,1:T(8,128)(2,1)} collective-permute-done((bf16[2304,576]{0,1:T(8,128)(2,1)}, bf16[2304,576]{0,1:T(8,128)(2,1)}, u32[]{:S(2)}, u32[]{:S(2)}) %collective-permute-start.17) | collective-permute-done | bytes 2654240 | tf_op jit(solution)/shard_map/ppermute | solution.py:24
  280.8 5.7 fusion.131
  286.6 6.8 fusion.136
  315.1 21.7 %collective-permute-done.75 = bf16[2,2,2,288,576]{4,3,2,1,0:T(8,128)(2,1)} collective-permute-done((bf16[2,2,2,288,576]{4,3,2,1,0:T(8,128)(2,1)}, bf16[2,2,2,288,576]{4,3,2,1,0:T(8,128)(2,1)}, u32[]{:S(2)}, u32[]{:S(2)}) %collective-permute-start.75) | collective-permute-done | bytes 2654240 | tf_op jit(solution)/shard_map/ppermute | solution.py:24
  355.4 5.1 attend_bwd.2
  377.1 25.0 %collective-permute-done.76 = bf16[2,2,288,576]{3,2,1,0:T(8,128)(2,1)} collective-permute-done((bf16[2,2,288,576]{3,2,1,0:T(8,128)(2,1)}, bf16[2,2,288,576]{3,2,1,0:T(8,128)(2,1)}, u32[]{:S(2)}, u32[]{:S(2)}) %collective-permute-start.76) | collective-permute-done | bytes 1327136 | tf_op jit(solution)/shard_map/ppermute | solution.py:28
  411.3 5.5 collective-permute-done.34
  431.9 4.6 collective-permute-done.67
  439.6 11.1 %collective-permute-done.77 = bf16[2,288,576]{2,1,0:T(8,128)(2,1)} collective-permute-done((bf16[2,288,576]{2,1,0:T(8,128)(2,1)}, bf16[2,288,576]{2,1,0:T(8,128)(2,1)}, u32[]{:S(2)}, u32[]{:S(2)}) %collective-permute-start.77) | collective-permute-done | bytes 663584 | tf_op jit(solution)/shard_map/ppermute | solution.py:28
  455.2 7.0 collective-permute-done.58
  462.7 4.8 collective-permute-done.68
  469.2 7.2 collective-permute-done.78
  478.0 5.8 collective-permute-done.59
  494.1 16.5 %attend_bwd.3 = (bf16[8,72,512]{2,1,0:T(8,128)(2,1)S(1)}, bf16[8,72,1024]{2,1,0:T(8,128)(2,1)S(1)}, bf16[8,72,1024]{2,1,0:T(8,128)(2,1)S(1)}) custom-call(s32[1]{0:T(128)} %dynamic_slice.7.length_ref, bf16[8,72,512]{2,1,0:T(8,128)(2,1)S(1)} %bitcast.490, bf16[8,72,1024]{2,1,0:T(8,128)(2,1)S(1)} %bitcast.481, bf16[8,72,1024]{2,1,0:T(8,128)(2,1)S(1)} %bitcast.483, ...), custom_call_target="tpu_custom_call" | custom-call | flops 5368709120 | bytes 7077888 | tf_op jit(solution)/shard_map/attend_bwd/pallas_call | solution.py:112
  552.3 8.6 %collective-permute-done.49 = bf16[2,2,2,72,576]{4,3,1,2,0:T(8,128)(2,1)S(1)} collective-permute-done((bf16[2,2,2,72,576]{4,3,1,2,0:T(8,128)(2,1)S(1)}, bf16[2,2,2,72,576]{4,3,1,2,0:T(8,128)(2,1)S(1)}, u32[]{:S(2)}, u32[]{:S(2)}) %collective-permute-start.49) | collective-permute-done | bytes 663584 | tf_op jit(solution)/shard_map/ppermute | solution.py:28
  563.6 38.9 %collective-permute-done.53 = bf16[2,2,2,72,576]{4,3,1,2,0:T(8,128)(2,1)S(1)} collective-permute-done((bf16[2,2,2,72,576]{4,3,1,2,0:T(8,128)(2,1)S(1)}, bf16[2,2,2,72,576]{4,3,1,2,0:T(8,128)(2,1)S(1)}, u32[]{:S(2)}, u32[]{:S(2)}) %collective-permute-start.53) | collective-permute-done | bytes 663584 | tf_op jit(solution)/shard_map/ppermute | solution.py:28
  604.6 7.1 collective-permute-done.50
  613.7 6.7 collective-permute-done.42
  620.8 7.2 collective-permute-done.54
  628.1 6.9 collective-permute-done.51
  662.8 12.8 %collective-permute-done.37 = f32[4896]{0:T(1024)S(1)} collective-permute-done((f32[4896]{0:T(1024)S(1)}, f32[4896]{0:T(1024)S(1)}, u32[]{:S(2)}, u32[]{:S(2)}) %collective-permute-start.37) | collective-permute-done | bytes 19616 | tf_op jit(solution)/shard_map/ppermute | solution.py:24
  703.8 8.8 %collective-permute-done.40 = f32[32544]{0:T(1024)S(1)} collective-permute-done((f32[32544]{0:T(1024)S(1)}, f32[32544]{0:T(1024)S(1)}, u32[]{:S(2)}, u32[]{:S(2)}) %collective-permute-start.40) | collective-permute-done | bytes 130208 | tf_op jit(solution)/shard_map/ppermute | solution.py:28
  722.3 9.8 %collective-permute-done.74 = bf16[72,2304]{1,0:T(8,128)(2,1)S(1)} collective-permute-done((bf16[72,2304]{1,0:T(8,128)(2,1)S(1)}, bf16[72,2304]{1,0:T(8,128)(2,1)S(1)}, u32[]{:S(2)}, u32[]{:S(2)}) %collective-permute-start.74) | collective-permute-done | bytes 331808 | tf_op jit(solution)/shard_map/ppermute | solution.py:28
  (739 shorter events, 311.2 us)
Async XLA Ops:
  2.8 26.7 %collective-permute-start.22 = (bf16[288,512]{1,0:T(8,128)(2,1)}, bf16[288,512]{1,0:T(8,128)(2,1)S(1)}, u32[]{:S(2)}, u32[]{:S(2)}) collective-permute-start(bf16[288,512]{1,0:T(8,128)(2,1)} %get-tuple-element.145), channel_id=1, source_target_pairs={{0,2},{2,0},{1,3},{3,1},{4,6},{6,4},{5,7},{7,5},{8,10},{10,8},{9,1... | collective-permute-start | bytes 884744 | tf_op jit(solution)/shard_map/ppermute | solution.py:24
  7.3 21.0 %collective-permute-start = (bf16[288,512]{1,0:T(8,128)(2,1)}, bf16[288,512]{1,0:T(8,128)(2,1)}, u32[]{:S(2)}, u32[]{:S(2)}) collective-permute-start(bf16[288,512]{1,0:T(8,128)(2,1)} %get-tuple-element.147), channel_id=1, source_target_pairs={{0,2},{2,0},{1,3},{3,1},{4,6},{6,4},{5,7},{7,5},{8,10},{10,8},{9,1... | collective-permute-start | bytes 884744 | tf_op jit(solution)/shard_map/ppermute | solution.py:24
  29.4 23.0 %collective-permute-start.1 = (bf16[2,288,512]{2,1,0:T(8,128)(2,1)S(1)}, bf16[2,288,512]{2,1,0:T(8,128)(2,1)S(1)}, u32[]{:S(2)}, u32[]{:S(2)}) collective-permute-start(bf16[2,288,512]{2,1,0:T(8,128)(2,1)S(1)} %pad_maximum_fusion.32), channel_id=1, source_target_pairs={{0,1},{1,0},{2,3},{3,2},{4,5},{5,4},{6,7},{7,6},{8,9},{9,8},{10,11... | collective-permute-start | bytes 1769480 | tf_op jit(solution)/shard_map/ppermute | solution.py:24
  29.6 113.4 %collective-permute-start.23 = (bf16[2,288,512]{2,1,0:T(8,128)(2,1)S(1)}, bf16[2,288,512]{2,1,0:T(8,128)(2,1)S(1)}, u32[]{:S(2)}, u32[]{:S(2)}) collective-permute-start(bf16[2,288,512]{2,1,0:T(8,128)(2,1)S(1)} %pad_maximum_fusion.34), channel_id=1, source_target_pairs={{0,1},{1,0},{2,3},{3,2},{4,5},{5,4},{6,7},{7,6},{8,9},{9,8},{10,11... | collective-permute-start | bytes 1769480 | tf_op jit(solution)/shard_map/ppermute | solution.py:24
  47.2 74.1 %collective-permute-start.14 = (bf16[1152,120]{1,0:T(8,128)(2,1)S(1)}, bf16[1152,120]{1,0:T(8,128)(2,1)S(1)}, u32[]{:S(2)}, u32[]{:S(2)}) collective-permute-start(bf16[1152,120]{1,0:T(8,128)(2,1)S(1)} %pad_maximum_fusion.41), channel_id=1, source_target_pairs={{0,4},{4,0},{8,12},{12,8},{16,20},{20,16},{24,28},{28,24},{1,5},{5... | collective-permute-start | bytes 829448 | tf_op jit(solution)/shard_map/ppermute | solution.py:28
  49.8 648.2 %collective-permute-start.63 = (bf16[4,120,256]{2,1,0:T(8,128)(2,1)}, bf16[4,120,256]{2,1,0:T(8,128)(2,1)}, u32[]{:S(2)}, u32[]{:S(2)}) collective-permute-start(bf16[4,120,256]{2,1,0:T(8,128)(2,1)} %get-tuple-element.149), channel_id=1, source_target_pairs={{0,16},{4,20},{8,24},{12,28},{16,0},{20,4},{24,8},{28,12},{1,17},{... | collective-permute-start | bytes 737288 | tf_op jit(solution)/shard_map/ppermute | solution.py:28
  52.4 49.9 %collective-permute-start.6 = (bf16[576,3,576]{2,0,1:T(8,128)(2,1)S(1)}, bf16[576,3,576]{2,0,1:T(8,128)(2,1)S(1)}, u32[]{:S(2)}, u32[]{:S(2)}) collective-permute-start(bf16[576,3,576]{2,0,1:T(8,128)(2,1)S(1)} %copy-done.57), channel_id=1, source_target_pairs={{0,2},{2,0},{1,3},{3,1},{4,6},{6,4},{5,7},{7,5},{8,10},{10,8},{9,1... | collective-permute-start | bytes 5971976 | tf_op jit(solution)/shard_map/ppermute | solution.py:24
  158.9 57.6 %collective-permute-start.16 = (bf16[576,2304]{1,0:T(8,128)(2,1)S(1)}, bf16[576,2304]{1,0:T(8,128)(2,1)S(1)}, u32[]{:S(2)}, u32[]{:S(2)}) collective-permute-start(bf16[576,2304]{1,0:T(8,128)(2,1)S(1)} %copy-done.53), channel_id=1, source_target_pairs={{0,2},{2,0},{1,3},{3,1},{4,6},{6,4},{5,7},{7,5},{8,10},{10,8},{9,1... | collective-permute-start | bytes 7962632 | tf_op jit(solution)/shard_map/ppermute | solution.py:24
  166.4 53.6 %collective-permute-start.18 = (bf16[1152,256]{1,0:T(8,128)(2,1)S(1)}, bf16[1152,256]{1,0:T(8,128)(2,1)S(1)}, u32[]{:S(2)}, u32[]{:S(2)}) collective-permute-start(bf16[1152,256]{1,0:T(8,128)(2,1)S(1)} %add_convert_fusion.5), channel_id=1, source_target_pairs={{0,1},{1,0},{2,3},{3,2},{4,5},{5,4},{6,7},{7,6},{8,9},{9,8},{10,11... | collective-permute-start | bytes 1769480 | tf_op jit(solution)/shard_map/ppermute | solution.py:24
  216.6 60.8 %collective-permute-start.17 = (bf16[2304,576]{0,1:T(8,128)(2,1)}, bf16[2304,576]{0,1:T(8,128)(2,1)}, u32[]{:S(2)}, u32[]{:S(2)}) collective-permute-start(bf16[2304,576]{0,1:T(8,128)(2,1)} %param.39), channel_id=1, source_target_pairs={{0,2},{2,0},{1,3},{3,1},{4,6},{6,4},{5,7},{7,5},{8,10},{10,8},{9,1... | collective-permute-start | bytes 7962632 | tf_op jit(solution)/shard_map/ppermute | solution.py:24
  246.4 90.4 %collective-permute-start.75 = (bf16[2,2,2,288,576]{4,3,2,1,0:T(8,128)(2,1)}, bf16[2,2,2,288,576]{4,3,2,1,0:T(8,128)(2,1)}, u32[]{:S(2)}, u32[]{:S(2)}) collective-permute-start(bf16[2,2,2,288,576]{4,3,2,1,0:T(8,128)(2,1)} %bitcast.513), channel_id=1, source_target_pairs={{0,2},{2,0},{1,3},{3,1},{4,6},{6,4},{5,7},{7,5},{8,10},{10,8},{9,1... | collective-permute-start | bytes 7962632 | tf_op jit(solution)/shard_map/ppermute | solution.py:24
  309.8 235.3 %collective-permute-start.71 = (bf16[2,2,2,72,2304]{4,3,1,2,0:T(8,128)(2,1)}, bf16[2,2,2,72,2304]{4,3,1,2,0:T(8,128)(2,1)}, u32[]{:S(2)}, u32[]{:S(2)}) collective-permute-start(bf16[2,2,2,72,2304]{4,3,1,2,0:T(8,128)(2,1)} %select_bitcast_fusion), channel_id=1, source_target_pairs={{0,4},{4,0},{8,12},{12,8},{16,20},{20,16},{24,28},{28,24},{1,5},{5... | collective-permute-start | bytes 7962632 | tf_op jit(solution)/shard_map/ppermute | solution.py:28
  315.0 25.2 %collective-permute-start.20 = (bf16[2,288,256]{2,1,0:T(8,128)(2,1)S(1)}, bf16[2,288,256]{2,1,0:T(8,128)(2,1)S(1)}, u32[]{:S(2)}, u32[]{:S(2)}) collective-permute-start(bf16[2,288,256]{2,1,0:T(8,128)(2,1)S(1)} %select_bitcast_fusion.22), channel_id=1, source_target_pairs={{0,1},{1,0},{2,3},{3,2},{4,5},{5,4},{6,7},{7,6},{8,9},{9,8},{10,11... | collective-permute-start | bytes 884744 | tf_op jit(solution)/shard_map/ppermute | solution.py:24
  344.1 58.0 %collective-permute-start.76 = (bf16[2,2,288,576]{3,2,1,0:T(8,128)(2,1)}, bf16[2,2,288,576]{3,2,1,0:T(8,128)(2,1)}, u32[]{:S(2)}, u32[]{:S(2)}) collective-permute-start(bf16[2,2,288,576]{3,2,1,0:T(8,128)(2,1)} %fusion.18), channel_id=1, source_target_pairs={{0,4},{4,0},{8,12},{12,8},{16,20},{20,16},{24,28},{28,24},{1,5},{5... | collective-permute-start | bytes 3981320 | tf_op jit(solution)/shard_map/ppermute | solution.py:28
  362.6 61.9 %collective-permute-start.26 = (bf16[1152,256]{1,0:T(8,128)(2,1)}, bf16[1152,256]{1,0:T(8,128)(2,1)}, u32[]{:S(2)}, u32[]{:S(2)}) collective-permute-start(bf16[1152,256]{1,0:T(8,128)(2,1)} %slice.1314), channel_id=1, source_target_pairs={{0,1},{1,0},{2,3},{3,2},{4,5},{5,4},{6,7},{7,6},{8,9},{9,8},{10,11... | collective-permute-start | bytes 1769480 | tf_op jit(solution)/shard_map/ppermute | solution.py:24
  363.2 44.4 %collective-permute-start.33 = (bf16[2,576,120]{2,1,0:T(8,128)(2,1)S(1)}, bf16[2,576,120]{2,1,0:T(8,128)(2,1)}, u32[]{:S(2)}, u32[]{:S(2)}) collective-permute-start(bf16[2,576,120]{2,1,0:T(8,128)(2,1)S(1)} %bitcast.524), channel_id=1, source_target_pairs={{0,4},{4,0},{8,12},{12,8},{16,20},{20,16},{24,28},{28,24},{1,5},{5... | collective-permute-start | bytes 829448 | tf_op jit(solution)/shard_map/ppermute | solution.py:28
  402.1 28.3 %collective-permute-start.57 = (bf16[2,2,2,72,576]{4,3,1,2,0:T(8,128)(2,1)}, bf16[2,2,2,72,576]{4,3,1,2,0:T(8,128)(2,1)}, u32[]{:S(2)}, u32[]{:S(2)}) collective-permute-start(bf16[2,2,2,72,576]{4,3,1,2,0:T(8,128)(2,1)} %select_bitcast_fusion.2), channel_id=1, source_target_pairs={{0,8},{4,12},{8,0},{12,4},{16,24},{20,28},{24,16},{28,20},{1,9},{5... | collective-permute-start | bytes 1990664 | tf_op jit(solution)/shard_map/ppermute | solution.py:28
  416.8 19.7 %collective-permute-start.67 = (bf16[2,2,2,72,576]{4,3,1,2,0:T(8,128)(2,1)}, bf16[2,2,2,72,576]{4,3,1,2,0:T(8,128)(2,1)}, u32[]{:S(2)}, u32[]{:S(2)}) collective-permute-start(bf16[2,2,2,72,576]{4,3,1,2,0:T(8,128)(2,1)} %select_bitcast_fusion.1), channel_id=1, source_target_pairs={{0,8},{4,12},{8,0},{12,4},{16,24},{20,28},{24,16},{28,20},{1,9},{5... | collective-permute-start | bytes 1990664 | tf_op jit(solution)/shard_map/ppermute | solution.py:28
  424.5 26.2 %collective-permute-start.77 = (bf16[2,288,576]{2,1,0:T(8,128)(2,1)}, bf16[2,288,576]{2,1,0:T(8,128)(2,1)}, u32[]{:S(2)}, u32[]{:S(2)}) collective-permute-start(bf16[2,288,576]{2,1,0:T(8,128)(2,1)} %fusion.48), channel_id=1, source_target_pairs={{0,8},{4,12},{8,0},{12,4},{16,24},{20,28},{24,16},{28,20},{1,9},{5... | collective-permute-start | bytes 1990664 | tf_op jit(solution)/shard_map/ppermute | solution.py:28
  438.6 51.5 %collective-permute-start.27 = (bf16[1152,256]{1,0:T(8,128)(2,1)S(1)}, bf16[1152,256]{1,0:T(8,128)(2,1)S(1)}, u32[]{:S(2)}, u32[]{:S(2)}) collective-permute-start(bf16[1152,256]{1,0:T(8,128)(2,1)S(1)} %multiply_convert_fusion.2), channel_id=1, source_target_pairs={{0,1},{1,0},{2,3},{3,2},{4,5},{5,4},{6,7},{7,6},{8,9},{9,8},{10,11... | collective-permute-start | bytes 1769480 | tf_op jit(solution)/shard_map/ppermute | solution.py:24
  467.5 75.0 %collective-permute-start.65 = (bf16[2,2,576,120]{3,2,0,1:T(8,128)(2,1)}, bf16[2,2,576,120]{3,2,0,1:T(8,128)(2,1)}, u32[]{:S(2)}, u32[]{:S(2)}) collective-permute-start(bf16[2,2,576,120]{3,2,0,1:T(8,128)(2,1)} %pad_maximum_fusion.35), channel_id=1, source_target_pairs={{0,8},{4,12},{8,0},{12,4},{16,24},{20,28},{24,16},{28,20},{1,9},{5... | collective-permute-start | bytes 1658888 | tf_op jit(solution)/shard_map/ppermute | solution.py:28
  489.3 51.0 %collective-permute-start.60 = (bf16[72,576]{1,0:T(8,128)(2,1)}, bf16[72,576]{1,0:T(8,128)(2,1)S(1)}, u32[]{:S(2)}, u32[]{:S(2)}) collective-permute-start(bf16[72,576]{1,0:T(8,128)(2,1)} %select_bitcast_fusion.36), channel_id=1, source_target_pairs={{0,16},{4,20},{8,24},{12,28},{16,0},{20,4},{24,8},{28,12},{1,17},{... | collective-permute-start | bytes 248840 | tf_op jit(solution)/shard_map/ppermute | solution.py:28
  490.1 51.1 %collective-permute-start.70 = (bf16[72,576]{1,0:T(8,128)(2,1)}, bf16[72,576]{1,0:T(8,128)(2,1)S(1)}, u32[]{:S(2)}, u32[]{:S(2)}) collective-permute-start(bf16[72,576]{1,0:T(8,128)(2,1)} %select_bitcast_fusion.35), channel_id=1, source_target_pairs={{0,16},{4,20},{8,24},{12,28},{16,0},{20,4},{24,8},{28,12},{1,17},{... | collective-permute-start | bytes 248840 | tf_op jit(solution)/shard_map/ppermute | solution.py:28
  541.3 112.3 %collective-permute-start.28 = (bf16[1152,256]{1,0:T(8,128)(2,1)S(1)}, bf16[1152,256]{1,0:T(8,128)(2,1)S(1)}, u32[]{:S(2)}, u32[]{:S(2)}) collective-permute-start(bf16[1152,256]{1,0:T(8,128)(2,1)S(1)} %copy-done.101), channel_id=1, source_target_pairs={{0,1},{1,0},{2,3},{3,2},{4,5},{5,4},{6,7},{7,6},{8,9},{9,8},{10,11... | collective-permute-start | bytes 1769480 | tf_op jit(solution)/shard_map/ppermute | solution.py:24
  542.4 18.5 %collective-permute-start.49 = (bf16[2,2,2,72,576]{4,3,1,2,0:T(8,128)(2,1)S(1)}, bf16[2,2,2,72,576]{4,3,1,2,0:T(8,128)(2,1)S(1)}, u32[]{:S(2)}, u32[]{:S(2)}) collective-permute-start(bf16[2,2,2,72,576]{4,3,1,2,0:T(8,128)(2,1)S(1)} %select_bitcast_fusion.4), channel_id=1, source_target_pairs={{0,4},{4,0},{8,12},{12,8},{16,20},{20,16},{24,28},{28,24},{1,5},{5... | collective-permute-start | bytes 1990664 | tf_op jit(solution)/shard_map/ppermute | solution.py:28
  550.7 52.0 %collective-permute-start.41 = (bf16[2,2,2,72,576]{4,3,2,1,0:T(8,128)(2,1)S(1)}, bf16[2,2,2,72,576]{4,3,2,1,0:T(8,128)(2,1)S(1)}, u32[]{:S(2)}, u32[]{:S(2)}) collective-permute-start(bf16[2,2,2,72,576]{4,3,2,1,0:T(8,128)(2,1)S(1)} %get-tuple-element.115), channel_id=1, source_target_pairs={{0,8},{4,12},{8,0},{12,4},{16,24},{20,28},{24,16},{28,20},{1,9},{5... | collective-permute-start | bytes 1990664 | tf_op jit(solution)/shard_map/ppermute | solution.py:28
  560.9 41.6 %collective-permute-start.53 = (bf16[2,2,2,72,576]{4,3,1,2,0:T(8,128)(2,1)S(1)}, bf16[2,2,2,72,576]{4,3,1,2,0:T(8,128)(2,1)S(1)}, u32[]{:S(2)}, u32[]{:S(2)}) collective-permute-start(bf16[2,2,2,72,576]{4,3,1,2,0:T(8,128)(2,1)S(1)} %select_bitcast_fusion.3), channel_id=1, source_target_pairs={{0,8},{4,12},{8,0},{12,4},{16,24},{20,28},{24,16},{28,20},{1,9},{5... | collective-permute-start | bytes 1990664 | tf_op jit(solution)/shard_map/ppermute | solution.py:28
  563.3 134.7 %collective-permute-start.66 = (bf16[4,2,576,120]{3,2,0,1:T(8,128)(2,1)}, bf16[4,2,576,120]{3,2,0,1:T(8,128)(2,1)}, u32[]{:S(2)}, u32[]{:S(2)}) collective-permute-start(bf16[4,2,576,120]{3,2,0,1:T(8,128)(2,1)} %pad_maximum_fusion.15), channel_id=1, source_target_pairs={{0,16},{4,20},{8,24},{12,28},{16,0},{20,4},{24,8},{28,12},{1,17},{... | collective-permute-start | bytes 3317768 | tf_op jit(solution)/shard_map/ppermute | solution.py:28
  612.1 42.5 %collective-permute-start.30 = (bf16[1152,256]{1,0:T(8,128)(2,1)S(1)}, bf16[1152,256]{1,0:T(8,128)(2,1)S(1)}, u32[]{:S(2)}, u32[]{:S(2)}) collective-permute-start(bf16[1152,256]{1,0:T(8,128)(2,1)S(1)} %fusion.33), channel_id=1, source_target_pairs={{0,4},{4,0},{8,12},{12,8},{16,20},{20,16},{24,28},{28,24},{1,5},{5... | collective-permute-start | bytes 1769480 | tf_op jit(solution)/shard_map/ppermute | solution.py:28
  651.7 41.4 %collective-permute-start.72 = (bf16[2,2,72,2304]{3,2,0,1:T(8,128)(2,1)}, bf16[2,2,72,2304]{3,2,0,1:T(8,128)(2,1)}, u32[]{:S(2)}, u32[]{:S(2)}) collective-permute-start(bf16[2,2,72,2304]{3,2,0,1:T(8,128)(2,1)} %slice_bitcast_fusion), channel_id=1, source_target_pairs={{0,2},{2,0},{1,3},{3,1},{4,6},{6,4},{5,7},{7,5},{8,10},{10,8},{9,1... | collective-permute-start | bytes 3981320 | tf_op jit(solution)/shard_map/ppermute | solution.py:24
  653.5 24.7 %collective-permute-start.52 = (bf16[72,576]{1,0:T(8,128)(2,1)}, bf16[72,576]{1,0:T(8,128)(2,1)}, u32[]{:S(2)}, u32[]{:S(2)}) collective-permute-start(bf16[72,576]{1,0:T(8,128)(2,1)} %select_bitcast_fusion.38), channel_id=1, source_target_pairs={{0,16},{4,20},{8,24},{12,28},{16,0},{20,4},{24,8},{28,12},{1,17},{... | collective-permute-start | bytes 248840 | tf_op jit(solution)/shard_map/ppermute | solution.py:28
  696.1 20.1 %collective-permute-start.73 = (bf16[2,72,2304]{2,1,0:T(8,128)(2,1)}, bf16[2,72,2304]{2,1,0:T(8,128)(2,1)}, u32[]{:S(2)}, u32[]{:S(2)}) collective-permute-start(bf16[2,72,2304]{2,1,0:T(8,128)(2,1)} %select_bitcast_fusion.6), channel_id=1, source_target_pairs={{0,8},{4,12},{8,0},{12,4},{16,24},{20,28},{24,16},{28,20},{1,9},{5... | collective-permute-start | bytes 1990664 | tf_op jit(solution)/shard_map/ppermute | solution.py:28
  (203 other events, 2258.7 us)

commit v2 on v1

v2 whole, which is shorter than its diff:
```python
from functools import partial

import jax
import jax.numpy as jnp
from jax import lax
from jax.experimental import pallas as pl
from jax.experimental.pallas import tpu as pltpu
from jax.sharding import PartitionSpec as P

HD = 72
TXT = 120
TXT_PAD = 128
SEQ_DEV = 512
LPP = 2
HALF = 256

norm_eps = 1e-06
masked_score = -1000000000.0
f32 = jnp.float32
bf16 = jnp.bfloat16
SMALL_COST = pl.CostEstimate(flops=1, bytes_accessed=1, transcendentals=0)


def swap(value, axis):
    return lax.ppermute(value, axis, [(0, 1), (1, 0)])


def swap_dp(value, bit):
    return lax.ppermute(value, "dp", [(i, i ^ (1 << bit)) for i in range(lax.axis_size("dp"))])


def pick(pair_first, pair_second, index):
    return jnp.where(index == 0, pair_first, pair_second)


def in_order(mine, other, index, axis):
    return jnp.concatenate([pick(mine, other, index), pick(other, mine, index)], axis=axis)


def after(value, *earlier):
    return lax.optimization_barrier((value, *earlier))[0]


def dot(left, right, left_dim, right_dim):
    return lax.dot_general(
        left, right, (((left_dim,), (right_dim,)), ((), ())), preferred_element_type=f32
    )


def scores_of(masked, length_ref, q, k):
    scores = dot(k, q, 0, 0) * (HD ** (-0.5))
    if masked:
        place = lax.broadcasted_iota(jnp.int32, scores.shape, 0)
        scores = jnp.where(place < length_ref[0], scores, masked_score)
    return scores


def attend_kernel(masked, length_ref, q_ref, k_ref, v_ref, o_ref, log_ref):
    scores = scores_of(masked, length_ref, q_ref[0], k_ref[0])
    largest = jnp.max(scores, axis=0, keepdims=True)
    raised = jnp.exp(scores - largest)
    total = jnp.sum(raised, axis=0, keepdims=True)
    mixture = dot(v_ref[0], raised.astype(bf16), 1, 0)
    o_ref[0] = (mixture / total).astype(bf16)
    log_ref[0] = largest + jnp.log(total)


def attend(q, k, v, length, masked):
    heads, hd, nq = q.shape
    nk = k.shape[2]
    head = lambda h: (h, 0, 0)
    return pl.pallas_call(
        partial(attend_kernel, masked),
        grid=(heads,),
        in_specs=[
            pl.BlockSpec(memory_space=pltpu.SMEM),
            pl.BlockSpec((1, hd, nq), head),
            pl.BlockSpec((1, hd, nk), head),
            pl.BlockSpec((1, hd, nk), head),
        ],
        out_specs=[pl.BlockSpec((1, hd, nq), head), pl.BlockSpec((1, 1, nq), head)],
        out_shape=[
            jax.ShapeDtypeStruct((heads, hd, nq), bf16),
            jax.ShapeDtypeStruct((heads, 1, nq), f32),
        ],
        compiler_params=pltpu.CompilerParams(vmem_limit_bytes=32 * 2**20),
        cost_estimate=SMALL_COST,
        name="attend_fwd",
    )(length, q, k, v)


def attend_grad_kernel(
    masked, length_ref, q_ref, k_ref, v_ref, g_ref, log_ref, dq_ref, dk_ref, dv_ref
):
    q, k, v, g = q_ref[0], k_ref[0], v_ref[0], g_ref[0]
    weights = jnp.exp(scores_of(masked, length_ref, q, k) - log_ref[0])
    grad_weights = dot(v, g, 0, 0)
    crossed = jnp.sum(grad_weights * weights, axis=0, keepdims=True)
    grad_scores = (weights * (grad_weights - crossed)).astype(bf16)
    dq_ref[0] = (dot(k, grad_scores, 1, 0) * (HD ** (-0.5))).astype(bf16)
    dk_ref[0] = (dot(q, grad_scores, 1, 1) * (HD ** (-0.5))).astype(bf16)
    dv_ref[0] = dot(g, weights.astype(bf16), 1, 1).astype(bf16)


def attend_grad(q, k, v, g, log_total, length, masked):
    heads, hd, nq = q.shape
    nk = k.shape[2]
    head = lambda h: (h, 0, 0)
    queries, keys = pl.BlockSpec((1, hd, nq), head), pl.BlockSpec((1, hd, nk), head)
    return pl.pallas_call(
        partial(attend_grad_kernel, masked),
        grid=(heads,),
        in_specs=[
            pl.BlockSpec(memory_space=pltpu.SMEM),
            queries,
            keys,
            keys,
            queries,
            pl.BlockSpec((1, 1, nq), head),
        ],
        out_specs=[queries, keys, keys],
        out_shape=[
            jax.ShapeDtypeStruct((heads, hd, nq), bf16),
            jax.ShapeDtypeStruct((heads, hd, nk), bf16),
            jax.ShapeDtypeStruct((heads, hd, nk), bf16),
        ],
        compiler_params=pltpu.CompilerParams(vmem_limit_bytes=40 * 2**20),
        cost_estimate=SMALL_COST,
        name="attend_bwd",
    )(length, q, k, v, g, log_total)


def assemble_kernel(kind, core_ref, mine_ref, other_ref, vectors_ref, *outs):
    quarter = mine_ref.shape[1]
    held = outs[-1]
    core = core_ref[0]
    for row in range(2):
        mine = pl.multiple_of((2 * row + core) * quarter, 16)
        other = pl.multiple_of((2 * row + 1 - core) * quarter, 16)
        held[pl.ds(mine, quarter), :] = mine_ref[row].astype(f32)
        held[pl.ds(other, quarter), :] = other_ref[row].astype(f32)
    state = held[...]
    if kind == "gate":
        outs[0][...] = state.astype(bf16)
        outs[1][...] = (state * vectors_ref[:, 5:6]).astype(bf16)
    else:
        mean = jnp.mean(state, axis=0, keepdims=True)
        center = state - mean
        inverse = lax.rsqrt(jnp.mean(center * center, axis=0, keepdims=True) + norm_eps)
        outs[0][...] = state.astype(bf16)
        scale, shift = 1.0 + vectors_ref[:, 1:2], vectors_ref[:, 0:1]
        outs[1][...] = (center * inverse * scale + shift).astype(bf16)
        outs[2][...] = mean
        outs[3][...] = inverse


def assemble(kind, mine, other, core, vectors):
    _, quarter, tokens = mine.shape
    features = 4 * quarter
    place = lambda t, core_ref: (0, 0, t - t % 2 + (t + core_ref[0]) % 2)
    columns = pl.BlockSpec(vectors.shape, lambda t, core_ref: (0, 0))
    block = pl.BlockSpec((features, HALF), lambda t, core_ref: (0, t))
    line = pl.BlockSpec((1, HALF), lambda t, core_ref: (0, t))
    outs, shapes = [block, block], [jax.ShapeDtypeStruct((features, tokens), bf16)] * 2
    if kind == "norm":
        outs, shapes = outs + [line] * 2, shapes + [jax.ShapeDtypeStruct((1, tokens), f32)] * 2
    return pl.pallas_call(
        partial(assemble_kernel, kind),
        grid_spec=pltpu.PrefetchScalarGridSpec(
            num_scalar_prefetch=1,
            grid=(tokens // HALF,),
            in_specs=[pl.BlockSpec((2, quarter, HALF), place)] * 2 + [columns],
            out_specs=outs,
            scratch_shapes=[pltpu.VMEM((features, HALF), f32)],
        ),
        out_shape=shapes,
        compiler_params=pltpu.CompilerParams(vmem_limit_bytes=32 * 2**20),
        cost_estimate=SMALL_COST,
        name="assemble_" + kind,
    )(core, mine, other, vectors)


class Weight:
    def __init__(self, pieces, places):
        self.arrays = [array for array, _ in pieces]
        self.leads = [lead for _, lead in pieces]
        self.rows = [array.shape[-2] for array in self.arrays]
        self.n = self.arrays[0].shape[-1]
        self.places = jnp.stack([jnp.asarray(place, jnp.int32) for place in places])

    def specs(self, cols, column):
        def spec(rows, lead):
            if lead is None:
                return pl.BlockSpec((rows, cols), lambda *grid: (0, column(*grid)))
            return pl.BlockSpec((None, rows, cols), lambda *grid: (lead, 0, column(*grid)))

        return [spec(rows, lead) for rows, lead in zip(self.rows, self.leads)]


def place_of(places_ref, index):
    return pl.multiple_of(places_ref[index], 16)


def gelu_parts(v):
    inner = 0.7978845608028654 * (v + 0.044715 * (v * v * v))
    bent = jnp.tanh(inner)
    slope = 0.7978845608028654 * (1.0 + 3 * 0.044715 * (v * v))
    return 0.5 * v * (1.0 + bent), 0.5 * (1.0 + bent) + 0.5 * v * (1.0 - bent * bent) * slope


def rows_in_kernel(count, kind, lane, places_ref, x_ref, *refs):
    pieces, rest = refs[:count], refs[count:]
    total = None
    for index, piece in enumerate(pieces):
        rows = x_ref[pl.ds(place_of(places_ref, index), piece.shape[0]), :]
        part = dot(piece[...], rows, 0, 0)
        total = part if total is None else total + part
    if kind == "plain":
        rest[0][...] = total.astype(bf16)
    elif kind == "bias":
        rest[1][...] = (total + rest[0][:, lane : lane + 1]).astype(bf16)
    elif kind == "gelu":
        value, slope = gelu_parts(total + rest[0][...])
        rest[1][...] = value.astype(bf16)
        rest[2][...] = slope.astype(bf16)
    elif kind == "slope":
        grad = total * rest[0][...].astype(f32)
        rest[1][...] = grad.astype(bf16)
        rest[2][...] = jnp.sum(grad, axis=1, keepdims=True)


def rows_in(weight, x, kind="plain", operand=None, lane=0):
    k, tokens = x.shape
    n = weight.n
    cols = 768 if n % 768 == 0 else n
    wide = min(tokens, 512)
    out_block = pl.BlockSpec((cols, wide), lambda i, t: (i, t))
    column = pl.BlockSpec((cols, 1), lambda i, t: (i, 0))
    out = jax.ShapeDtypeStruct((n, tokens), bf16)
    lanes = pl.BlockSpec((cols, operand.shape[1]), lambda i, t: (i, 0)) if kind == "bias" else None
    extra = {"plain": [], "bias": [lanes], "gelu": [column], "slope": [out_block]}[kind]
    specs, shapes = [out_block], [out]
    if kind == "gelu":
        specs, shapes = [out_block] * 2, [out] * 2
    if kind == "slope":
        specs, shapes = [out_block, column], [out, jax.ShapeDtypeStruct((n, 1), f32)]
    result = pl.pallas_call(
        partial(rows_in_kernel, len(weight.arrays), kind, lane),
        grid=(n // cols, tokens // wide),
        in_specs=[
            pl.BlockSpec(memory_space=pltpu.SMEM),
            pl.BlockSpec((k, wide), lambda i, t: (0, t)),
        ]
        + weight.specs(cols, lambda i, t: i)
        + extra,
        out_specs=specs,
        out_shape=shapes,
        compiler_params=pltpu.CompilerParams(vmem_limit_bytes=48 * 2**20),
        cost_estimate=SMALL_COST,
        name="rows_in_" + kind,
    )(weight.places, x, *weight.arrays, *([] if operand is None else [operand]))
    return result[0] if len(result) == 1 else result


def rows_out_kernel(counts, steps, *refs):
    sides = len(counts)
    places, ys = refs[:sides], refs[sides : 2 * sides]
    pieces, (keep_ref, send_ref) = refs[2 * sides : -2], refs[-2:]
    step = pl.program_id(0)

    def rows_of(side, index, piece):
        return pl.ds(place_of(places[side], index), piece.shape[0])

    def write(target, active):
        start = 0
        for side in range(sides):
            if side in active:
                for index, piece in enumerate(pieces[start : start + counts[side]]):
                    rows = rows_of(side, index, piece)
                    part = dot(piece[...], ys[side][...], 1, 0)
                    if side != active[0]:
                        part = part + target[rows, :].astype(f32)
                    target[rows, :] = part.astype(target.dtype)
            start += counts[side]

    for number in range(max(steps)):
        active = [side for side in range(sides) if number < steps[side]]

        @pl.when(step == number)
        def _():
            write(keep_ref if number % 2 == 0 else send_ref, active)


def rows_out(pairs):
    k = 2 * pairs[0][0].rows[0]
    steps = [y.shape[1] // HALF for _, y in pairs]
    most = max(steps)

    def y_spec(y, count):
        return pl.BlockSpec((y.shape[0], HALF), lambda t: (0, jnp.minimum(t, count - 1)))

    in_specs = [pl.BlockSpec(memory_space=pltpu.SMEM) for _ in pairs]
    in_specs += [y_spec(y, count) for (_, y), count in zip(pairs, steps)]
    operands = [w.places for w, _ in pairs] + [y for _, y in pairs]
    for w, _ in pairs:
        in_specs += w.specs(w.n, lambda t: 0)
        operands += w.arrays
    width = most // 2 * HALF
    out_block = pl.BlockSpec((k, HALF), lambda t: (0, t // 2))
    return pl.pallas_call(
        partial(rows_out_kernel, [len(w.arrays) for w, _ in pairs], steps),
        grid=(most,),
        in_specs=in_specs,
        out_specs=[out_block, out_block],
        out_shape=[jax.ShapeDtypeStruct((k, width), f32), jax.ShapeDtypeStruct((k, width), bf16)],
        compiler_params=pltpu.CompilerParams(vmem_limit_bytes=48 * 2**20),
        cost_estimate=SMALL_COST,
        name="rows_out",
    )(*operands)


def weight_grad_kernel(inputs_ref, grads_ref, out_ref):
    out_ref[0] = dot(inputs_ref[...], grads_ref[0], 1, 1).astype(bf16)


def weight_grad(inputs, grads, first=0, groups=None):
    k, tokens = inputs.shape
    total, n, _ = grads.shape
    groups = total if groups is None else groups
    rows = 384 if k % 384 == 0 else 288
    return pl.pallas_call(
        weight_grad_kernel,
        grid=(groups, k // rows),
        in_specs=[
            pl.BlockSpec((rows, tokens), lambda g, i: (i, 0)),
            pl.BlockSpec((1, n, tokens), lambda g, i: (first + g, 0, 0)),
        ],
        out_specs=pl.BlockSpec((1, rows, n), lambda g, i: (g, i, 0)),
        out_shape=jax.ShapeDtypeStruct((groups, k, n), bf16),
        compiler_params=pltpu.CompilerParams(vmem_limit_bytes=40 * 2**20),
        cost_estimate=SMALL_COST,
        name="weight_grad",
    )(inputs, grads)


def norm_forward(state):
    center = state - jnp.mean(state, axis=0, keepdims=True)
    inverse = lax.rsqrt(jnp.mean(center * center, axis=0, keepdims=True) + norm_eps)
    return (center * inverse, inverse)


def norm_backward(grad_normed, normed, inverse):
    return inverse * (
        grad_normed
        - jnp.mean(grad_normed, axis=0, keepdims=True)
        - normed * jnp.mean(grad_normed * normed, axis=0, keepdims=True)
    )


def split_sum(pairs):
    keep, send = rows_out(pairs)
    return keep + swap(send, "col").astype(f32)


def join_cols(own):
    return jnp.concatenate([own, swap(own, "col")], axis=1)


def reduce_pieces(held, order, dp_index):
    bits = lax.axis_size("dp").bit_length() - 1
    left = ["row"] + list(range(bits - 1, -1, -1))
    for step, name in enumerate(order):
        axis = left.index(name)
        if name == "row":
            keep = lax.index_in_dim(held, 0, axis, keepdims=False)
            send = lax.index_in_dim(held, 1, axis, keepdims=False)
        else:
            bit = (dp_index >> name) & 1
            keep = lax.dynamic_index_in_dim(held, bit, axis, keepdims=False)
            send = lax.dynamic_index_in_dim(held, 1 - bit, axis, keepdims=False)
        got = yield (name, send)
        left.pop(axis)
        held = keep.astype(f32) + got.astype(f32)
        if step < len(order) - 1:
            held = held.astype(bf16)
    return held


class Task:
    def __init__(self, steps):
        self.steps, self.done, self.result, self.half = steps, False, None, None


class Links:
    def __init__(self):
        self.free, self.events, self.waits = {}, [], []
        self.last, self.now, self.count, self.halves = None, 0.0, 0, []

    def push(self, time, task, got, tie):
        self.count += 1
        self.events.append((time, self.count, task, got, tie))

    def spawn(self, steps):
        task = Task(steps)
        self.push(self.now, task, None, False)
        return task

    def ask(self, task, request):
        kind = request[0]
        if kind == "wait":
            self.waits.append((task, request[1]))
            return
        if kind == "half":
            self.halves.append((task, request[1]))
            return
        if kind == "set":
            task.half = request[1]
            self.push(self.now, task, None, False)
            return
        if kind == "compute":
            end = max(self.now, self.free.get("compute", 0.0)) + request[2]
            self.free["compute"] = end
            self.push(end, task, request[1], True)
            return
        value = request[1]
        link = {"row": "x", 0: "y"}.get(kind, "z")
        hops = 2 ** max(kind - 1, 0) if isinstance(kind, int) else 1
        end = max(self.now, self.free.get(link, 0.0)) + 2.0
        end += hops * value.size * value.dtype.itemsize / 46e3
        self.free[link] = end
        got = swap_dp(value, kind) if isinstance(kind, int) else swap(value, kind)
        self.push(end, task, got, True)

    def run(self):
        while self.events:
            event = min(self.events, key=lambda item: item[:2])
            self.events.remove(event)
            self.now, _, task, got, tie = event
            if tie:
                if self.last is not None:
                    got = after(got, self.last)
                self.last = got
            try:
                self.ask(task, task.steps.send(got))
            except StopIteration as stop:
                task.done, task.result = True, stop.value
            still = []
            for waiting, others in self.waits:
                if all(other.done for other in others):
                    self.push(self.now, waiting, [other.result for other in others], False)
                else:
                    still.append((waiting, others))
            self.waits = still
            for waiting, other in [pair for pair in self.halves if pair[1].half is not None]:
                self.halves.remove((waiting, other))
                self.push(self.now, waiting, None, False)


def local(
    latents,
    text,
    text_len,
    time_ids,
    time_table,
    shift_table,
    w_qkv,
    b_qv,
    w_out,
    b_out,
    w_cross_q,
    b_cross_q,
    w_cross_kv,
    b_cross_v,
    w_cross_out,
    b_cross_out,
    w_fc1,
    b_fc1,
    w_fc2,
    b_fc2,
    grad_out,
):
    quarter = latents.shape[1]
    half = 2 * quarter
    heads = half // HD
    n_dp = lax.axis_size("dp")
    bits = n_dp.bit_length() - 1
    d = lax.axis_index("dp")
    r = lax.axis_index("row")
    c = lax.axis_index("col")
    upper = d % 2
    pair = d // 2
    my_latent = pair * LPP + r

    def own_and_sent(values):
        turned = values.T
        return tuple(
            lax.dynamic_slice_in_dim(turned, place * SEQ_DEV, SEQ_DEV, 1) for place in (r, 1 - r)
        )

    links = Links()
    core = c[None].astype(jnp.int32)

    def fetch(blocks, first, bit, behind, *choices):
        w, (rows, n) = len(choices), blocks.shape[1:]
        if behind is not None:
            yield ("half", behind)
            blocks = after(blocks, behind.half)
        mine = (d >> bit) & 1
        half_rows = rows // 2
        got = yield (
            "row",
            lax.dynamic_slice(blocks, (first, mine * half_rows, 0), (w, half_rows, n)),
        )
        yield ("set", got)
        relayed = yield (bit, got)
        more = [(got, rows + half_rows * mine), (relayed, rows + half_rows * (1 - mine))]
        return [
            Weight([own] + [(array, i) for array, _ in more], [0] + [place for _, place in more])
            for i, own in enumerate(choices)
        ]

    def near_task(values):
        own, sent = own_and_sent(values)
        return jnp.stack([own, (yield ("row", sent))])

    def latents_in_task():
        near = yield from near_task(latents)
        far = yield (0, near)
        both = jnp.concatenate([near, far], axis=-1)
        return both, swap(both, "col")

    def grad_out_task():
        near = yield from near_task(grad_out)
        return near, swap(near, "col")

    def vectors_in_task():
        pair_times = lax.dynamic_slice_in_dim(time_ids, pair * LPP, LPP)
        one_hot = hot_of(pair_times)
        modulation = shift_table[None] + jnp.einsum(
            "ln,nkf->lkf", one_hot, time_table, precision=lax.Precision.HIGHEST
        )
        feature_biases = jnp.stack([b_out, b_cross_out, b_fc2])
        wide = jnp.concatenate(
            [modulation, jnp.broadcast_to(feature_biases, (LPP, 3, quarter))], axis=1
        )
        col_biases = jnp.concatenate([b_qv.reshape(-1), b_cross_q, b_cross_v, b_fc1])
        got = yield (
            "row",
            jnp.concatenate([pick(wide[1], wide[0], r).reshape(-1), col_biases]),
        )
        wide_rows = jnp.stack(
            [pick(wide[0], wide[1], r), got[: 9 * quarter].reshape(9, quarter)]
        )
        wide_other = swap(wide_rows, "col")
        wide_all = jnp.stack(
            [pick(wide_rows, wide_other, c), pick(wide_other, wide_rows, c)], axis=1
        )
        vectors = wide_all.transpose(0, 1, 3, 2).reshape(2 * half, 9)
        got_cols = got[9 * quarter :]
        four, four_got = (v[: 4 * quarter].reshape(4, quarter) for v in (col_biases, got_cols))
        fc1 = in_order(col_biases[4 * quarter :], got_cols[4 * quarter :], r, 0)[:, None]
        return vectors, in_order(four, four_got, r, 1).T, fc1

    def spread_task():
        yield ("wait", [fetch_three])
        return (yield ("compute", text_all, 0.0))

    def captions_in_task():
        ((_, cols, _),) = yield ("wait", [vectors_in])
        kv_part = jnp.einsum("ti,iko->kot", text_row, w_cross_kv, preferred_element_type=f32)
        far = yield ("row", kv_part.astype(bf16))
        kv_total = kv_part + far.astype(f32)
        kv_total = jnp.concatenate(
            [kv_total[0].astype(bf16), (kv_total[1] + cols[:, 3:]).astype(bf16)]
        )
        kv_far = yield (0, kv_total)
        kv_mine = pick(kv_total, kv_far, r ^ upper).reshape(2, heads, HD, TXT)
        kv_mine = jnp.pad(kv_mine, ((0, 0), (0, 0), (0, 0), (0, TXT_PAD - TXT)))
        return kv_mine[0], kv_mine[1]

    dp_bits = list(range(bits))
    order_x = ["row"] + dp_bits
    order_y = [0, "row"] + dp_bits[1:]
    order_z = [1, "row", 0] + dp_bits[2:]

    def by_block(grads, n):
        return grads.reshape((2,) + (2,) * bits + (-1, n))

    def reduce(grads, order):
        return links.spawn(reduce_pieces(grads, order, d))

    def to_features(own):
        blocks = own.reshape(2, 2, quarter, HALF)
        keep = lax.dynamic_index_in_dim(blocks, c, 1, keepdims=False)
        got = swap(lax.dynamic_index_in_dim(blocks, 1 - c, 1, keepdims=False), "col")
        tokens = in_order(keep, got, c, 2)
        other = yield ("row", tokens[1])
        return in_order(tokens[0], other, r, 1).T

    def main_task():
        ((lat_both, lat_other), (vectors, biases, bias_fc1)) = yield (
            "wait",
            [latents_in, vectors_in],
        )
        shift_one, scale_one, gate_one, shift_two, scale_two, gate_two = (
            vectors[:, i : i + 1] for i in range(6)
        )
        bias_out, bias_co, bias_fc2 = (vectors[:, i : i + 1] for i in range(6, 9))
        lat_all, mod_all, mean_all, inverse_all = assemble(
            "norm", lat_both, lat_other, core, vectors
        )
        mod_all = yield ("compute", mod_all, 6.0)
        mod_own = mod_all[:, :SEQ_DEV]
        ((weight_k, weight_v),) = yield ("wait", [fetch_kv])
        keys = rows_in(weight_k, mod_all).reshape(heads, HD, -1)
        values = rows_in(weight_v, mod_all, "bias", biases, 1).reshape(heads, HD, -1)
        values = yield ("compute", values, 8.0)
        ((weight_q,),) = yield ("wait", [fetch_q])
        queries = rows_in(weight_q, mod_own, "bias", biases, 0).reshape(heads, HD, -1)
        attended, log_self = attend(queries, keys, values, length, False)
        attended = yield ("compute", attended, 13.0)
        attended = attended.reshape(half, -1)
        ((weight_out, weight_cq, weight_co),) = yield ("wait", [fetch_three])
        branch = split_sum([(weight_out, attended)]) + bias_out
        residual = lat_all[:, :HALF].astype(f32)
        after_self = residual + gate_one * branch
        cross_in = join_cols(after_self.astype(bf16))
        cross_in = yield ("compute", cross_in, 12.0)

        ((text_k, text_v),) = yield ("wait", [captions_in])
        cross_q = rows_in(weight_cq, cross_in, "bias", biases, 2).reshape(heads, HD, -1)
        crossed, log_cross = attend(cross_q, text_k, text_v, length, True)
        crossed = yield ("compute", crossed, 8.0)
        crossed = crossed.reshape(half, -1)
        after_cross = after_self + split_sum([(weight_co, crossed)]) + bias_co

        normed_two, inverse_two = norm_forward(after_cross)
        mod_two = join_cols((normed_two * (1.0 + scale_two) + shift_two).astype(bf16))
        mod_two = yield ("compute", mod_two, 15.0)
        ((weight_fc1,),) = yield ("wait", [fetch_fc1])
        activated, slope = rows_in(weight_fc1, mod_two, "gelu", bias_fc1)
        activated = yield ("compute", activated, 10.0)

        ((grad_near, grad_other),) = yield ("wait", [grad_in])
        grad_all, grad_mlp = assemble("gate", grad_near, grad_other, core, vectors)
        grad_w_fc2 = by_block(weight_grad(activated, grad_mlp.reshape(2, half, -1)), half)
        grad_w_fc2 = yield ("compute", grad_w_fc2, 9.0)
        sum_fc2 = reduce(grad_w_fc2, order_x)
        ((weight_fc2,),) = yield ("wait", [fetch_fc2])
        grad_hidden, grad_b_fc1 = rows_in(weight_fc2, grad_mlp, "slope", slope)
        grad_hidden = yield ("compute", grad_hidden, 9.0)
        grad_w_fc1 = weight_grad(mod_two, grad_hidden[None])
        grad_w_fc1 = yield ("compute", by_block(grad_w_fc1, grad_hidden.shape[0]), 5.0)
        sum_fc1 = reduce(grad_w_fc1, order_y)
        grad_mod_two = split_sum([(weight_fc1, grad_hidden)])
        grad_own = grad_all[:, :HALF].astype(f32)
        grad_after_cross = grad_own + norm_backward(
            grad_mod_two * (1.0 + scale_two), normed_two, inverse_two
        )
        grad_cross = join_cols(grad_after_cross.astype(bf16))
        grad_cross = yield ("compute", grad_cross, 26.0)

        grad_crossed = rows_in(weight_co, grad_cross).reshape(heads, HD, -1)
        grad_cq, *grad_kv = attend_grad(
            cross_q, text_k, text_v, grad_crossed, log_cross, length, True
        )
        grad_cq = yield ("compute", grad_cq, 11.0)
        grad_cq = grad_cq.reshape(half, -1)
        grad_kv = jnp.stack(grad_kv)[..., :TXT].reshape(2, half, TXT)
        captions_out = links.spawn(captions_out_task(grad_kv))
        grad_w_co = by_block(weight_grad(crossed, grad_cross.reshape(2, half, -1)), half)
        grad_w_cq = by_block(weight_grad(cross_in, grad_cq[None]), half)
        grad_w_cq = yield ("compute", grad_w_cq, 7.0)
        grad_after_self = grad_after_cross + split_sum([(weight_cq, grad_cq)])
        grad_branch = join_cols((gate_one * grad_after_self).astype(bf16))
        grad_branch = yield ("compute", grad_branch, 18.0)
        grad_attended = rows_in(weight_out, grad_branch).reshape(heads, HD, -1)
        grad_w_out = by_block(weight_grad(attended, grad_branch.reshape(2, half, -1)), half)
        grad_w_three = jnp.stack([grad_w_out, grad_w_co, grad_w_cq], axis=bits + 1)
        grad_w_three = yield ("compute", grad_w_three, 10.0)
        grad_attended = yield ("compute", grad_attended, 3.0)
        sum_three = reduce(grad_w_three, order_x)

        grad_q, grad_k, grad_v = attend_grad(
            queries, keys, values, grad_attended, log_self, length, False
        )
        grad_k = yield ("compute", grad_k, 17.0)
        grad_q, grad_k, grad_v = (g.reshape(half, -1) for g in (grad_q, grad_k, grad_v))
        grad_w_kv = jnp.stack(
            [by_block(weight_grad(mod_all, g[None]), half) for g in (grad_k, grad_v)],
            axis=bits + 1,
        )
        grad_w_kv = yield ("compute", grad_w_kv, 7.0)
        sum_kv = reduce(grad_w_kv, order_y)
        grad_w_q = by_block(weight_grad(mod_own, grad_q[None]), half)
        grad_w_q = yield ("compute", grad_w_q, 3.0)
        sum_q = reduce(grad_w_q, order_z)
        keep, send = rows_out([(weight_k, grad_k), (weight_v, grad_v), (weight_q, grad_q)])
        total = keep + swap(send, "col").astype(f32)
        total = yield ("compute", total, 16.0)
        far_part = yield (0, total[:, HALF:].astype(bf16))
        grad_mod_one = total[:, :HALF] + far_part.astype(f32)
        normed_one = (residual - mean_all[:, :HALF]) * inverse_all[:, :HALF]
        grad_latents = grad_after_self + norm_backward(
            grad_mod_one * (1.0 + scale_one), normed_one, inverse_all[:, :HALF]
        )
        latents_out = links.spawn(to_features(grad_latents.astype(bf16)))
        mlp_out = split_sum([(weight_fc2, activated)]) + bias_fc2
        result = (after_cross + gate_two * mlp_out).astype(bf16)
        result = yield ("compute", result, 12.0)
        result_out = links.spawn(to_features(result))

        ((grad_text, summed_ckv, grad_b_cv),) = yield ("wait", [captions_out])
        grad_vectors = jnp.concatenate(
            [
                jnp.sum(value, axis=1, keepdims=True)
                for value in (
                    grad_mod_one,
                    grad_mod_one * normed_one,
                    grad_after_self * branch,
                    grad_mod_two,
                    grad_mod_two * normed_two,
                    grad_own * mlp_out,
                    gate_one * grad_after_self,
                    grad_after_cross,
                    gate_two * grad_own,
                )
            ],
            axis=1,
        ).reshape(2, 2, quarter, 9)
        keep = lax.dynamic_index_in_dim(grad_vectors, c, 1, keepdims=False)
        sent = lax.dynamic_index_in_dim(grad_vectors, 1 - c, 1, keepdims=False)
        keep = (keep + swap(sent, "col")).transpose(0, 2, 1)
        col_grads = jnp.concatenate(
            [
                jnp.sum(grad_q.astype(f32), axis=1, keepdims=True),
                jnp.sum(grad_v.astype(f32), axis=1, keepdims=True),
                jnp.sum(grad_cq.astype(f32), axis=1, keepdims=True),
                0.5 * grad_b_cv,
            ],
            axis=1,
        )
        col_grads = jnp.concatenate(
            [
                col_grads.T.reshape(4, 2, quarter).transpose(1, 0, 2).reshape(2, -1),
                grad_b_fc1.reshape(2, -1),
            ],
            axis=1,
        )
        mine_cols = lax.dynamic_index_in_dim(col_grads, r, 0, keepdims=False)
        sent_cols = lax.dynamic_index_in_dim(col_grads, 1 - r, 0, keepdims=False)
        sent = jnp.concatenate([keep[1].reshape(-1), sent_cols])
        got = yield ("row", sent)
        got_wide = got[: 9 * quarter].reshape(9, quarter)
        own_wide = keep[0]
        latent_wide = jnp.stack([pick(own_wide, got_wide, r), pick(got_wide, own_wide, r)])
        mine_cols = mine_cols + got[9 * quarter :]
        flat = jnp.concatenate(
            [
                latent_wide[:, :6].reshape(-1),
                (own_wide + got_wide)[6:].reshape(-1),
                mine_cols,
            ]
        )
        flat = flat + (yield (0, flat))
        n_latent = LPP * 6 * quarter
        gathered, sums = flat[None, :n_latent], flat[n_latent:]
        for bit in range(1, bits):
            got = yield (bit, jnp.concatenate([gathered.reshape(-1), sums]))
            got_latents = got[: gathered.size].reshape(gathered.shape)
            sums = sums + got[gathered.size :]
            gathered = in_order(gathered, got_latents, (d >> bit) & 1, 0)
        gathered = gathered.reshape(-1, 6, quarter)
        grad_time_table = jnp.einsum(
            "ln,lkf->nkf", hot_of(time_ids), gathered, precision=lax.Precision.HIGHEST
        )
        wide_sums = sums[: 3 * quarter].reshape(3, quarter)
        col_sums = sums[3 * quarter :]

        waited = [sum_fc2, sum_fc1, sum_three, sum_kv, sum_q, latents_out, result_out]
        fc2, fc1, three, kv, sum_q, grad_latents, output = yield ("wait", waited)
        return (
            output,
            grad_latents.astype(f32),
            grad_text,
            grad_time_table,
            jnp.sum(gathered, axis=0),
            jnp.stack([sum_q, kv[0], kv[1]], axis=1),
            col_sums[: 2 * quarter].reshape(2, quarter),
            three[0],
            wide_sums[0],
            three[2],
            col_sums[2 * quarter : 3 * quarter],
            summed_ckv,
            col_sums[3 * quarter : 4 * quarter],
            three[1],
            wide_sums[1],
            fc1,
            col_sums[4 * quarter :],
            fc2,
            wide_sums[2],
        )

    def captions_out_task(grad_kv):
        far = yield (0, grad_kv)
        kv_sum = grad_kv.astype(f32) + far.astype(f32)
        grad_b_cv = jnp.sum(kv_sum[1], axis=1, keepdims=True)
        kv_latent = kv_sum.astype(bf16)
        kv_other = yield ("row", kv_latent)
        kv_own = pick(kv_latent, kv_other, r ^ upper)
        text_part = jnp.einsum("kot,iko->ti", kv_own, w_cross_kv, preferred_element_type=f32)
        text_quarter = text.shape[2]
        keep = pick(text_part[:, :text_quarter], text_part[:, text_quarter:], c)
        send = pick(text_part[:, text_quarter:], text_part[:, :text_quarter], c)
        grad_text = (keep + swap(send.astype(bf16), "col").astype(f32))[None]
        kv_all = lax.all_gather(kv_own, "dp")
        (text_rows,) = yield ("wait", [spread])
        summed_ckv = jnp.einsum(
            "lti,lkot->iko", text_rows, kv_all, preferred_element_type=f32
        )
        return grad_text, summed_ckv, grad_b_cv

    def hot_of(ids):
        return (ids[:, None] == jnp.arange(time_table.shape[0])[None, :]).astype(f32)

    text_row = in_order(text[0], swap(text[0], "col"), c, 1)
    text_block = 2 * text.shape[2] // n_dp
    text_mine = lax.dynamic_slice_in_dim(
        lax.all_gather(text[0], "dp"), d % (n_dp // 2) * text_block, text_block, 2
    )
    text_all = pick(text_mine, swap(text_mine, "col"), c ^ (d // (n_dp // 2)))
    length = lax.dynamic_slice_in_dim(text_len, my_latent, 1)

    latents_in = links.spawn(latents_in_task())
    q_k_v = w_qkv.transpose(1, 0, 2)
    fetch_kv = links.spawn(fetch(q_k_v, 1, 0, None, (q_k_v, 1), (q_k_v, 2)))
    vectors_in = links.spawn(vectors_in_task())
    fetch_q = links.spawn(fetch(q_k_v, 0, 1, None, (q_k_v, 0)))
    w_three = jnp.stack([w_out.T, w_cross_q, w_cross_out.T])
    fetch_three = links.spawn(fetch(w_three, 0, 1, fetch_kv, *((w_three, i) for i in range(3))))
    captions_in = links.spawn(captions_in_task())
    w_fc2_t = w_fc2.T
    fetch_fc1 = links.spawn(fetch(w_fc1[None], 0, 0, fetch_three, (w_fc1, None)))
    fetch_fc2 = links.spawn(fetch(w_fc2_t[None], 0, 1, fetch_fc1, (w_fc2_t, None)))
    spread = links.spawn(spread_task())
    grad_in = links.spawn(grad_out_task())
    main = links.spawn(main_task())
    links.run()
    return main.result


def solution(mesh):
    return jax.shard_map(
        local,
        mesh=mesh,
        in_specs=(
            P("dp", ("row", "col")),
            P("dp", None, ("row", "col")),
            P(),
            P(),
            P(None, None, ("row", "col")),
            P(None, ("row", "col")),
            P("row", None, "col"),
            P(None, ("col", "row")),
            P("col", "row"),
            P(("row", "col")),
            P("row", "col"),
            P(("col", "row")),
            P("row", None, "col"),
            P(("col", "row")),
            P("col", "row"),
            P(("row", "col")),
            P("row", "col"),
            P(("col", "row")),
            P("col", "row"),
            P(("row", "col")),
            P("dp", ("row", "col")),
        ),
        out_specs=(
            P("dp", ("row", "col")),
            P("dp", ("row", "col")),
            P("dp", None, ("row", "col")),
            P(None, None, ("row", "col")),
            P(None, ("row", "col")),
            P(("row", "dp"), None, "col"),
            P(None, ("col", "row")),
            P(("col", "dp"), "row"),
            P(("row", "col")),
            P(("row", "dp"), "col"),
            P(("col", "row")),
            P(("row", "dp"), None, "col"),
            P(("col", "row")),
            P(("col", "dp"), "row"),
            P(("row", "col")),
            P(("row", "dp"), "col"),
            P(("col", "row")),
            P(("col", "dp"), "row"),
            P(("row", "col")),
        ),
        check_vma=False,
    )
```

time: 740 us -> 564 us (0.76)
  waiting for transfers between devices: 397 us -> 192 us
  Pallas kernels: 35.5 us -> 130 us
  matrix products: 77.5 us -> 13 us
  between operations: 3.96 us -> 16.5 us
  other arithmetic: 85.4 us -> 74.5 us
  starting transfers between devices: 67.3 us -> 57.6 us
  local copies, waits for them, and re-layouts: 66.7 us -> 75 us
    ppermute x42 -> x37, waiting for transfers between devices: 231 us -> 58.2 us  [swap(): return lax.ppermute(value, axis, [(0, 1), (1, 0)])]
    pallas_call x0 -> x24, Pallas kernels: none -> 94.9 us  [the longest x8 36.5 us: rows_in(): pl.pallas_call(partial(rows_in_kernel, len(weight.arrays), kind, lane), g...]
    dot_general x32 -> x5, matrix products: 77.5 us -> 13 us  [the longest x1 4.66 us: captions_in_task(): jnp.einsum('ti,iko->kot', text_row, w_cross_kv, preferred_element_type=f32)]
    ppermute x37 -> x27, waiting for transfers between devices: 166 us -> 133 us  [swap_dp(): lax.ppermute(value, 'dp', [(i, i ^ 1 << bit) for i in range(lax.axis_size...]
    convert_element_type x7 -> x1, local copies, waits for them, and re-layouts: 19.1 us -> 0.02 us  [captions_in_task(): kv_total[0].astype(bf16)]
    squeeze x11 -> x24, local copies, waits for them, and re-layouts: 3.96 us -> 18.3 us  [the longest x15 9.04 us: reduce_pieces(): send = lax.dynamic_index_in_dim(held, 1 - bit, axis, keepdims=False)]
    select_n x45 -> x13, other arithmetic: 20 us -> 7.16 us  [pick(): return jnp.where(index == 0, pair_first, pair_second)]
    unnamed x323 -> x287, local copies, waits for them, and re-layouts: 18.9 us -> 31.2 us
  transfers between devices with their start and end apart: 79 -> 66, of which waited for: 39 -> 23; matrix products, arithmetic and copies ran while one was open for 29% -> 23% of each run, Pallas kernels for 5% -> 22%
where the time goes in v2:
time: 564 us; the launch traced here: 558 us
  waiting for transfers between devices  192 us (34%)
  Pallas kernels  130 us (23%)
  local copies, waits for them, and re-layouts  75 us (13%)
  other arithmetic  74.5 us (13%)
  starting transfers between devices  57.6 us (10%)
  between operations  16.5 us (3%)
  matrix products  13 us (2%)
    ppermute x27, waiting for transfers between devices, swap_dp(): lax.ppermute(value, 'dp', [(i, i ^ 1 << bit) for i in range(lax.axis_size...  133 us
    ppermute x37, waiting for transfers between devices, swap(): return lax.ppermute(value, axis, [(0, 1), (1, 0)])  58.2 us
    pallas_call x8, Pallas kernels, rows_in(): pl.pallas_call(partial(rows_in_kernel, len(weight.arrays), kind, lane), g...  36.5 us
    ppermute x27, starting transfers between devices, swap_dp(): lax.ppermute(value, 'dp', [(i, i ^ 1 << bit) for i in range(lax.axis_size...  35.4 us
    unnamed x287, local copies, waits for them, and re-layouts  31.2 us
    pallas_call x6, Pallas kernels, rows_out(): pl.pallas_call(partial(rows_out_kernel, [len(w.arrays) for w, _ in pairs]...  30.6 us
    ppermute x37, starting transfers between devices, swap(): return lax.ppermute(value, axis, [(0, 1), (1, 0)])  22.1 us
    pallas_call x8, Pallas kernels, weight_grad(): pl.pallas_call(weight_grad_kernel, grid=(groups, k // rows), in_specs=[pl...  21.6 us
  transfers between devices with their start and end apart: 66, of which 23 were waited for; matrix products, arithmetic and copies ran while one was open for 23% of the time, Pallas kernels for 22%

profile of v2, /device:TPU:0, one launch (start us, length us, event | category | flops | bytes accessed | tf_op | source)
XLA Modules:
  0.0 558.0 jit_solution(7708258362401621702)
XLA Ops:
  31.4 6.2 %collective-permute-done.1 = bf16[2,288,512]{2,1,0:T(8,128)(2,1)} collective-permute-done((bf16[2,288,512]{2,1,0:T(8,128)(2,1)}, bf16[2,288,512]{2,1,0:T(8,128)(2,1)}, u32[]{:S(2)}, u32[]{:S(2)}) %collective-permute-start.1) | collective-permute-done | bytes 589856 | tf_op jit(solution)/shard_map/ppermute | solution.py:29
  47.7 4.7 fusion.68
  56.1 5.4 assemble_norm.1
  67.3 4.0 collective-permute-done.9.refs_2_.refs_8_.refs_11_
  71.3 4.1 rows_in_bias.4
  75.4 4.6 rows_in_plain.3
  83.2 9.6 %attend_fwd.2 = (bf16[8,72,512]{2,1,0:T(8,128)(2,1)S(1)}, f32[8,1,512]{2,1,0:T(1,128)S(1)}) custom-call(s32[1]{0:T(128)} %dynamic_slice.172.length_ref, bf16[8,72,512]{2,1,0:T(8,128)(2,1)S(1)} %bitcast.338, bf16[8,72,1024]{2,1,0:T(8,128)(2,1)S(1)} %bitcast.314, bf16[8,72,1024]{2,1,0:T(8,128)(2,1)S(1)} %bitcast.318), custom_call_target="tpu_custom_call" | custom-call | flops 1 | bytes 1 | tf_op jit(solution)/shard_map/attend_fwd/pallas_call | solution.py:72
  98.1 6.5 %collective-permute-done.14 = bf16[1152,120]{1,0:T(8,128)(2,1)S(1)} collective-permute-done((bf16[1152,120]{1,0:T(8,128)(2,1)S(1)}, bf16[1152,120]{1,0:T(8,128)(2,1)S(1)}, u32[]{:S(2)}, u32[]{:S(2)}) %collective-permute-start.14) | collective-permute-done | bytes 276512 | tf_op jit(solution)/shard_map/ppermute | solution.py:29
  104.6 14.9 %collective-permute-done.11.refs_4_.refs_2_ = bf16[3,288,576]{2,1,0:T(8,128)(2,1)S(1)} collective-permute-done((bf16[3,288,576]{2,1,0:T(8,128)(2,1)}, bf16[3,288,576]{2,1,0:T(8,128)(2,1)S(1)}, u32[]{:S(2)}, u32[]{:S(2)}) %collective-permute-start.11) | collective-permute-done | bytes 995360 | tf_op jit(solution)/shard_map/ppermute | solution.py:29
  121.0 3.5 rows_out.6
  137.1 23.3 %collective-permute-done.18.refs_1_.refs_3_ = bf16[1,288,2304]{2,1,0:T(8,128)(2,1)} collective-permute-done((bf16[1,288,2304]{2,1,0:T(8,128)(2,1)}, bf16[1,288,2304]{2,1,0:T(8,128)(2,1)}, u32[]{:S(2)}, u32[]{:S(2)}) %collective-permute-start.18) | collective-permute-done | bytes 1327136 | tf_op jit(solution)/shard_map/ppermute | solution.py:25
  160.3 4.0 attend_fwd.3
  175.9 24.0 %collective-permute-done.21.refs_2_.refs_4_ = bf16[1,288,2304]{2,1,0:T(8,128)(2,1)S(1)} collective-permute-done((bf16[1,288,2304]{2,1,0:T(8,128)(2,1)}, bf16[1,288,2304]{2,1,0:T(8,128)(2,1)S(1)}, u32[]{:S(2)}, u32[]{:S(2)}) %collective-permute-start.21) | collective-permute-done | bytes 1327136 | tf_op jit(solution)/shard_map/ppermute | solution.py:29
  206.6 9.9 %rows_in_gelu.1 = (bf16[2304,512]{1,0:T(8,128)(2,1)}, bf16[2304,512]{1,0:T(8,128)(2,1)}) custom-call(s32[3]{0:T(128)S(1)} %fusion.58.places_ref.refs_0_.refs_1_, bf16[1152,512]{1,0:T(8,128)(2,1)S(1)} %pad_maximum_fusion.5.x_ref.inputs_ref, bf16[576,2304]{1,0:T(8,128)(2,1)} %refs_2_.1, bf16[1,288,2304]{2,1,0:T(8,128)(2,1)} %collective-permute-done.18.refs_1_.refs_3_, ...), custom_call_target="tpu_custom_call" | custom-call | flops 1 | bytes 1 | tf_op jit(solution)/shard_map/rows_in_gelu/pallas_call | solution.py:247
  218.2 6.1 %weight_grad.8 = bf16[2,2304,576]{2,1,0:T(8,128)(2,1)S(1)} custom-call(bf16[2304,512]{1,0:T(8,128)(2,1)S(1)} %copy-done.27, bf16[2,576,512]{2,1,0:T(8,128)(2,1)S(1)} %bitcast.340), custom_call_target="tpu_custom_call" | custom-call | flops 1 | bytes 1 | tf_op jit(solution)/shard_map/weight_grad/pallas_call | solution.py:331
  231.4 7.4 %rows_in_slope.1 = (bf16[2304,512]{1,0:T(8,128)(2,1)}, f32[2304,1]{1,0:T(8,128)S(1)}) custom-call(s32[3]{0:T(128)S(1)} %fusion.57.places_ref.refs_0_.refs_2_, bf16[1152,512]{1,0:T(8,128)(2,1)S(1)} %get-tuple-element.154.x_ref, bf16[576,2304]{1,0:T(8,128)(2,1)} %bitcast.354, bf16[1,288,2304]{2,1,0:T(8,128)(2,1)S(1)} %collective-permute-done.22.refs_3_.refs_1_, ...), custom_call_target="tpu_custom_call" | custom-call | flops 1 | bytes 1 | tf_op jit(solution)/shard_map/rows_in_slope/pallas_call | solution.py:247
  239.9 5.7 %rows_out.9 = (f32[1152,256]{1,0:T(8,128)S(1)}, bf16[1152,256]{1,0:T(8,128)(2,1)S(1)}) custom-call(s32[3]{0:T(128)S(1)} %fusion.58.places_ref.refs_0_.refs_1_, bf16[2304,512]{1,0:T(8,128)(2,1)} %get-tuple-element.162.refs_1_, bf16[576,2304]{1,0:T(8,128)(2,1)} %refs_2_.1, bf16[1,288,2304]{2,1,0:T(8,128)(2,1)} %collective-permute-done.18.refs_1_.refs_3_, ...), custom_call_target="tpu_custom_call" | custom-call | flops 1 | bytes 1 | tf_op jit(solution)/shard_map/rows_out/pallas_call | solution.py:310
  245.7 5.3 rows_out.8
  259.7 3.7 weight_grad.9
  271.4 4.8 attend_bwd.2
  276.9 17.0 %collective-permute-done.26 = bf16[2,2,2,288,576]{4,3,0,1,2:T(8,128)(2,1)} collective-permute-done((bf16[2,2,2,288,576]{4,3,0,1,2:T(8,128)(2,1)}, bf16[2,2,2,288,576]{4,3,0,1,2:T(8,128)(2,1)}, u32[]{:S(2)}, u32[]{:S(2)}) %collective-permute-start.26) | collective-permute-done | bytes 2654240 | tf_op jit(solution)/shard_map/ppermute | solution.py:25
  293.9 3.5 rows_out.10
  340.8 16.3 %attend_bwd.3 = (bf16[8,72,512]{2,1,0:T(8,128)(2,1)S(1)}, bf16[8,72,1024]{2,1,0:T(8,128)(2,1)S(1)}, bf16[8,72,1024]{2,1,0:T(8,128)(2,1)S(1)}) custom-call(s32[1]{0:T(128)} %dynamic_slice.172.length_ref, bf16[8,72,512]{2,1,0:T(8,128)(2,1)S(1)} %bitcast.339, bf16[8,72,1024]{2,1,0:T(8,128)(2,1)S(1)} %bitcast.315, bf16[8,72,1024]{2,1,0:T(8,128)(2,1)S(1)} %bitcast.319, ...), custom_call_target="tpu_custom_call" | custom-call | flops 1 | bytes 1 | tf_op jit(solution)/shard_map/attend_bwd/pallas_call | solution.py:110
  358.7 5.8 %collective-permute-done.29 = bf16[2,2,288,576]{3,2,0,1:T(8,128)(2,1)} collective-permute-done((bf16[2,2,288,576]{3,2,0,1:T(8,128)(2,1)}, bf16[2,2,288,576]{3,2,0,1:T(8,128)(2,1)}, u32[]{:S(2)}, u32[]{:S(2)}) %collective-permute-start.29) | collective-permute-done | bytes 1327136 | tf_op jit(solution)/shard_map/ppermute | solution.py:29
  374.8 3.5 slice_bitcast_fusion.2
  386.2 9.8 %rows_out.11 = (f32[1152,512]{1,0:T(8,128)}, bf16[1152,512]{1,0:T(8,128)(2,1)S(1)}) custom-call(s32[3]{0:T(128)S(1)} %fusion.58.places_ref.refs_0_.refs_1_, s32[3]{0:T(128)S(1)} %fusion.58.places_ref.refs_0_.refs_1_, s32[3]{0:T(128)S(1)} %fusion.57.places_ref.refs_0_.refs_2_, bf16[576,1024]{1,0:T(8,128)(2,1)S(1)} %bitcast.341, bf16[576,1024]{1,0:T(8,128)(2,1)} %bitcast.317, ...), custom_call_target="tpu_custom_call" | custom-call | flops 1 | bytes 1 | tf_op jit(solution)/shard_map/rows_out/pallas_call | solution.py:310
  410.6 29.2 %collective-permute-done.42 = bf16[2,2,2,2,72,576]{5,4,3,1,2,0:T(8,128)(2,1)S(1)} collective-permute-done((bf16[2,2,2,2,72,576]{5,4,3,1,2,0:T(8,128)(2,1)S(1)}, bf16[2,2,2,2,72,576]{5,4,3,1,2,0:T(8,128)(2,1)S(1)}, u32[]{:S(2)}, u32[]{:S(2)}) %collective-permute-start.42) | collective-permute-done | bytes 1327136 | tf_op jit(solution)/shard_map/ppermute | solution.py:29
  465.6 5.1 collective-permute-done.46
  474.8 15.9 %collective-permute-done.51 = bf16[2,2,3,72,576]{4,3,2,0,1:T(8,128)(2,1)} collective-permute-done((bf16[2,2,3,72,576]{4,3,2,0,1:T(8,128)(2,1)}, bf16[2,2,3,72,576]{4,3,2,0,1:T(8,128)(2,1)}, u32[]{:S(2)}, u32[]{:S(2)}) %collective-permute-start.51) | collective-permute-done | bytes 995360 | tf_op jit(solution)/shard_map/ppermute | solution.py:29
  516.5 7.9 %collective-permute-done.61 = bf16[2,3,72,576]{3,2,1,0:T(8,128)(2,1)S(1)} collective-permute-done((bf16[2,3,72,576]{3,2,1,0:T(8,128)(2,1)}, bf16[2,3,72,576]{3,2,1,0:T(8,128)(2,1)S(1)}, u32[]{:S(2)}, u32[]{:S(2)}) %collective-permute-start.61) | collective-permute-done | bytes 497696 | tf_op jit(solution)/shard_map/ppermute | solution.py:29
  530.3 12.1 %collective-permute-done.63 = bf16[3,72,576]{2,1,0:T(8,128)(2,1)S(1)} collective-permute-done((bf16[3,72,576]{2,1,0:T(8,128)(2,1)S(1)}, bf16[3,72,576]{2,1,0:T(8,128)(2,1)S(1)}, u32[]{:S(2)}, u32[]{:S(2)}) %collective-permute-start.63) | collective-permute-done | bytes 248864 | tf_op jit(solution)/shard_map/ppermute | solution.py:29
  547.2 3.7 convolution_bitcast_fusion.1
  (622 shorter events, 254.1 us)
Async XLA Ops:
  7.3 121.6 %all-gather.4.cloned.1.call-start = ((), (), s32[]{:S(2)}) async-start(), calls=%async_computation | async-start | bytes 2211840 | tf_op jit(solution)/shard_map/all_gather | solution.py:829
  8.0 539.2 %all-gather.6.cloned.1.call-start = ((), (), s32[]{:S(2)}) async-start(), calls=%async_computation.1 | async-start | bytes 2654208 | tf_op jit(solution)/shard_map/all_gather | solution.py:816
  12.9 31.9 %collective-permute-start.3 = (f32[4896]{0:T(1024)S(1)}, f32[4896]{0:T(1024)S(1)}, u32[]{:S(2)}, u32[]{:S(2)}) collective-permute-start(f32[4896]{0:T(1024)S(1)} %concatenate.96), channel_id=1, source_target_pairs={{0,2},{2,0},{1,3},{3,1},{4,6},{6,4},{5,7},{7,5},{8,10},{10,8},{9,1... | collective-permute-start | bytes 58760 | tf_op jit(solution)/shard_map/ppermute | solution.py:25
  13.0 27.2 %collective-permute-start.12 = (bf16[120,1024]{1,0:T(8,128)(2,1)}, bf16[120,1024]{1,0:T(8,128)(2,1)}, u32[]{:S(2)}, u32[]{:S(2)}) collective-permute-start(bf16[120,1024]{1,0:T(8,128)(2,1)} %bitcast.28), channel_id=1, source_target_pairs={{0,1},{1,0},{2,3},{3,2},{4,5},{5,4},{6,7},{7,6},{8,9},{9,8},{10,11... | collective-permute-start | bytes 737288 | tf_op jit(solution)/shard_map/ppermute | solution.py:25
  14.8 49.6 %collective-permute-start.6 = (bf16[1,288,576]{2,1,0:T(8,128)(2,1)}, bf16[1,288,576]{2,1,0:T(8,128)(2,1)}, u32[]{:S(2)}, u32[]{:S(2)}) collective-permute-start(bf16[1,288,576]{2,1,0:T(8,128)(2,1)} %dynamic-slice_bitcast_fusion.9), channel_id=1, source_target_pairs={{0,2},{2,0},{1,3},{3,1},{4,6},{6,4},{5,7},{7,5},{8,10},{10,8},{9,1... | collective-permute-start | bytes 995336 | tf_op jit(solution)/shard_map/ppermute | solution.py:25
  37.6 42.6 %collective-permute-start.8 = (bf16[288,512]{1,0:T(8,128)(2,1)}, bf16[288,512]{1,0:T(8,128)(2,1)}, u32[]{:S(2)}, u32[]{:S(2)}) collective-permute-start(bf16[288,512]{1,0:T(8,128)(2,1)} %get-tuple-element.260), channel_id=1, source_target_pairs={{0,2},{2,0},{1,3},{3,1},{4,6},{6,4},{5,7},{7,5},{8,10},{10,8},{9,1... | collective-permute-start | bytes 884744 | tf_op jit(solution)/shard_map/ppermute | solution.py:25
  46.1 47.5 %collective-permute-start.10 = (bf16[3,288,576]{2,1,0:T(8,128)(2,1)}, bf16[3,288,576]{2,1,0:T(8,128)(2,1)}, u32[]{:S(2)}, u32[]{:S(2)}) collective-permute-start(bf16[3,288,576]{2,1,0:T(8,128)(2,1)} %constant_dynamic-slice_fusion.9), channel_id=1, source_target_pairs={{0,2},{2,0},{1,3},{3,1},{4,6},{6,4},{5,7},{7,5},{8,10},{10,8},{9,1... | collective-permute-start | bytes 2985992 | tf_op jit(solution)/shard_map/ppermute | solution.py:25
  54.2 41.0 %collective-permute-start.13 = (bf16[2,576,120]{2,1,0:T(8,128)(2,1)}, bf16[2,576,120]{2,1,0:T(8,128)(2,1)}, u32[]{:S(2)}, u32[]{:S(2)}) collective-permute-start(bf16[2,576,120]{2,1,0:T(8,128)(2,1)} %get-tuple-element.298), channel_id=1, source_target_pairs={{0,2},{2,0},{1,3},{3,1},{4,6},{6,4},{5,7},{7,5},{8,10},{10,8},{9,1... | collective-permute-start | bytes 829448 | tf_op jit(solution)/shard_map/ppermute | solution.py:25
  93.6 25.9 %collective-permute-start.11 = (bf16[3,288,576]{2,1,0:T(8,128)(2,1)}, bf16[3,288,576]{2,1,0:T(8,128)(2,1)S(1)}, u32[]{:S(2)}, u32[]{:S(2)}) collective-permute-start(bf16[3,288,576]{2,1,0:T(8,128)(2,1)} %collective-permute-done.10.refs_3_.refs_1_), channel_id=1, source_target_pairs={{0,8},{4,12},{8,0},{12,4},{16,24},{20,28},{24,16},{28,20},{1,9},{5... | collective-permute-start | bytes 2985992 | tf_op jit(solution)/shard_map/ppermute | solution.py:29
  128.5 31.8 %collective-permute-start.18 = (bf16[1,288,2304]{2,1,0:T(8,128)(2,1)}, bf16[1,288,2304]{2,1,0:T(8,128)(2,1)}, u32[]{:S(2)}, u32[]{:S(2)}) collective-permute-start(bf16[1,288,2304]{2,1,0:T(8,128)(2,1)} %constant_dynamic-slice_fusion.7), channel_id=1, source_target_pairs={{0,2},{2,0},{1,3},{3,1},{4,6},{6,4},{5,7},{7,5},{8,10},{10,8},{9,1... | collective-permute-start | bytes 3981320 | tf_op jit(solution)/shard_map/ppermute | solution.py:25
  168.1 31.8 %collective-permute-start.21 = (bf16[1,288,2304]{2,1,0:T(8,128)(2,1)}, bf16[1,288,2304]{2,1,0:T(8,128)(2,1)S(1)}, u32[]{:S(2)}, u32[]{:S(2)}) collective-permute-start(bf16[1,288,2304]{2,1,0:T(8,128)(2,1)} %collective-permute-done.18.refs_1_.refs_3_), channel_id=1, source_target_pairs={{0,4},{4,0},{8,12},{12,8},{16,20},{20,16},{24,28},{28,24},{1,5},{5... | collective-permute-start | bytes 3981320 | tf_op jit(solution)/shard_map/ppermute | solution.py:29
  169.8 31.3 %collective-permute-start.22 = (bf16[1,288,2304]{2,1,0:T(8,128)(2,1)S(1)}, bf16[1,288,2304]{2,1,0:T(8,128)(2,1)S(1)}, u32[]{:S(2)}, u32[]{:S(2)}) collective-permute-start(bf16[1,288,2304]{2,1,0:T(8,128)(2,1)S(1)} %constant_dynamic-slice_fusion.6), channel_id=1, source_target_pairs={{0,2},{2,0},{1,3},{3,1},{4,6},{6,4},{5,7},{7,5},{8,10},{10,8},{9,1... | collective-permute-start | bytes 3981320 | tf_op jit(solution)/shard_map/ppermute | solution.py:25
  201.0 30.4 %collective-permute-start.23 = (bf16[1,288,2304]{2,1,0:T(8,128)(2,1)S(1)}, bf16[1,288,2304]{2,1,0:T(8,128)(2,1)S(1)}, u32[]{:S(2)}, u32[]{:S(2)}) collective-permute-start(bf16[1,288,2304]{2,1,0:T(8,128)(2,1)S(1)} %collective-permute-done.22.refs_3_.refs_1_), channel_id=1, source_target_pairs={{0,8},{4,12},{8,0},{12,4},{16,24},{20,28},{24,16},{28,20},{1,9},{5... | collective-permute-start | bytes 3981320 | tf_op jit(solution)/shard_map/ppermute | solution.py:29
  227.6 66.2 %collective-permute-start.26 = (bf16[2,2,2,288,576]{4,3,0,1,2:T(8,128)(2,1)}, bf16[2,2,2,288,576]{4,3,0,1,2:T(8,128)(2,1)}, u32[]{:S(2)}, u32[]{:S(2)}) collective-permute-start(bf16[2,2,2,288,576]{4,3,0,1,2:T(8,128)(2,1)} %slice_bitcast_fusion), channel_id=1, source_target_pairs={{0,2},{2,0},{1,3},{3,1},{4,6},{6,4},{5,7},{7,5},{8,10},{10,8},{9,1... | collective-permute-start | bytes 7962632 | tf_op jit(solution)/shard_map/ppermute | solution.py:25
  266.7 61.9 %collective-permute-start.32 = (bf16[2,2,2,72,2304]{4,3,1,2,0:T(8,128)(2,1)}, bf16[2,2,2,72,2304]{4,3,1,2,0:T(8,128)(2,1)}, u32[]{:S(2)}, u32[]{:S(2)}) collective-permute-start(bf16[2,2,2,72,2304]{4,3,1,2,0:T(8,128)(2,1)} %copy_bitcast_fusion), channel_id=1, source_target_pairs={{0,4},{4,0},{8,12},{12,8},{16,20},{20,16},{24,28},{28,24},{1,5},{5... | collective-permute-start | bytes 7962632 | tf_op jit(solution)/shard_map/ppermute | solution.py:29
  306.0 75.5 %collective-permute-start.35 = (bf16[2,576,120]{2,1,0:T(8,128)(2,1)}, bf16[2,576,120]{2,1,0:T(8,128)(2,1)}, u32[]{:S(2)}, u32[]{:S(2)}) collective-permute-start(bf16[2,576,120]{2,1,0:T(8,128)(2,1)} %bitcast.75), channel_id=1, source_target_pairs={{0,4},{4,0},{8,12},{12,8},{16,20},{20,16},{24,28},{28,24},{1,5},{5... | collective-permute-start | bytes 829448 | tf_op jit(solution)/shard_map/ppermute | solution.py:29
  326.3 38.3 %collective-permute-start.29 = (bf16[2,2,288,576]{3,2,0,1:T(8,128)(2,1)}, bf16[2,2,288,576]{3,2,0,1:T(8,128)(2,1)}, u32[]{:S(2)}, u32[]{:S(2)}) collective-permute-start(bf16[2,2,288,576]{3,2,0,1:T(8,128)(2,1)} %dynamic-slice_bitcast_fusion.1), channel_id=1, source_target_pairs={{0,4},{4,0},{8,12},{12,8},{16,20},{20,16},{24,28},{28,24},{1,5},{5... | collective-permute-start | bytes 3981320 | tf_op jit(solution)/shard_map/ppermute | solution.py:29
  334.8 43.9 %collective-permute-start.34 = (bf16[2,2,72,2304]{3,2,0,1:T(8,128)(2,1)}, bf16[2,2,72,2304]{3,2,0,1:T(8,128)(2,1)}, u32[]{:S(2)}, u32[]{:S(2)}) collective-permute-start(bf16[2,2,72,2304]{3,2,0,1:T(8,128)(2,1)} %slice_bitcast_fusion.4), channel_id=1, source_target_pairs={{0,2},{2,0},{1,3},{3,1},{4,6},{6,4},{5,7},{7,5},{8,10},{10,8},{9,1... | collective-permute-start | bytes 3981320 | tf_op jit(solution)/shard_map/ppermute | solution.py:25
  367.4 31.8 %collective-permute-start.33 = (bf16[2,288,576]{2,1,0:T(8,128)(2,1)}, bf16[2,288,576]{2,1,0:T(8,128)(2,1)}, u32[]{:S(2)}, u32[]{:S(2)}) collective-permute-start(bf16[2,288,576]{2,1,0:T(8,128)(2,1)} %dynamic-slice_bitcast_fusion.3), channel_id=1, source_target_pairs={{0,8},{4,12},{8,0},{12,4},{16,24},{20,28},{24,16},{28,20},{1,9},{5... | collective-permute-start | bytes 1990664 | tf_op jit(solution)/shard_map/ppermute | solution.py:29
  378.2 61.9 %collective-permute-start.41 = (bf16[2,2,2,3,72,576]{5,4,3,0,1,2:T(8,128)(2,1)}, bf16[2,2,2,3,72,576]{5,4,3,0,1,2:T(8,128)(2,1)}, u32[]{:S(2)}, u32[]{:S(2)}) collective-permute-start(bf16[2,2,2,3,72,576]{5,4,3,0,1,2:T(8,128)(2,1)} %slice_bitcast_fusion.2), channel_id=1, source_target_pairs={{0,2},{2,0},{1,3},{3,1},{4,6},{6,4},{5,7},{7,5},{8,10},{10,8},{9,1... | collective-permute-start | bytes 5971976 | tf_op jit(solution)/shard_map/ppermute | solution.py:25
  383.0 62.8 %collective-permute-start.39 = (bf16[2,576,120]{2,1,0:T(8,128)(2,1)S(1)}, bf16[2,576,120]{2,1,0:T(8,128)(2,1)S(1)}, u32[]{:S(2)}, u32[]{:S(2)}) collective-permute-start(bf16[2,576,120]{2,1,0:T(8,128)(2,1)S(1)} %get-tuple-element.271), channel_id=1, source_target_pairs={{0,2},{2,0},{1,3},{3,1},{4,6},{6,4},{5,7},{7,5},{8,10},{10,8},{9,1... | collective-permute-start | bytes 829448 | tf_op jit(solution)/shard_map/ppermute | solution.py:25
  385.7 22.4 %collective-permute-start.43 = (bf16[2,72,2304]{2,1,0:T(8,128)(2,1)S(1)}, bf16[2,72,2304]{2,1,0:T(8,128)(2,1)S(1)}, u32[]{:S(2)}, u32[]{:S(2)}) collective-permute-start(bf16[2,72,2304]{2,1,0:T(8,128)(2,1)S(1)} %dynamic-slice_bitcast_fusion.5), channel_id=1, source_target_pairs={{0,8},{4,12},{8,0},{12,4},{16,24},{20,28},{24,16},{28,20},{1,9},{5... | collective-permute-start | bytes 1990664 | tf_op jit(solution)/shard_map/ppermute | solution.py:29
  402.4 54.9 %collective-permute-start.36 = (bf16[288,576]{1,0:T(8,128)(2,1)}, bf16[288,576]{1,0:T(8,128)(2,1)}, u32[]{:S(2)}, u32[]{:S(2)}) collective-permute-start(bf16[288,576]{1,0:T(8,128)(2,1)} %dynamic-slice_bitcast_fusion.8), channel_id=1, source_target_pairs={{0,16},{4,20},{8,24},{12,28},{16,0},{20,4},{24,8},{28,12},{1,17},{... | collective-permute-start | bytes 995336 | tf_op jit(solution)/shard_map/ppermute | solution.py:29
  405.4 34.5 %collective-permute-start.42 = (bf16[2,2,2,2,72,576]{5,4,3,1,2,0:T(8,128)(2,1)S(1)}, bf16[2,2,2,2,72,576]{5,4,3,1,2,0:T(8,128)(2,1)S(1)}, u32[]{:S(2)}, u32[]{:S(2)}) collective-permute-start(bf16[2,2,2,2,72,576]{5,4,3,1,2,0:T(8,128)(2,1)S(1)} %dynamic-slice_bitcast_fusion), channel_id=1, source_target_pairs={{0,4},{4,0},{8,12},{12,8},{16,20},{20,16},{24,28},{28,24},{1,5},{5... | collective-permute-start | bytes 3981320 | tf_op jit(solution)/shard_map/ppermute | solution.py:29
  408.1 36.5 %collective-permute-start.40 = (bf16[2,2,2,72,576]{4,3,1,2,0:T(8,128)(2,1)S(1)}, bf16[2,2,2,72,576]{4,3,1,2,0:T(8,128)(2,1)S(1)}, u32[]{:S(2)}, u32[]{:S(2)}) collective-permute-start(bf16[2,2,2,72,576]{4,3,1,2,0:T(8,128)(2,1)S(1)} %copy_bitcast_fusion.2), channel_id=1, source_target_pairs={{0,8},{4,12},{8,0},{12,4},{16,24},{20,28},{24,16},{28,20},{1,9},{5... | collective-permute-start | bytes 1990664 | tf_op jit(solution)/shard_map/ppermute | solution.py:29
  439.8 54.0 %collective-permute-start.53 = (bf16[72,2304]{1,0:T(8,128)(2,1)}, bf16[72,2304]{1,0:T(8,128)(2,1)}, u32[]{:S(2)}, u32[]{:S(2)}) collective-permute-start(bf16[72,2304]{1,0:T(8,128)(2,1)} %dynamic-slice_bitcast_fusion.10), channel_id=1, source_target_pairs={{0,16},{4,20},{8,24},{12,28},{16,0},{20,4},{24,8},{28,12},{1,17},{... | collective-permute-start | bytes 995336 | tf_op jit(solution)/shard_map/ppermute | solution.py:29
  451.0 19.7 %collective-permute-start.46 = (bf16[2,2,2,72,576]{4,3,2,0,1:T(8,128)(2,1)}, bf16[2,2,2,72,576]{4,3,2,0,1:T(8,128)(2,1)}, u32[]{:S(2)}, u32[]{:S(2)}) collective-permute-start(bf16[2,2,2,72,576]{4,3,2,0,1:T(8,128)(2,1)} %slice_bitcast_fusion.5), channel_id=1, source_target_pairs={{0,2},{2,0},{1,3},{3,1},{4,6},{6,4},{5,7},{7,5},{8,10},{10,8},{9,1... | collective-permute-start | bytes 1990664 | tf_op jit(solution)/shard_map/ppermute | solution.py:25
  453.5 38.5 %collective-permute-start.50 = (bf16[2,2,72,576]{3,2,0,1:T(8,128)(2,1)}, bf16[2,2,72,576]{3,2,0,1:T(8,128)(2,1)}, u32[]{:S(2)}, u32[]{:S(2)}) collective-permute-start(bf16[2,2,72,576]{3,2,0,1:T(8,128)(2,1)} %slice_bitcast_fusion.7), channel_id=1, source_target_pairs={{0,2},{2,0},{1,3},{3,1},{4,6},{6,4},{5,7},{7,5},{8,10},{10,8},{9,1... | collective-permute-start | bytes 995336 | tf_op jit(solution)/shard_map/ppermute | solution.py:25
  455.9 34.8 %collective-permute-start.51 = (bf16[2,2,3,72,576]{4,3,2,0,1:T(8,128)(2,1)}, bf16[2,2,3,72,576]{4,3,2,0,1:T(8,128)(2,1)}, u32[]{:S(2)}, u32[]{:S(2)}) collective-permute-start(bf16[2,2,3,72,576]{4,3,2,0,1:T(8,128)(2,1)} %dynamic-slice_bitcast_fusion.2), channel_id=1, source_target_pairs={{0,4},{4,0},{8,12},{12,8},{16,20},{20,16},{24,28},{28,24},{1,5},{5... | collective-permute-start | bytes 2985992 | tf_op jit(solution)/shard_map/ppermute | solution.py:29
  472.3 33.8 %collective-permute-start.56 = (f32[4896]{0:T(1024)S(1)}, f32[4896]{0:T(1024)S(1)}, u32[]{:S(2)}, u32[]{:S(2)}) collective-permute-start(f32[4896]{0:T(1024)S(1)} %pad_maximum_fusion.19), channel_id=1, source_target_pairs={{0,2},{2,0},{1,3},{3,1},{4,6},{6,4},{5,7},{7,5},{8,10},{10,8},{9,1... | collective-permute-start | bytes 58760 | tf_op jit(solution)/shard_map/ppermute | solution.py:25
  473.0 32.2 %collective-permute-start.47 = (bf16[2,2,72,576]{3,2,1,0:T(8,128)(2,1)S(1)}, bf16[2,2,72,576]{3,2,1,0:T(8,128)(2,1)S(1)}, u32[]{:S(2)}, u32[]{:S(2)}) collective-permute-start(bf16[2,2,72,576]{3,2,1,0:T(8,128)(2,1)S(1)} %dynamic-slice_bitcast_fusion.7), channel_id=1, source_target_pairs={{0,8},{4,12},{8,0},{12,4},{16,24},{20,28},{24,16},{28,20},{1,9},{5... | collective-permute-start | bytes 995336 | tf_op jit(solution)/shard_map/ppermute | solution.py:29
  501.3 23.1 %collective-permute-start.61 = (bf16[2,3,72,576]{3,2,1,0:T(8,128)(2,1)}, bf16[2,3,72,576]{3,2,1,0:T(8,128)(2,1)S(1)}, u32[]{:S(2)}, u32[]{:S(2)}) collective-permute-start(bf16[2,3,72,576]{3,2,1,0:T(8,128)(2,1)} %dynamic-slice_bitcast_fusion.6), channel_id=1, source_target_pairs={{0,8},{4,12},{8,0},{12,4},{16,24},{20,28},{24,16},{28,20},{1,9},{5... | collective-permute-start | bytes 1493000 | tf_op jit(solution)/shard_map/ppermute | solution.py:29
  (171 other events, 1233.0 us)
Sparse Core Ops, SparseCore 0:
  10.3 51.8 all-gather.3
  446.7 62.1 all-gather.5

commit v3 on v2

--- a/solution.py
+++ b/solution.py
@@ -394,6 +394,7 @@
 class Links:
     def __init__(self):
         self.free, self.events, self.waits = {}, [], []
+        self.rate = 138e3
         self.last, self.now, self.count, self.halves = None, 0.0, 0, []
 
     def push(self, time, task, got, tie):
@@ -426,7 +427,7 @@
         link = {"row": "x", 0: "y"}.get(kind, "z")
         hops = 2 ** max(kind - 1, 0) if isinstance(kind, int) else 1
         end = max(self.now, self.free.get(link, 0.0)) + 2.0
-        end += hops * value.size * value.dtype.itemsize / 46e3
+        end += hops * value.size * value.dtype.itemsize / self.rate
         self.free[link] = end
         got = swap_dp(value, kind) if isinstance(kind, int) else swap(value, kind)
         self.push(end, task, got, True)
@@ -579,9 +580,12 @@
         return kv_mine[0], kv_mine[1]
 
     dp_bits = list(range(bits))
-    order_x = ["row"] + dp_bits
-    order_y = [0, "row"] + dp_bits[1:]
-    order_z = [1, "row", 0] + dp_bits[2:]
+    rest = dp_bits[2:]
+    order_fc2 = ["row", 0, 1] + rest
+    order_fc1 = ([0, 1, "row"] + rest, [1, 0, "row"] + rest)
+    order_three = [0, 1, "row"] + rest
+    order_kv = ["row", 0, 1] + rest
+    order_q = [1, "row", 0] + rest
 
     def by_block(grads, n):
         return grads.reshape((2,) + (2,) * bits + (-1, n))
@@ -640,18 +644,23 @@
         ((weight_fc1,),) = yield ("wait", [fetch_fc1])
         activated, slope = rows_in(weight_fc1, mod_two, "gelu", bias_fc1)
         activated = yield ("compute", activated, 10.0)
+        links.rate = 46e3
 
         ((grad_near, grad_other),) = yield ("wait", [grad_in])
         grad_all, grad_mlp = assemble("gate", grad_near, grad_other, core, vectors)
         grad_w_fc2 = by_block(weight_grad(activated, grad_mlp.reshape(2, half, -1)), half)
         grad_w_fc2 = yield ("compute", grad_w_fc2, 9.0)
-        sum_fc2 = reduce(grad_w_fc2, order_x)
+        sum_fc2 = reduce(grad_w_fc2, order_fc2)
         ((weight_fc2,),) = yield ("wait", [fetch_fc2])
         grad_hidden, grad_b_fc1 = rows_in(weight_fc2, grad_mlp, "slope", slope)
         grad_hidden = yield ("compute", grad_hidden, 9.0)
-        grad_w_fc1 = weight_grad(mod_two, grad_hidden[None])
-        grad_w_fc1 = yield ("compute", by_block(grad_w_fc1, grad_hidden.shape[0]), 5.0)
-        sum_fc1 = reduce(grad_w_fc1, order_y)
+        ff_half = grad_hidden.shape[0] // 2
+        split = grad_hidden.reshape(2, ff_half, -1)
+        sum_fc1 = []
+        for i, order in enumerate(order_fc1):
+            grad_w_fc1 = by_block(weight_grad(mod_two, split, i, 1), ff_half)
+            grad_w_fc1 = yield ("compute", grad_w_fc1, 3.0)
+            sum_fc1.append(reduce(grad_w_fc1, order))
         grad_mod_two = split_sum([(weight_fc1, grad_hidden)])
         grad_own = grad_all[:, :HALF].astype(f32)
         grad_after_cross = grad_own + norm_backward(
@@ -679,7 +688,7 @@
         grad_w_three = jnp.stack([grad_w_out, grad_w_co, grad_w_cq], axis=bits + 1)
         grad_w_three = yield ("compute", grad_w_three, 10.0)
         grad_attended = yield ("compute", grad_attended, 3.0)
-        sum_three = reduce(grad_w_three, order_x)
+        sum_three = reduce(grad_w_three, order_three)
 
         grad_q, grad_k, grad_v = attend_grad(
             queries, keys, values, grad_attended, log_self, length, False
@@ -691,10 +700,10 @@
             axis=bits + 1,
         )
         grad_w_kv = yield ("compute", grad_w_kv, 7.0)
-        sum_kv = reduce(grad_w_kv, order_y)
+        sum_kv = reduce(grad_w_kv, order_kv)
         grad_w_q = by_block(weight_grad(mod_own, grad_q[None]), half)
         grad_w_q = yield ("compute", grad_w_q, 3.0)
-        sum_q = reduce(grad_w_q, order_z)
+        sum_q = reduce(grad_w_q, order_q)
         keep, send = rows_out([(weight_k, grad_k), (weight_v, grad_v), (weight_q, grad_q)])
         total = keep + swap(send, "col").astype(f32)
         total = yield ("compute", total, 16.0)
@@ -777,8 +786,8 @@
         wide_sums = sums[: 3 * quarter].reshape(3, quarter)
         col_sums = sums[3 * quarter :]
 
-        waited = [sum_fc2, sum_fc1, sum_three, sum_kv, sum_q, latents_out, result_out]
-        fc2, fc1, three, kv, sum_q, grad_latents, output = yield ("wait", waited)
+        waited = [sum_fc2, *sum_fc1, sum_three, sum_kv, sum_q, latents_out, result_out]
+        fc2, fc1_a, fc1_b, three, kv, sum_q, grad_latents, output = yield ("wait", waited)
         return (
             output,
             grad_latents.astype(f32),
@@ -795,7 +804,7 @@
             col_sums[3 * quarter : 4 * quarter],
             three[1],
             wide_sums[1],
-            fc1,
+            jnp.concatenate([fc1_a, fc1_b], axis=1),
             col_sums[4 * quarter :],
             fc2,
             wide_sums[2],

time: 564 us -> 536 us (0.950)
  waiting for transfers between devices: 192 us -> 174 us
  other arithmetic: 74.5 us -> 64.7 us
    ppermute x27 -> x30, waiting for transfers between devices: 133 us -> 117 us  [swap_dp(): lax.ppermute(value, 'dp', [(i, i ^ 1 << bit) for i in range(lax.axis_size...]
    squeeze x15 -> x18, local copies, waits for them, and re-layouts: 9.04 us -> 14.7 us  [reduce_pieces(): send = lax.dynamic_index_in_dim(held, 1 - bit, axis, keepdims=False)]
    unnamed x287 -> x283, local copies, waits for them, and re-layouts: 31.2 us -> 26.3 us
    ppermute x27 -> x30, starting transfers between devices: 35.4 us -> 37.6 us  [swap_dp(): lax.ppermute(value, 'dp', [(i, i ^ 1 << bit) for i in range(lax.axis_size...]
    ppermute x37 -> x38, starting transfers between devices: 22.1 us -> 23.9 us  [swap(): return lax.ppermute(value, axis, [(0, 1), (1, 0)])]
    convert_element_type x15 -> x18, other arithmetic: 21.2 us -> 22.8 us  [reduce_pieces(): held = held.astype(bf16)]
    ppermute x37 -> x38, waiting for transfers between devices: 58.2 us -> 56.7 us  [swap(): return lax.ppermute(value, axis, [(0, 1), (1, 0)])]
    pallas_call x8 -> x9, Pallas kernels: 21.6 us -> 22.5 us  [weight_grad(): pl.pallas_call(weight_grad_kernel, grid=(groups, k // rows), in_specs=[pl...]
  transfers between devices with their start and end apart: 66 -> 70, of which waited for: 23 -> 22; matrix products, arithmetic and copies ran while one was open for 23% -> 23% of each run, Pallas kernels for 22% -> 18%
where the time goes in v3:
time: 536 us; the launch traced here: 530 us
  waiting for transfers between devices  174 us (32%)
  Pallas kernels  129 us (24%)
  local copies, waits for them, and re-layouts  72.1 us (13%)
  other arithmetic  64.7 us (12%)
  starting transfers between devices  61.6 us (11%)
  between operations  17.1 us (3%)
  matrix products  11.6 us (2%)
    ppermute x30, waiting for transfers between devices, swap_dp(): lax.ppermute(value, 'dp', [(i, i ^ 1 << bit) for i in range(lax.axis_size...  117 us
    ppermute x38, waiting for transfers between devices, swap(): return lax.ppermute(value, axis, [(0, 1), (1, 0)])  56.7 us
    ppermute x30, starting transfers between devices, swap_dp(): lax.ppermute(value, 'dp', [(i, i ^ 1 << bit) for i in range(lax.axis_size...  37.6 us
    pallas_call x8, Pallas kernels, rows_in(): pl.pallas_call(partial(rows_in_kernel, len(weight.arrays), kind, lane), g...  36.2 us
    pallas_call x6, Pallas kernels, rows_out(): pl.pallas_call(partial(rows_out_kernel, [len(w.arrays) for w, _ in pairs]...  29.7 us
    unnamed x283, local copies, waits for them, and re-layouts  26.3 us
    ppermute x38, starting transfers between devices, swap(): return lax.ppermute(value, axis, [(0, 1), (1, 0)])  23.9 us
    convert_element_type x18, other arithmetic, reduce_pieces(): held = held.astype(bf16)  22.8 us
  transfers between devices with their start and end apart: 70, of which 22 were waited for; matrix products, arithmetic and copies ran while one was open for 23% of the time, Pallas kernels for 18%

profile of v3, /device:TPU:0, one launch (start us, length us, event | category | flops | bytes accessed | tf_op | source)
XLA Modules:
  0.0 530.2 jit_solution(367386097622095435)
XLA Ops:
  28.0 10.9 %collective-permute-done.1 = bf16[2,288,512]{2,1,0:T(8,128)(2,1)S(1)} collective-permute-done((bf16[2,288,512]{2,1,0:T(8,128)(2,1)S(1)}, bf16[2,288,512]{2,1,0:T(8,128)(2,1)S(1)}, u32[]{:S(2)}, u32[]{:S(2)}) %collective-permute-start.1) | collective-permute-done | bytes 589856 | tf_op jit(solution)/shard_map/ppermute | solution.py:29
  39.0 5.2 collective-permute-done.4.refs_1_.refs_7_.refs_10_
  54.7 13.7 %collective-permute-done.6.refs_2_.refs_8_.refs_11_ = bf16[2,288,576]{2,1,0:T(8,128)(2,1)S(1)} collective-permute-done((bf16[2,288,576]{2,1,0:T(8,128)(2,1)S(1)}, bf16[2,288,576]{2,1,0:T(8,128)(2,1)S(1)}, u32[]{:S(2)}, u32[]{:S(2)}) %collective-permute-start.6) | collective-permute-done | bytes 663584 | tf_op jit(solution)/shard_map/ppermute | solution.py:29
  71.5 5.1 assemble_norm.1
  80.6 4.1 rows_in_bias.4
  95.1 3.9 rows_in_plain.3
  101.9 9.6 %attend_fwd.2 = (bf16[8,72,512]{2,1,0:T(8,128)(2,1)S(1)}, f32[8,1,512]{2,1,0:T(1,128)S(1)}) custom-call(s32[1]{0:T(128)} %dynamic_slice.190.length_ref, bf16[8,72,512]{2,1,0:T(8,128)(2,1)S(1)} %bitcast.362, bf16[8,72,1024]{2,1,0:T(8,128)(2,1)S(1)} %bitcast.335, bf16[8,72,1024]{2,1,0:T(8,128)(2,1)S(1)} %bitcast.343), custom_call_target="tpu_custom_call" | custom-call | flops 1 | bytes 1 | tf_op jit(solution)/shard_map/attend_fwd/pallas_call | solution.py:72
  125.2 4.0 attend_fwd.3
  130.1 18.2 %collective-permute-done.20.refs_2_.refs_4_ = bf16[1,288,2304]{2,1,0:T(8,128)(2,1)S(1)} collective-permute-done((bf16[1,288,2304]{2,1,0:T(8,128)(2,1)}, bf16[1,288,2304]{2,1,0:T(8,128)(2,1)S(1)}, u32[]{:S(2)}, u32[]{:S(2)}) %collective-permute-start.20) | collective-permute-done | bytes 1327136 | tf_op jit(solution)/shard_map/ppermute | solution.py:29
  149.5 3.3 rows_out.7
  160.6 24.9 %collective-permute-done.23.refs_4_.refs_2_ = bf16[1,288,2304]{2,1,0:T(8,128)(2,1)S(1)} collective-permute-done((bf16[1,288,2304]{2,1,0:T(8,128)(2,1)S(1)}, bf16[1,288,2304]{2,1,0:T(8,128)(2,1)S(1)}, u32[]{:S(2)}, u32[]{:S(2)}) %collective-permute-start.23) | collective-permute-done | bytes 1327136 | tf_op jit(solution)/shard_map/ppermute | solution.py:29
  185.6 10.4 %rows_in_gelu.1 = (bf16[2304,512]{1,0:T(8,128)(2,1)}, bf16[2304,512]{1,0:T(8,128)(2,1)}) custom-call(s32[3]{0:T(128)S(1)} %fusion.61.places_ref.refs_0_.refs_1_, bf16[1152,512]{1,0:T(8,128)(2,1)S(1)} %pad_maximum_fusion.5.x_ref.inputs_ref, bf16[576,2304]{1,0:T(8,128)(2,1)} %refs_2_.1, bf16[1,288,2304]{2,1,0:T(8,128)(2,1)} %collective-permute-done.17.refs_1_.refs_3_, ...), custom_call_target="tpu_custom_call" | custom-call | flops 1 | bytes 1 | tf_op jit(solution)/shard_map/rows_in_gelu/pallas_call | solution.py:247
  197.6 6.1 %weight_grad.9 = bf16[2,2304,576]{2,1,0:T(8,128)(2,1)S(1)} custom-call(bf16[2304,512]{1,0:T(8,128)(2,1)S(1)} %copy-done.32, bf16[2,576,512]{2,1,0:T(8,128)(2,1)S(1)} %bitcast.364), custom_call_target="tpu_custom_call" | custom-call | flops 1 | bytes 1 | tf_op jit(solution)/shard_map/weight_grad/pallas_call | solution.py:331
  206.3 7.4 %rows_in_slope.1 = (bf16[2304,512]{1,0:T(8,128)(2,1)}, f32[2304,1]{1,0:T(8,128)S(1)}) custom-call(s32[3]{0:T(128)S(1)} %fusion.60.places_ref.refs_0_.refs_2_, bf16[1152,512]{1,0:T(8,128)(2,1)S(1)} %get-tuple-element.163.x_ref, bf16[576,2304]{1,0:T(8,128)(2,1)} %bitcast.380, bf16[1,288,2304]{2,1,0:T(8,128)(2,1)S(1)} %collective-permute-done.19.refs_3_.refs_1_, ...), custom_call_target="tpu_custom_call" | custom-call | flops 1 | bytes 1 | tf_op jit(solution)/shard_map/rows_in_slope/pallas_call | solution.py:247
  214.7 5.7 %rows_out.9 = (f32[1152,256]{1,0:T(8,128)S(1)}, bf16[1152,256]{1,0:T(8,128)(2,1)S(1)}) custom-call(s32[3]{0:T(128)S(1)} %fusion.61.places_ref.refs_0_.refs_1_, bf16[2304,512]{1,0:T(8,128)(2,1)} %get-tuple-element.167.refs_1_, bf16[576,2304]{1,0:T(8,128)(2,1)} %refs_2_.1, bf16[1,288,2304]{2,1,0:T(8,128)(2,1)} %collective-permute-done.17.refs_1_.refs_3_, ...), custom_call_target="tpu_custom_call" | custom-call | flops 1 | bytes 1 | tf_op jit(solution)/shard_map/rows_out/pallas_call | solution.py:310
  224.2 5.5 %rows_out.8 = (f32[1152,256]{1,0:T(8,128)S(1)}, bf16[1152,256]{1,0:T(8,128)(2,1)S(1)}) custom-call(s32[3]{0:T(128)S(1)} %fusion.60.places_ref.refs_0_.refs_2_, bf16[2304,512]{1,0:T(8,128)(2,1)} %get-tuple-element.159.refs_1_.inputs_ref, bf16[576,2304]{1,0:T(8,128)(2,1)} %bitcast.381, bf16[1,288,2304]{2,1,0:T(8,128)(2,1)S(1)} %copy-done.39, ...), custom_call_target="tpu_custom_call" | custom-call | flops 1 | bytes 1 | tf_op jit(solution)/shard_map/rows_out/pallas_call | solution.py:310
  241.3 3.0 fusion.23
  248.4 3.7 slice_bitcast_fusion.1
  259.8 4.8 attend_bwd.2
  290.8 27.8 %collective-permute-done.33 = bf16[2,2,2,288,576]{4,3,0,1,2:T(8,128)(2,1)} collective-permute-done((bf16[2,2,2,288,576]{4,3,0,1,2:T(8,128)(2,1)}, bf16[2,2,2,288,576]{4,3,0,1,2:T(8,128)(2,1)}, u32[]{:S(2)}, u32[]{:S(2)}) %collective-permute-start.33) | collective-permute-done | bytes 2654240 | tf_op jit(solution)/shard_map/ppermute | solution.py:25
  321.2 3.4 fusion
  331.5 4.0 collective-permute-done.34
  352.8 4.4 convolution_bitcast_fusion
  360.1 16.2 %attend_bwd.3 = (bf16[8,72,512]{2,1,0:T(8,128)(2,1)S(1)}, bf16[8,72,1024]{2,1,0:T(8,128)(2,1)S(1)}, bf16[8,72,1024]{2,1,0:T(8,128)(2,1)S(1)}) custom-call(s32[1]{0:T(128)} %dynamic_slice.190.length_ref, bf16[8,72,512]{2,1,0:T(8,128)(2,1)S(1)} %bitcast.363, bf16[8,72,1024]{2,1,0:T(8,128)(2,1)S(1)} %bitcast.336, bf16[8,72,1024]{2,1,0:T(8,128)(2,1)S(1)} %bitcast.344, ...), custom_call_target="tpu_custom_call" | custom-call | flops 1 | bytes 1 | tf_op jit(solution)/shard_map/attend_bwd/pallas_call | solution.py:110
  391.4 9.3 %rows_out.11 = (f32[1152,512]{1,0:T(8,128)}, bf16[1152,512]{1,0:T(8,128)(2,1)S(1)}) custom-call(s32[3]{0:T(128)S(1)} %fusion.61.places_ref.refs_0_.refs_1_, s32[3]{0:T(128)S(1)} %fusion.61.places_ref.refs_0_.refs_1_, s32[3]{0:T(128)S(1)} %fusion.60.places_ref.refs_0_.refs_2_, bf16[576,1024]{1,0:T(8,128)(2,1)S(1)} %bitcast.365, bf16[576,1024]{1,0:T(8,128)(2,1)} %bitcast.338, ...), custom_call_target="tpu_custom_call" | custom-call | flops 1 | bytes 1 | tf_op jit(solution)/shard_map/rows_out/pallas_call | solution.py:310
  407.6 11.9 %collective-permute-done.43 = bf16[2,288,576]{2,1,0:T(8,128)(2,1)} collective-permute-done((bf16[2,288,576]{2,1,0:T(8,128)(2,1)}, bf16[2,288,576]{2,1,0:T(8,128)(2,1)}, u32[]{:S(2)}, u32[]{:S(2)}) %collective-permute-start.43) | collective-permute-done | bytes 663584 | tf_op jit(solution)/shard_map/ppermute | solution.py:29
  422.1 20.3 %collective-permute-done.45 = bf16[2,2,2,72,576]{4,3,1,2,0:T(8,128)(2,1)S(1)} collective-permute-done((bf16[2,2,2,72,576]{4,3,1,2,0:T(8,128)(2,1)S(1)}, bf16[2,2,2,72,576]{4,3,1,2,0:T(8,128)(2,1)S(1)}, u32[]{:S(2)}, u32[]{:S(2)}) %collective-permute-start.45) | collective-permute-done | bytes 663584 | tf_op jit(solution)/shard_map/ppermute | solution.py:29
  454.3 5.7 %collective-permute-done.44 = bf16[1152,256]{1,0:T(8,128)(2,1)S(1)} collective-permute-done((bf16[1152,256]{1,0:T(8,128)(2,1)S(1)}, bf16[1152,256]{1,0:T(8,128)(2,1)S(1)}, u32[]{:S(2)}, u32[]{:S(2)}) %collective-permute-start.44) | collective-permute-done | bytes 589856 | tf_op jit(solution)/shard_map/ppermute | solution.py:29
  467.3 7.0 %collective-permute-done.51 = bf16[288,512]{1,0:T(8,128)(2,1)S(1)} collective-permute-done((bf16[288,512]{1,0:T(8,128)(2,1)S(1)}, bf16[288,512]{1,0:T(8,128)(2,1)S(1)}, u32[]{:S(2)}, u32[]{:S(2)}) %collective-permute-start.51) | collective-permute-done | bytes 294944 | tf_op jit(solution)/shard_map/ppermute | solution.py:25
  484.4 5.9 %collective-permute-done.53 = bf16[288,512]{1,0:T(8,128)(2,1)S(1)} collective-permute-done((bf16[288,512]{1,0:T(8,128)(2,1)S(1)}, bf16[288,512]{1,0:T(8,128)(2,1)S(1)}, u32[]{:S(2)}, u32[]{:S(2)}) %collective-permute-start.53) | collective-permute-done | bytes 294944 | tf_op jit(solution)/shard_map/ppermute | solution.py:25
  501.3 7.6 %collective-permute-done.62 = bf16[72,576]{1,0:T(8,128)(2,1)S(1)} collective-permute-done((bf16[72,576]{1,0:T(8,128)(2,1)S(1)}, bf16[72,576]{1,0:T(8,128)(2,1)S(1)}, u32[]{:S(2)}, u32[]{:S(2)}) %collective-permute-start.62) | collective-permute-done | bytes 82976 | tf_op jit(solution)/shard_map/ppermute | solution.py:29
  513.5 3.7 convolution_bitcast_fusion.1
  (636 shorter events, 236.2 us)
Async XLA Ops:
  7.3 81.9 %all-gather.4.cloned.1.call-start = ((), (), s32[]{:S(2)}) async-start(), calls=%async_computation | async-start | bytes 2211840 | tf_op jit(solution)/shard_map/all_gather | solution.py:838
  8.0 505.4 %all-gather.6.cloned.1.call-start = ((), (), s32[]{:S(2)}) async-start(), calls=%async_computation.1 | async-start | bytes 2654208 | tf_op jit(solution)/shard_map/all_gather | solution.py:825
  13.6 37.5 %collective-permute-start.3 = (f32[4896]{0:T(1024)S(1)}, f32[4896]{0:T(1024)S(1)}, u32[]{:S(2)}, u32[]{:S(2)}) collective-permute-start(f32[4896]{0:T(1024)S(1)} %concatenate.99), channel_id=1, source_target_pairs={{0,2},{2,0},{1,3},{3,1},{4,6},{6,4},{5,7},{7,5},{8,10},{10,8},{9,1... | collective-permute-start | bytes 58760 | tf_op jit(solution)/shard_map/ppermute | solution.py:25
  15.5 37.1 %collective-permute-start.7 = (bf16[1,288,576]{2,1,0:T(8,128)(2,1)}, bf16[1,288,576]{2,1,0:T(8,128)(2,1)}, u32[]{:S(2)}, u32[]{:S(2)}) collective-permute-start(bf16[1,288,576]{2,1,0:T(8,128)(2,1)} %dynamic-slice_bitcast_fusion.10), channel_id=1, source_target_pairs={{0,2},{2,0},{1,3},{3,1},{4,6},{6,4},{5,7},{7,5},{8,10},{10,8},{9,1... | collective-permute-start | bytes 995336 | tf_op jit(solution)/shard_map/ppermute | solution.py:25
  19.5 24.8 %collective-permute-start.4 = (bf16[2,288,576]{2,1,0:T(8,128)(2,1)}, bf16[2,288,576]{2,1,0:T(8,128)(2,1)S(1)}, u32[]{:S(2)}, u32[]{:S(2)}) collective-permute-start(bf16[2,288,576]{2,1,0:T(8,128)(2,1)} %dynamic-slice_bitcast_fusion.5), channel_id=1, source_target_pairs={{0,2},{2,0},{1,3},{3,1},{4,6},{6,4},{5,7},{7,5},{8,10},{10,8},{9,1... | collective-permute-start | bytes 1990664 | tf_op jit(solution)/shard_map/ppermute | solution.py:25
  44.2 24.2 %collective-permute-start.6 = (bf16[2,288,576]{2,1,0:T(8,128)(2,1)S(1)}, bf16[2,288,576]{2,1,0:T(8,128)(2,1)S(1)}, u32[]{:S(2)}, u32[]{:S(2)}) collective-permute-start(bf16[2,288,576]{2,1,0:T(8,128)(2,1)S(1)} %collective-permute-done.4.refs_1_.refs_7_.refs_10_), channel_id=1, source_target_pairs={{0,4},{4,0},{8,12},{12,8},{16,20},{20,16},{24,28},{28,24},{1,5},{5... | collective-permute-start | bytes 1990664 | tf_op jit(solution)/shard_map/ppermute | solution.py:29
  47.1 37.6 %collective-permute-start.10 = (bf16[3,288,576]{2,1,0:T(8,128)(2,1)}, bf16[3,288,576]{2,1,0:T(8,128)(2,1)}, u32[]{:S(2)}, u32[]{:S(2)}) collective-permute-start(bf16[3,288,576]{2,1,0:T(8,128)(2,1)} %constant_dynamic-slice_fusion.10), channel_id=1, source_target_pairs={{0,2},{2,0},{1,3},{3,1},{4,6},{6,4},{5,7},{7,5},{8,10},{10,8},{9,1... | collective-permute-start | bytes 2985992 | tf_op jit(solution)/shard_map/ppermute | solution.py:25
  52.6 32.1 %collective-permute-start.9 = (bf16[288,512]{1,0:T(8,128)(2,1)}, bf16[288,512]{1,0:T(8,128)(2,1)}, u32[]{:S(2)}, u32[]{:S(2)}) collective-permute-start(bf16[288,512]{1,0:T(8,128)(2,1)} %get-tuple-element.270), channel_id=1, source_target_pairs={{0,2},{2,0},{1,3},{3,1},{4,6},{6,4},{5,7},{7,5},{8,10},{10,8},{9,1... | collective-permute-start | bytes 884744 | tf_op jit(solution)/shard_map/ppermute | solution.py:25
  53.2 32.2 %collective-permute-start.13 = (bf16[2,576,120]{2,1,0:T(8,128)(2,1)S(1)}, bf16[2,576,120]{2,1,0:T(8,128)(2,1)}, u32[]{:S(2)}, u32[]{:S(2)}) collective-permute-start(bf16[2,576,120]{2,1,0:T(8,128)(2,1)S(1)} %get-tuple-element.308), channel_id=1, source_target_pairs={{0,2},{2,0},{1,3},{3,1},{4,6},{6,4},{5,7},{7,5},{8,10},{10,8},{9,1... | collective-permute-start | bytes 829448 | tf_op jit(solution)/shard_map/ppermute | solution.py:25
  84.7 26.8 %collective-permute-start.11 = (bf16[3,288,576]{2,1,0:T(8,128)(2,1)}, bf16[3,288,576]{2,1,0:T(8,128)(2,1)}, u32[]{:S(2)}, u32[]{:S(2)}) collective-permute-start(bf16[3,288,576]{2,1,0:T(8,128)(2,1)} %collective-permute-done.10.refs_3_.refs_1_), channel_id=1, source_target_pairs={{0,8},{4,12},{8,0},{12,4},{16,24},{20,28},{24,16},{28,20},{1,9},{5... | collective-permute-start | bytes 2985992 | tf_op jit(solution)/shard_map/ppermute | solution.py:29
  86.5 30.6 %collective-permute-start.17 = (bf16[1,288,2304]{2,1,0:T(8,128)(2,1)}, bf16[1,288,2304]{2,1,0:T(8,128)(2,1)}, u32[]{:S(2)}, u32[]{:S(2)}) collective-permute-start(bf16[1,288,2304]{2,1,0:T(8,128)(2,1)} %constant_dynamic-slice_fusion.9), channel_id=1, source_target_pairs={{0,2},{2,0},{1,3},{3,1},{4,6},{6,4},{5,7},{7,5},{8,10},{10,8},{9,1... | collective-permute-start | bytes 3981320 | tf_op jit(solution)/shard_map/ppermute | solution.py:25
  90.3 24.6 %collective-permute-start.18 = (bf16[8,120,256]{2,1,0:T(8,128)(2,1)S(1)}, bf16[8,120,256]{2,1,0:T(8,128)(2,1)S(1)}, u32[]{:S(2)}, u32[]{:S(2)}) collective-permute-start(bf16[8,120,256]{2,1,0:T(8,128)(2,1)S(1)} %constant_dynamic-slice_fusion.8), channel_id=1, source_target_pairs={{0,1},{1,0},{2,3},{3,2},{4,5},{5,4},{6,7},{7,6},{8,9},{9,8},{10,11... | collective-permute-start | bytes 1474568 | tf_op jit(solution)/shard_map/ppermute | solution.py:25
  117.2 31.2 %collective-permute-start.20 = (bf16[1,288,2304]{2,1,0:T(8,128)(2,1)}, bf16[1,288,2304]{2,1,0:T(8,128)(2,1)S(1)}, u32[]{:S(2)}, u32[]{:S(2)}) collective-permute-start(bf16[1,288,2304]{2,1,0:T(8,128)(2,1)} %collective-permute-done.17.refs_1_.refs_3_), channel_id=1, source_target_pairs={{0,4},{4,0},{8,12},{12,8},{16,20},{20,16},{24,28},{28,24},{1,5},{5... | collective-permute-start | bytes 3981320 | tf_op jit(solution)/shard_map/ppermute | solution.py:29
  118.5 31.0 %collective-permute-start.19 = (bf16[1,288,2304]{2,1,0:T(8,128)(2,1)S(1)}, bf16[1,288,2304]{2,1,0:T(8,128)(2,1)S(1)}, u32[]{:S(2)}, u32[]{:S(2)}) collective-permute-start(bf16[1,288,2304]{2,1,0:T(8,128)(2,1)S(1)} %constant_dynamic-slice_fusion.7), channel_id=1, source_target_pairs={{0,2},{2,0},{1,3},{3,1},{4,6},{6,4},{5,7},{7,5},{8,10},{10,8},{9,1... | collective-permute-start | bytes 3981320 | tf_op jit(solution)/shard_map/ppermute | solution.py:25
  154.4 31.1 %collective-permute-start.23 = (bf16[1,288,2304]{2,1,0:T(8,128)(2,1)S(1)}, bf16[1,288,2304]{2,1,0:T(8,128)(2,1)S(1)}, u32[]{:S(2)}, u32[]{:S(2)}) collective-permute-start(bf16[1,288,2304]{2,1,0:T(8,128)(2,1)S(1)} %collective-permute-done.19.refs_3_.refs_1_), channel_id=1, source_target_pairs={{0,8},{4,12},{8,0},{12,4},{16,24},{20,28},{24,16},{28,20},{1,9},{5... | collective-permute-start | bytes 3981320 | tf_op jit(solution)/shard_map/ppermute | solution.py:29
  236.2 32.5 %collective-permute-start.29 = (bf16[2,2,2,72,1152]{4,3,1,0,2:T(8,128)(2,1)}, bf16[2,2,2,72,1152]{4,3,1,0,2:T(8,128)(2,1)}, u32[]{:S(2)}, u32[]{:S(2)}) collective-permute-start(bf16[2,2,2,72,1152]{4,3,1,0,2:T(8,128)(2,1)} %copy_bitcast_fusion.1), channel_id=1, source_target_pairs={{0,4},{4,0},{8,12},{12,8},{16,20},{20,16},{24,28},{28,24},{1,5},{5... | collective-permute-start | bytes 3981320 | tf_op jit(solution)/shard_map/ppermute | solution.py:29
  237.9 31.3 %collective-permute-start.28 = (bf16[2,2,2,72,1152]{4,3,1,0,2:T(8,128)(2,1)}, bf16[2,2,2,72,1152]{4,3,1,0,2:T(8,128)(2,1)}, u32[]{:S(2)}, u32[]{:S(2)}) collective-permute-start(bf16[2,2,2,72,1152]{4,3,1,0,2:T(8,128)(2,1)} %copy_bitcast_fusion.2), channel_id=1, source_target_pairs={{0,8},{4,12},{8,0},{12,4},{16,24},{20,28},{24,16},{28,20},{1,9},{5... | collective-permute-start | bytes 3981320 | tf_op jit(solution)/shard_map/ppermute | solution.py:29
  252.0 66.6 %collective-permute-start.33 = (bf16[2,2,2,288,576]{4,3,0,1,2:T(8,128)(2,1)}, bf16[2,2,2,288,576]{4,3,0,1,2:T(8,128)(2,1)}, u32[]{:S(2)}, u32[]{:S(2)}) collective-permute-start(bf16[2,2,2,288,576]{4,3,0,1,2:T(8,128)(2,1)} %slice_bitcast_fusion.1), channel_id=1, source_target_pairs={{0,2},{2,0},{1,3},{3,1},{4,6},{6,4},{5,7},{7,5},{8,10},{10,8},{9,1... | collective-permute-start | bytes 7962632 | tf_op jit(solution)/shard_map/ppermute | solution.py:25
  265.4 59.2 %collective-permute-start.35 = (bf16[2,576,120]{2,1,0:T(8,128)(2,1)}, bf16[2,576,120]{2,1,0:T(8,128)(2,1)}, u32[]{:S(2)}, u32[]{:S(2)}) collective-permute-start(bf16[2,576,120]{2,1,0:T(8,128)(2,1)} %bitcast.63), channel_id=1, source_target_pairs={{0,4},{4,0},{8,12},{12,8},{16,20},{20,16},{24,28},{28,24},{1,5},{5... | collective-permute-start | bytes 829448 | tf_op jit(solution)/shard_map/ppermute | solution.py:29
  274.9 43.7 %collective-permute-start.32 = (bf16[2,2,72,1152]{3,2,1,0:T(8,128)(2,1)}, bf16[2,2,72,1152]{3,2,1,0:T(8,128)(2,1)}, u32[]{:S(2)}, u32[]{:S(2)}) collective-permute-start(bf16[2,2,72,1152]{3,2,1,0:T(8,128)(2,1)} %dynamic-slice_bitcast_fusion.7), channel_id=1, source_target_pairs={{0,8},{4,12},{8,0},{12,4},{16,24},{20,28},{24,16},{28,20},{1,9},{5... | collective-permute-start | bytes 1990664 | tf_op jit(solution)/shard_map/ppermute | solution.py:29
  286.5 33.4 %collective-permute-start.36 = (bf16[2,2,72,1152]{3,2,1,0:T(8,128)(2,1)}, bf16[2,2,72,1152]{3,2,1,0:T(8,128)(2,1)}, u32[]{:S(2)}, u32[]{:S(2)}) collective-permute-start(bf16[2,2,72,1152]{3,2,1,0:T(8,128)(2,1)} %dynamic-slice_bitcast_fusion.6), channel_id=1, source_target_pairs={{0,4},{4,0},{8,12},{12,8},{16,20},{20,16},{24,28},{28,24},{1,5},{5... | collective-permute-start | bytes 1990664 | tf_op jit(solution)/shard_map/ppermute | solution.py:29
  330.0 58.0 %collective-permute-start.41 = (bf16[2,2,288,576]{3,2,0,1:T(8,128)(2,1)}, bf16[2,2,288,576]{3,2,0,1:T(8,128)(2,1)}, u32[]{:S(2)}, u32[]{:S(2)}) collective-permute-start(bf16[2,2,288,576]{3,2,0,1:T(8,128)(2,1)} %dynamic-slice_bitcast_fusion.1), channel_id=1, source_target_pairs={{0,4},{4,0},{8,12},{12,8},{16,20},{20,16},{24,28},{28,24},{1,5},{5... | collective-permute-start | bytes 3981320 | tf_op jit(solution)/shard_map/ppermute | solution.py:29
  384.4 62.8 %collective-permute-start.48 = (bf16[2,2,2,3,72,576]{5,4,3,1,0,2:T(8,128)(2,1)}, bf16[2,2,2,3,72,576]{5,4,3,1,0,2:T(8,128)(2,1)}, u32[]{:S(2)}, u32[]{:S(2)}) collective-permute-start(bf16[2,2,2,3,72,576]{5,4,3,1,0,2:T(8,128)(2,1)} %dynamic-slice_bitcast_fusion), channel_id=1, source_target_pairs={{0,4},{4,0},{8,12},{12,8},{16,20},{20,16},{24,28},{28,24},{1,5},{5... | collective-permute-start | bytes 5971976 | tf_op jit(solution)/shard_map/ppermute | solution.py:29
  390.8 28.7 %collective-permute-start.43 = (bf16[2,288,576]{2,1,0:T(8,128)(2,1)}, bf16[2,288,576]{2,1,0:T(8,128)(2,1)}, u32[]{:S(2)}, u32[]{:S(2)}) collective-permute-start(bf16[2,288,576]{2,1,0:T(8,128)(2,1)} %dynamic-slice_bitcast_fusion.4), channel_id=1, source_target_pairs={{0,8},{4,12},{8,0},{12,4},{16,24},{20,28},{24,16},{28,20},{1,9},{5... | collective-permute-start | bytes 1990664 | tf_op jit(solution)/shard_map/ppermute | solution.py:29
  405.3 37.0 %collective-permute-start.45 = (bf16[2,2,2,72,576]{4,3,1,2,0:T(8,128)(2,1)S(1)}, bf16[2,2,2,72,576]{4,3,1,2,0:T(8,128)(2,1)S(1)}, u32[]{:S(2)}, u32[]{:S(2)}) collective-permute-start(bf16[2,2,2,72,576]{4,3,1,2,0:T(8,128)(2,1)S(1)} %copy_bitcast_fusion.3), channel_id=1, source_target_pairs={{0,8},{4,12},{8,0},{12,4},{16,24},{20,28},{24,16},{28,20},{1,9},{5... | collective-permute-start | bytes 1990664 | tf_op jit(solution)/shard_map/ppermute | solution.py:29
  406.8 37.5 %collective-permute-start.49 = (bf16[2,2,2,2,72,576]{5,4,3,0,1,2:T(8,128)(2,1)S(1)}, bf16[2,2,2,2,72,576]{5,4,3,0,1,2:T(8,128)(2,1)S(1)}, u32[]{:S(2)}, u32[]{:S(2)}) collective-permute-start(bf16[2,2,2,2,72,576]{5,4,3,0,1,2:T(8,128)(2,1)S(1)} %slice_bitcast_fusion.2), channel_id=1, source_target_pairs={{0,2},{2,0},{1,3},{3,1},{4,6},{6,4},{5,7},{7,5},{8,10},{10,8},{9,1... | collective-permute-start | bytes 3981320 | tf_op jit(solution)/shard_map/ppermute | solution.py:25
  420.9 28.6 %collective-permute-start.47 = (bf16[288,576]{1,0:T(8,128)(2,1)S(1)}, bf16[288,576]{1,0:T(8,128)(2,1)S(1)}, u32[]{:S(2)}, u32[]{:S(2)}) collective-permute-start(bf16[288,576]{1,0:T(8,128)(2,1)S(1)} %dynamic-slice_bitcast_fusion.9), channel_id=1, source_target_pairs={{0,16},{4,20},{8,24},{12,28},{16,0},{20,4},{24,8},{28,12},{1,17},{... | collective-permute-start | bytes 995336 | tf_op jit(solution)/shard_map/ppermute | solution.py:29
  445.8 30.3 %collective-permute-start.54 = (bf16[2,2,2,72,576]{4,3,2,0,1:T(8,128)(2,1)}, bf16[2,2,2,72,576]{4,3,2,0,1:T(8,128)(2,1)}, u32[]{:S(2)}, u32[]{:S(2)}) collective-permute-start(bf16[2,2,2,72,576]{4,3,2,0,1:T(8,128)(2,1)} %dynamic-slice_bitcast_fusion.3), channel_id=1, source_target_pairs={{0,4},{4,0},{8,12},{12,8},{16,20},{20,16},{24,28},{28,24},{1,5},{5... | collective-permute-start | bytes 1990664 | tf_op jit(solution)/shard_map/ppermute | solution.py:29
  450.7 25.3 %collective-permute-start.55 = (bf16[2,2,3,72,576]{4,3,2,1,0:T(8,128)(2,1)}, bf16[2,2,3,72,576]{4,3,2,1,0:T(8,128)(2,1)}, u32[]{:S(2)}, u32[]{:S(2)}) collective-permute-start(bf16[2,2,3,72,576]{4,3,2,1,0:T(8,128)(2,1)} %dynamic-slice_bitcast_fusion.2), channel_id=1, source_target_pairs={{0,8},{4,12},{8,0},{12,4},{16,24},{20,28},{24,16},{28,20},{1,9},{5... | collective-permute-start | bytes 2985992 | tf_op jit(solution)/shard_map/ppermute | solution.py:29
  453.5 36.8 %collective-permute-start.59 = (bf16[2,72,576]{2,1,0:T(8,128)(2,1)}, bf16[2,72,576]{2,1,0:T(8,128)(2,1)}, u32[]{:S(2)}, u32[]{:S(2)}) collective-permute-start(bf16[2,72,576]{2,1,0:T(8,128)(2,1)} %dynamic-slice_bitcast_fusion.19), channel_id=1, source_target_pairs={{0,4},{4,0},{8,12},{12,8},{16,20},{20,16},{24,28},{28,24},{1,5},{5... | collective-permute-start | bytes 497672 | tf_op jit(solution)/shard_map/ppermute | solution.py:29
  466.1 24.1 %collective-permute-start.58 = (f32[4896]{0:T(1024)S(1)}, f32[4896]{0:T(1024)S(1)}, u32[]{:S(2)}, u32[]{:S(2)}) collective-permute-start(f32[4896]{0:T(1024)S(1)} %pad_maximum_fusion.20), channel_id=1, source_target_pairs={{0,2},{2,0},{1,3},{3,1},{4,6},{6,4},{5,7},{7,5},{8,10},{10,8},{9,1... | collective-permute-start | bytes 58760 | tf_op jit(solution)/shard_map/ppermute | solution.py:25
  482.1 27.1 %collective-permute-start.66 = (bf16[2,3,72,576]{3,2,1,0:T(8,128)(2,1)}, bf16[2,3,72,576]{3,2,1,0:T(8,128)(2,1)}, u32[]{:S(2)}, u32[]{:S(2)}) collective-permute-start(bf16[2,3,72,576]{3,2,1,0:T(8,128)(2,1)} %slice_bitcast_fusion.4), channel_id=1, source_target_pairs={{0,2},{2,0},{1,3},{3,1},{4,6},{6,4},{5,7},{7,5},{8,10},{10,8},{9,1... | collective-permute-start | bytes 1493000 | tf_op jit(solution)/shard_map/ppermute | solution.py:25
  (173 other events, 1442.5 us)
Sparse Core Ops, SparseCore 0:
  10.3 56.3 all-gather.3
  353.0 63.4 all-gather.5
